TPU v7x, 32 devices: a whole 2x2x4 slice. The times are simulated.
32 devices in a mesh: seg: 2 (over y), chan: 16 (over z, x, core).
Axes of the slice: x: 2, y: 2, z: 4, core: 2. Of those that a mesh axis runs over, the one named last changes fastest.
Arguments:
- traces: bfloat16 [2, 1024, 4096], P('seg', 'chan'), may hold values from -60 to 60
- partners: int32 [16, 11], P('chan'), may hold values from -1 to 15, as said below
Outputs:
- stacked: float32 [16, 11, 65, 4096], P('chan', None, None, 'seg')
Inputs may be any that keep to these rules, and one draw needn't show every extreme that they name: `partners`: entry q of block i is i + q - 5 if blocks i and i + q - 5 form a pair and -1 otherwise. Entry 5 is always i. The list is symmetric: j stands in the row of i exactly when i stands in the row of j.
All inputs are finite; a program needn't handle non-finite values.
Results may differ from a plain program's by a relative error of at most 0.013.
Values may be sent and summed in bfloat16 or wider, within the bound.
No kernel may reach another device: no remote copies, remote signals or barrier semaphores. Data moves between devices by JAX's collectives and lax.ppermute only.
A program may use at most 128 MiB of HBM per device.

v0:
```python
import math

import jax
import jax.numpy as jnp
from jax import lax
from jax.sharding import PartitionSpec as P

BAND = 256
BAND_LO = 16
LAG = 32


full_turn = 2.0 * math.pi
water_level = 0.5
epsilon = 1e-06


def from_behind(value, axis, by):
    length = lax.axis_size(axis)
    pairs = [(i, i + by) for i in range(length) if 0 <= i + by < length]
    return lax.ppermute(value, axis, pairs)


def lag_tables(band_bins, band_low, lag_count, samples):
    lag_half = (lag_count - 1) // 2
    bins = jnp.arange(band_bins, dtype=jnp.int32) + band_low
    shifts = jnp.arange(lag_count, dtype=jnp.int32) - lag_half
    phase = jnp.mod(shifts[:, None] * bins[None, :], samples)
    angle = phase.astype(jnp.float32) * (full_turn / samples)
    return (jnp.cos(angle), jnp.sin(angle))


def dft_table(samples, band_bins, band_low):
    times = lax.broadcasted_iota(jnp.int32, (samples, band_bins), 0)
    bins = lax.broadcasted_iota(jnp.int32, (samples, band_bins), 1) + band_low
    phase = jnp.mod(times * bins, samples)
    angle = phase.astype(jnp.float32) * (full_turn / samples)
    return jnp.concatenate([jnp.cos(angle), -jnp.sin(angle)], axis=1)


def whiten(real_part, imag_part):
    power = real_part * real_part + imag_part * imag_part
    level = jnp.mean(power, axis=-1, keepdims=True)
    denom = jnp.sqrt(power + water_level * level + epsilon)
    return jnp.concatenate([real_part / denom, imag_part / denom], axis=-1).astype(jnp.bfloat16)


def lagged(spectra, cos_table, sin_table):
    band_bins = cos_table.shape[1]
    lag_count = cos_table.shape[0]
    real_part = spectra[..., :band_bins].astype(jnp.float32)[None]
    imag_part = spectra[..., band_bins:].astype(jnp.float32)[None]
    cosine = cos_table[:, None, None, :]
    sine = sin_table[:, None, None, :]
    turned = jnp.concatenate(
        [real_part * cosine - imag_part * sine, real_part * sine + imag_part * cosine], axis=-1
    )
    return turned.reshape(lag_count * spectra.shape[0], spectra.shape[1] * 2 * band_bins).astype(
        jnp.bfloat16
    )


def columns(window):
    moved = jnp.transpose(window, (0, 3, 1, 2))
    return moved.reshape(window.shape[0] * window.shape[3], window.shape[1] * window.shape[2])


def tile_block(lagged_rows, partner_columns, live_pairs, rows_a, norm_scale):
    product = jnp.dot(lagged_rows, partner_columns, preferred_element_type=jnp.float32)
    slots = live_pairs.shape[0]
    lag_count = product.shape[0] // rows_a
    width = product.shape[1] // slots
    product = product.reshape(lag_count, rows_a, slots, width).transpose(2, 0, 1, 3)
    product = product.reshape(slots, lag_count, rows_a * width)
    return product * norm_scale * live_pairs[:, None, None]


def local(traces, partners):
    block_channels = traces.shape[1]
    samples = traces.shape[2]
    slot_count = partners.shape[1]
    reach_blocks = (slot_count - 1) // 2
    segment_count = lax.axis_size("seg")
    transform = dft_table(samples, BAND, BAND_LO)
    table_high = transform.astype(jnp.bfloat16)
    table_low = (transform - table_high.astype(jnp.float32)).astype(jnp.bfloat16)
    spectrum = jnp.dot(traces[0], table_high, preferred_element_type=jnp.float32)
    spectrum = spectrum + jnp.dot(traces[0], table_low, preferred_element_type=jnp.float32)
    own_spectra = whiten(spectrum[:, :BAND], spectrum[:, BAND:])
    cos_table, sin_table = lag_tables(BAND, BAND_LO, 2 * LAG + 1, samples)
    norm_scale = (segment_count * BAND) ** (-0.5)
    live_pairs = (partners[0] >= 0).astype(jnp.float32)
    pieces = []
    for offset in range(-reach_blocks, reach_blocks + 1):
        if offset == 0:
            pieces.append(own_spectra)
        else:
            pieces.append(from_behind(own_spectra, "chan", -offset))
    window = jnp.stack(pieces, axis=0)
    both_segments = lax.all_gather(window[None], "seg", axis=0, tiled=True)
    half_rows = block_channels // segment_count
    seg_index = lax.axis_index("seg")
    own_both = lax.dynamic_slice_in_dim(
        both_segments[:, reach_blocks], seg_index * half_rows, half_rows, 1
    )
    rows = lagged(jnp.transpose(own_both, (1, 0, 2)), cos_table, sin_table)
    stacked = tile_block(rows, columns(both_segments), live_pairs, half_rows, norm_scale)
    return stacked[None]


def solution(mesh):
    placed = (P("seg", "chan", None), P("chan", None))
    return jax.shard_map(
        local, mesh=mesh, in_specs=placed, out_specs=P("chan", None, None, "seg"), check_vma=False
    )
```

profile of v0, /device:TPU:0, one launch (start us, length us, event | category | flops | bytes accessed | tf_op | source)
XLA Modules:
  0.0 158.4 jit_solution(9878714981907307302)
XLA Ops:
  6.5 16.5 %fusion.15 = (f32[4096,256]{1,0:T(8,128)S(1)}, f32[4096,256]{1,0:T(8,128)S(1)}) fusion(s32[256]{0:T(256)S(1)} %iota_add_fusion), kind=kLoop, calls=%fused_computation.22 | loop fusion | flops 15728640 | bytes 8389632 | tf_op jit(solution)/shard_map/cos | solution.py:38
  25.0 4.4 %collective-permute-start = (bf16[64,512]{1,0:T(8,128)(2,1)S(1)}, bf16[64,512]{1,0:T(8,128)(2,1)S(1)}, u32[]{:S(2)}, u32[]{:S(2)}) collective-permute-start(bf16[64,512]{1,0:T(8,128)(2,1)S(1)} %pad_maximum_fusion.2), channel_id=1, source_target_pairs={{0,5},{1,6},{2,7},{3,8},{4,9},{5,10},{6,11},{7,12},{8,13},{9,14},{... | collective-permute-start | bytes 196616 | tf_op jit(solution)/shard_map/ppermute | solution.py:21
  29.4 3.5 %collective-permute-start.1 = (bf16[64,512]{1,0:T(8,128)(2,1)S(1)}, bf16[64,512]{1,0:T(8,128)(2,1)S(1)}, u32[]{:S(2)}, u32[]{:S(2)}) collective-permute-start(bf16[64,512]{1,0:T(8,128)(2,1)S(1)} %pad_maximum_fusion.2), channel_id=1, source_target_pairs={{0,4},{1,5},{2,6},{3,7},{4,8},{5,9},{6,10},{7,11},{8,12},{9,13},{1... | collective-permute-start | bytes 196616 | tf_op jit(solution)/shard_map/ppermute | solution.py:21
  32.9 4.4 %collective-permute-start.2 = (bf16[64,512]{1,0:T(8,128)(2,1)S(1)}, bf16[64,512]{1,0:T(8,128)(2,1)S(1)}, u32[]{:S(2)}, u32[]{:S(2)}) collective-permute-start(bf16[64,512]{1,0:T(8,128)(2,1)S(1)} %pad_maximum_fusion.2), channel_id=1, source_target_pairs={{0,3},{1,4},{2,5},{3,6},{4,7},{5,8},{6,9},{7,10},{8,11},{9,12},{10... | collective-permute-start | bytes 196616 | tf_op jit(solution)/shard_map/ppermute | solution.py:21
  37.3 3.4 %collective-permute-start.3 = (bf16[64,512]{1,0:T(8,128)(2,1)S(1)}, bf16[64,512]{1,0:T(8,128)(2,1)S(1)}, u32[]{:S(2)}, u32[]{:S(2)}) collective-permute-start(bf16[64,512]{1,0:T(8,128)(2,1)S(1)} %pad_maximum_fusion.2), channel_id=1, source_target_pairs={{0,2},{1,3},{2,4},{3,5},{4,6},{5,7},{6,8},{7,9},{8,10},{9,11},{10,... | collective-permute-start | bytes 196616 | tf_op jit(solution)/shard_map/ppermute | solution.py:21
  40.7 1.3 collective-permute-start.4
  42.0 1.3 collective-permute-start.5
  43.3 1.3 collective-permute-start.6
  44.7 1.3 collective-permute-start.7
  46.0 1.3 collective-permute-start.8
  47.3 1.3 collective-permute-start.9
  48.7 2.2 %collective-permute-done.6 = bf16[64,512]{1,0:T(8,128)(2,1)S(1)} collective-permute-done((bf16[64,512]{1,0:T(8,128)(2,1)S(1)}, bf16[64,512]{1,0:T(8,128)(2,1)S(1)}, u32[]{:S(2)}, u32[]{:S(2)}) %collective-permute-start.6) | collective-permute-done | bytes 65568 | tf_op jit(solution)/shard_map/ppermute | solution.py:21
  50.9 1.2 collective-permute-done.7
  52.1 4.1 %collective-permute-done.8 = bf16[64,512]{1,0:T(8,128)(2,1)S(1)} collective-permute-done((bf16[64,512]{1,0:T(8,128)(2,1)S(1)}, bf16[64,512]{1,0:T(8,128)(2,1)S(1)}, u32[]{:S(2)}, u32[]{:S(2)}) %collective-permute-start.8) | collective-permute-done | bytes 65568 | tf_op jit(solution)/shard_map/ppermute | solution.py:21
  56.2 1.2 collective-permute-done.9
  58.8 27.3 %all-gather.3.cloned.1.call-done = bf16[22,64,512]{2,1,0:T(8,128)(2,1)} async-done(((bf16[11,64,512]{2,1,0:T(8,128)(2,1)}), bf16[22,64,512]{2,1,0:T(8,128)(2,1)}) %all-gather.3.cloned.1.call-update) | async-done | bytes 1441808 | tf_op jit(solution)/shard_map/all_gather | solution.py:100
  87.1 5.5 %subtract_convert_fusion.1 = (bf16[65,32,2,256]{3,2,1,0:T(2,128)(2,1)S(1)}, bf16[65,32,2,256]{3,2,1,0:T(2,128)(2,1)}) fusion(f32[65,256]{1,0:T(8,128)S(1)} %get-tuple-element.12, f32[32,2,256]{2,1,0:T(2,128)S(1)} %copy.16, f32[65,256]{1,0:T(8,128)S(1)} %get-tuple-element.11, f32[32,2,256]{2,1,0:T(2,128)S(1)} %copy.15), kind=kLoop, calls=%fused_computation.12 | loop fusion | flops 8519680 | bytes 4524032 | tf_op jit(solution)/shard_map/convert
  92.6 10.0 %pad_maximum_fusion.1 = bf16[65,32,2,512]{3,2,1,0:T(2,128)(2,1)} fusion(bf16[65,32,2,256]{3,2,1,0:T(2,128)(2,1)} %get-tuple-element.6, bf16[65,32,2,256]{3,2,1,0:T(2,128)(2,1)S(1)} %get-tuple-element.5), kind=kLoop, calls=%fused_computation.8 | loop fusion | flops 8519680 | bytes 8519680 | tf_op jit(solution)/shard_map/concatenate | solution.py:55
  102.6 10.7 %reshape.148 = bf16[65,32,1024,1]{2,1,0,3:T(8,128)(2,1)} reshape(bf16[65,32,2,512]{3,2,1,0:T(2,128)(2,1)} %pad_maximum_fusion.1) | data formatting | bytes 8519680 | tf_op jit(solution)/shard_map/convert_element_type | solution.py:58
  113.3 1.5 copy.17
  115.5 9.6 %fusion.12 = f32[11,65,32,64]{3,2,0,1:T(8,128)} fusion(bf16[11,64,1024,1]{2,1,0,3:T(8,128)(2,1)S(1)} %bitcast.64, bf16[65,32,1024,1]{2,1,0,3:T(8,128)(2,1)S(1)} %copy-done.1), kind=kOutput, calls=%fused_computation.21 | convolution fusion | flops 2998927360 | bytes 11558912 | tf_op jit(solution)/shard_map/dot_general | solution.py:69
  125.1 12.5 %reshape.151 = f32[1,11,65,2048]{3,1,2,0:T(8,128)} reshape(f32[11,65,32,64]{3,2,0,1:T(8,128)} %fusion.12) | data formatting | bytes 11714560 | tf_op jit(solution)/shard_map/reshape | solution.py:74
  137.6 6.8 %copy_multiply_fusion = f32[1,11,65,2048]{3,2,1,0:T(8,128)S(1)} fusion(f32[1,11,65,2048]{3,1,2,0:T(8,128)} %reshape.151, f32[11]{0:T(128)S(1)} %fusion.25), kind=kLoop, calls=%fused_computation.3 | loop fusion | flops 1464320 | bytes 11714604 | tf_op jit(solution)/shard_map/mul | solution.py:75
  144.5 7.1 %copy.19 = f32[1,11,65,2048]{3,0,2,1:T(1,128)} copy(f32[1,11,65,2048]{3,2,1,0:T(8,128)S(1)} %copy_multiply_fusion) | data formatting | bytes 11714560 | tf_op jit(solution)/shard_map/mul | solution.py:75
  (45 shorter events, 5.0 us)
Async XLA Ops:
  6.5 16.5 %copy-start = (bf16[1,64,4096]{2,1,0:T(8,128)(2,1)S(1)}, bf16[1,64,4096]{2,1,0:T(8,128)(2,1)}, u32[]{:S(2)}) copy-start(bf16[1,64,4096]{2,1,0:T(8,128)(2,1)} %param.2) | copy-start | bytes 1572868
  6.5 79.5 %all-gather.3.cloned.1.call-start = ((), (), s32[]{:S(2)}) async-start(), calls=%async_computation | async-start | bytes 2162688 | tf_op jit(solution)/shard_map/all_gather | solution.py:100
  23.9 34.5 %copy-start.4 = (s32[1,11]{1,0:T(1,128)S(1)}, s32[1,11]{1,0:T(1,128)}, u32[]{:S(2)}) copy-start(s32[1,11]{1,0:T(1,128)} %param.3) | copy-start | bytes 136
  25.0 17.0 %collective-permute-start = (bf16[64,512]{1,0:T(8,128)(2,1)S(1)}, bf16[64,512]{1,0:T(8,128)(2,1)S(1)}, u32[]{:S(2)}, u32[]{:S(2)}) collective-permute-start(bf16[64,512]{1,0:T(8,128)(2,1)S(1)} %pad_maximum_fusion.2), channel_id=1, source_target_pairs={{0,5},{1,6},{2,7},{3,8},{4,9},{5,10},{6,11},{7,12},{8,13},{9,14},{... | collective-permute-start | bytes 196616 | tf_op jit(solution)/shard_map/ppermute | solution.py:21
  29.4 13.9 %collective-permute-start.1 = (bf16[64,512]{1,0:T(8,128)(2,1)S(1)}, bf16[64,512]{1,0:T(8,128)(2,1)S(1)}, u32[]{:S(2)}, u32[]{:S(2)}) collective-permute-start(bf16[64,512]{1,0:T(8,128)(2,1)S(1)} %pad_maximum_fusion.2), channel_id=1, source_target_pairs={{0,4},{1,5},{2,6},{3,7},{4,8},{5,9},{6,10},{7,11},{8,12},{9,13},{1... | collective-permute-start | bytes 196616 | tf_op jit(solution)/shard_map/ppermute | solution.py:21
  32.9 11.8 %collective-permute-start.2 = (bf16[64,512]{1,0:T(8,128)(2,1)S(1)}, bf16[64,512]{1,0:T(8,128)(2,1)S(1)}, u32[]{:S(2)}, u32[]{:S(2)}) collective-permute-start(bf16[64,512]{1,0:T(8,128)(2,1)S(1)} %pad_maximum_fusion.2), channel_id=1, source_target_pairs={{0,3},{1,4},{2,5},{3,6},{4,7},{5,8},{6,9},{7,10},{8,11},{9,12},{10... | collective-permute-start | bytes 196616 | tf_op jit(solution)/shard_map/ppermute | solution.py:21
  37.3 8.7 %collective-permute-start.3 = (bf16[64,512]{1,0:T(8,128)(2,1)S(1)}, bf16[64,512]{1,0:T(8,128)(2,1)S(1)}, u32[]{:S(2)}, u32[]{:S(2)}) collective-permute-start(bf16[64,512]{1,0:T(8,128)(2,1)S(1)} %pad_maximum_fusion.2), channel_id=1, source_target_pairs={{0,2},{1,3},{2,4},{3,5},{4,6},{5,7},{6,8},{7,9},{8,10},{9,11},{10,... | collective-permute-start | bytes 196616 | tf_op jit(solution)/shard_map/ppermute | solution.py:21
  40.7 6.6 %collective-permute-start.4 = (bf16[64,512]{1,0:T(8,128)(2,1)S(1)}, bf16[64,512]{1,0:T(8,128)(2,1)S(1)}, u32[]{:S(2)}, u32[]{:S(2)}) collective-permute-start(bf16[64,512]{1,0:T(8,128)(2,1)S(1)} %pad_maximum_fusion.2), channel_id=1, source_target_pairs={{0,1},{1,2},{2,3},{3,4},{4,5},{5,6},{6,7},{7,8},{8,9},{9,10},{10,1... | collective-permute-start | bytes 196616 | tf_op jit(solution)/shard_map/ppermute | solution.py:21
  42.0 6.6 %collective-permute-start.5 = (bf16[64,512]{1,0:T(8,128)(2,1)S(1)}, bf16[64,512]{1,0:T(8,128)(2,1)S(1)}, u32[]{:S(2)}, u32[]{:S(2)}) collective-permute-start(bf16[64,512]{1,0:T(8,128)(2,1)S(1)} %pad_maximum_fusion.2), channel_id=1, source_target_pairs={{1,0},{2,1},{3,2},{4,3},{5,4},{6,5},{7,6},{8,7},{9,8},{10,9},{11,1... | collective-permute-start | bytes 196616 | tf_op jit(solution)/shard_map/ppermute | solution.py:21
  43.3 7.5 %collective-permute-start.6 = (bf16[64,512]{1,0:T(8,128)(2,1)S(1)}, bf16[64,512]{1,0:T(8,128)(2,1)S(1)}, u32[]{:S(2)}, u32[]{:S(2)}) collective-permute-start(bf16[64,512]{1,0:T(8,128)(2,1)S(1)} %pad_maximum_fusion.2), channel_id=1, source_target_pairs={{2,0},{3,1},{4,2},{5,3},{6,4},{7,5},{8,6},{9,7},{10,8},{11,9},{12,... | collective-permute-start | bytes 196616 | tf_op jit(solution)/shard_map/ppermute | solution.py:21
  44.7 7.4 %collective-permute-start.7 = (bf16[64,512]{1,0:T(8,128)(2,1)S(1)}, bf16[64,512]{1,0:T(8,128)(2,1)S(1)}, u32[]{:S(2)}, u32[]{:S(2)}) collective-permute-start(bf16[64,512]{1,0:T(8,128)(2,1)S(1)} %pad_maximum_fusion.2), channel_id=1, source_target_pairs={{3,0},{4,1},{5,2},{6,3},{7,4},{8,5},{9,6},{10,7},{11,8},{12,9},{13... | collective-permute-start | bytes 196616 | tf_op jit(solution)/shard_map/ppermute | solution.py:21
  46.0 10.2 %collective-permute-start.8 = (bf16[64,512]{1,0:T(8,128)(2,1)S(1)}, bf16[64,512]{1,0:T(8,128)(2,1)S(1)}, u32[]{:S(2)}, u32[]{:S(2)}) collective-permute-start(bf16[64,512]{1,0:T(8,128)(2,1)S(1)} %pad_maximum_fusion.2), channel_id=1, source_target_pairs={{4,0},{5,1},{6,2},{7,3},{8,4},{9,5},{10,6},{11,7},{12,8},{13,9},{1... | collective-permute-start | bytes 196616 | tf_op jit(solution)/shard_map/ppermute | solution.py:21
  47.3 10.2 %collective-permute-start.9 = (bf16[64,512]{1,0:T(8,128)(2,1)S(1)}, bf16[64,512]{1,0:T(8,128)(2,1)S(1)}, u32[]{:S(2)}, u32[]{:S(2)}) collective-permute-start(bf16[64,512]{1,0:T(8,128)(2,1)S(1)} %pad_maximum_fusion.2), channel_id=1, source_target_pairs={{5,0},{6,1},{7,2},{8,3},{9,4},{10,5},{11,6},{12,7},{13,8},{14,9},{... | collective-permute-start | bytes 196616 | tf_op jit(solution)/shard_map/ppermute | solution.py:21
  57.5 0.9 copy-start.3
  102.6 10.7 %copy-start.2 = (bf16[22,64,512]{2,1,0:T(8,128)(2,1)S(1)}, bf16[22,64,512]{2,1,0:T(8,128)(2,1)}, u32[]{:S(2)}) copy-start(bf16[22,64,512]{2,1,0:T(8,128)(2,1)} %all-gather.3.cloned.1.call-done) | copy-start | bytes 4325380
  113.3 2.2 %copy-start.1 = (bf16[65,32,1024,1]{2,1,0,3:T(8,128)(2,1)S(1)}, bf16[65,32,1024,1]{2,1,0,3:T(8,128)(2,1)}, u32[]{:S(2)}) copy-start(bf16[65,32,1024,1]{2,1,0,3:T(8,128)(2,1)} %reshape.148) | copy-start | bytes 12779524
Sparse Core Ops, SparseCore 0:
  58.5 27.4 all-gather.2
where the time goes:
time: 159 us; the launch traced here: 158 us
  other arithmetic  39.5 us (25%)
  waiting for transfers between devices  36.1 us (23%)
  local copies, waits for them, and re-layouts  34.4 us (22%)
  starting transfers between devices  23.4 us (15%)
  between operations  13.7 us (9%)
  matrix products  11.3 us (7%)
    all_gather x1, waiting for transfers between devices, local(): both_segments = lax.all_gather(window[None], 'seg', axis=0, tiled=True)  27.3 us
    ppermute x10, starting transfers between devices, from_behind(): return lax.ppermute(value, axis, pairs)  23.4 us
    cos x1, other arithmetic, dft_table(): return jnp.concatenate([jnp.cos(angle), -jnp.sin(angle)], axis=1)  16.5 us
    reshape x1, local copies, waits for them, and re-layouts, tile_block(): product = product.reshape(slots, lag_count, rows_a * width)  12.5 us
    convert_element_type x1, local copies, waits for them, and re-layouts, lagged(): turned.reshape(lag_count * spectra.shape[0], spectra.shape[1] * 2 * band_...  10.7 us
    concatenate x1, other arithmetic, lagged(): jnp.concatenate([real_part * cosine - imag_part * sine, real_part * sine...  9.99 us
    dot_general x1, matrix products, tile_block(): jnp.dot(lagged_rows, partner_columns, preferred_element_type=jnp.float32)  9.64 us
    ppermute x10, waiting for transfers between devices, from_behind(): return lax.ppermute(value, axis, pairs)  8.79 us
  transfers between devices with their start and end apart: 11, of which 5 were waited for; matrix products, arithmetic and copies ran while one was open for 0% of the time, Pallas kernels for 0%

commit v1 on v0

v1 whole, which is shorter than its diff:
```python
import functools
import math

import jax
import jax.numpy as jnp
import numpy as np
from jax import lax
from jax.experimental import pallas as pl
from jax.experimental.pallas import tpu as pltpu
from jax.sharding import PartitionSpec as P

BAND = 256
BAND_LO = 16
LAG = 32
LAGS = 2 * LAG + 1
LAG_ROWS = 72
QUAD = 4

water_level = 0.5
epsilon = 1e-06


def split_table(samples, step):
    bins = np.arange(BAND) + BAND_LO
    angle = (np.arange(step)[:, None] * bins[None, :] % samples) * (2.0 * math.pi / samples)
    table = np.concatenate([np.cos(angle), -np.sin(angle)], axis=1).astype(np.float32)
    high = table.astype(jnp.bfloat16)
    low = (table - high.astype(np.float32)).astype(jnp.bfloat16)
    stretches = samples // step
    turn = (np.arange(stretches)[:, None] * step * bins[None, :] % samples) * (2.0 * math.pi / samples)
    return high, low, np.cos(turn).astype(np.float32), np.sin(turn).astype(np.float32)


def lag_tables(samples):
    bins = np.arange(BAND) + BAND_LO
    shifts = np.arange(LAG_ROWS) - LAG
    angle = (shifts[:, None] * bins[None, :] % samples) * (2.0 * math.pi / samples)
    return np.cos(angle).astype(np.float32), np.sin(angle).astype(np.float32)


def spectrum_kernel(step, traces_ref, high_ref, low_ref, cos_ref, sin_ref, white_ref):
    stretches = traces_ref.shape[1] // step
    real = imag = None
    for stretch in range(stretches):
        part = traces_ref[:, stretch * step : (stretch + 1) * step]
        y = jnp.dot(part, high_ref[...], preferred_element_type=jnp.float32)
        y = y + jnp.dot(part, low_ref[...], preferred_element_type=jnp.float32)
        y_real, y_imag = y[:, :BAND], y[:, BAND:]
        if stretch == 0:
            real, imag = y_real, y_imag
            continue
        cosine = cos_ref[stretch : stretch + 1, :]
        sine = sin_ref[stretch : stretch + 1, :]
        real = real + (y_real * cosine + y_imag * sine)
        imag = imag + (y_imag * cosine - y_real * sine)
    power = real * real + imag * imag
    level = jnp.mean(power, axis=1, keepdims=True)
    denom = jnp.sqrt(power + water_level * level + epsilon)
    white_ref[:, :BAND] = (real / denom).astype(jnp.bfloat16)
    white_ref[:, BAND:] = (imag / denom).astype(jnp.bfloat16)


def spectra(traces):
    channels, samples = traces.shape
    step = 256
    tables = split_table(samples, step)
    return pl.pallas_call(
        functools.partial(spectrum_kernel, step),
        out_shape=jax.ShapeDtypeStruct((channels, 2 * BAND), jnp.bfloat16),
        compiler_params=pltpu.CompilerParams(vmem_limit_bytes=32 * 2**20),
    )(traces, *(jnp.asarray(t) for t in tables))


def stack_kernel(norm_scale, place_ref, live_ref, own_ref, cos_ref, sin_ref, blobs_ref, out_ref,
                 own, rows, window, tiles, in_sems, out_sems):
    slots = live_ref.shape[1]
    width = window.shape[1]
    half = own.shape[0]
    pairs = half // 2
    pair_rows = 2 * LAG_ROWS
    copies = [
        pltpu.make_async_copy(blobs_ref.at[place_ref[slot]], window.at[slot], in_sems.at[slot])
        for slot in range(slots)
    ]
    for copy in copies:
        copy.start()
    first = pl.multiple_of(place_ref[slots], half)
    own[...] = own_ref[pl.ds(first, half), :].astype(jnp.float32)

    def turn(pair, carry):
        for part in range(own.shape[1] // (2 * BAND)):
            left = part * 2 * BAND
            reals, imags = [], []
            for member in range(2):
                real = own[pl.ds(pair * 2 + member, 1), left : left + BAND]
                imag = own[pl.ds(pair * 2 + member, 1), left + BAND : left + 2 * BAND]
                reals.append(real * cos_ref[...] - imag * sin_ref[...])
                imags.append(real * sin_ref[...] + imag * cos_ref[...])
            at = pl.ds(pl.multiple_of(pair * pair_rows, pair_rows), pair_rows)
            rows[at, left : left + BAND] = jnp.concatenate(reals, axis=0).astype(jnp.bfloat16)
            rows[at, left + BAND : left + 2 * BAND] = jnp.concatenate(imags, axis=0).astype(jnp.bfloat16)
        return carry

    lax.fori_loop(0, pairs, turn, 0)
    group = 4
    chunk = 4
    sent = []
    for number, start in enumerate(range(0, slots, group)):
        members = list(range(start, min(start + group, slots)))
        buffer = number % 2
        for slot in members:
            copies[slot].wait()
        if number >= 2:
            for copy in sent[number - 2]:
                copy.wait()
        partner = window[start : start + len(members)].reshape(len(members) * width, window.shape[2])
        scales = [jnp.where(live_ref[0, slot] >= 0, norm_scale, 0.0) for slot in members]

        def multiply(step, carry):
            at = pl.multiple_of(step * chunk * pair_rows, chunk * pair_rows)
            product = lax.dot_general(
                rows[pl.ds(at, chunk * pair_rows), :], partner, (((1,), (1,)), ((), ())),
                preferred_element_type=jnp.float32,
            )
            lane = lax.broadcasted_iota(jnp.int32, (LAG_ROWS, 2 * width), 1)
            for inner in range(chunk):
                lanes = pl.ds(pl.multiple_of((step * chunk + inner) * 2 * width, 2 * width), 2 * width)
                even = product[inner * pair_rows : inner * pair_rows + LAG_ROWS]
                odd = product[inner * pair_rows + LAG_ROWS : (inner + 1) * pair_rows]
                for place in range(0, len(members), 2):
                    both = min(2, len(members) - place)
                    a = even[:, place * width : (place + both) * width]
                    b = odd[:, place * width : (place + both) * width]
                    if both == 1:
                        tiles[buffer, place, :, lanes] = (jnp.concatenate([a, b], axis=1) * scales[place])[:LAGS]
                        continue
                    a_far, b_far = pltpu.roll(a, width, 1), pltpu.roll(b, width, 1)
                    tiles[buffer, place, :, lanes] = (jnp.where(lane < width, a, b_far) * scales[place])[:LAGS]
                    tiles[buffer, place + 1, :, lanes] = (jnp.where(lane < width, a_far, b) * scales[place + 1])[:LAGS]
            return carry

        lax.fori_loop(0, pairs // chunk, multiply, 0)
        out = [
            pltpu.make_async_copy(
                tiles.at[buffer, place], out_ref.at[slot], out_sems.at[buffer, place]
            )
            for place, slot in enumerate(members)
        ]
        for copy in out:
            copy.start()
        sent.append(out)
    for out in sent[-2:]:
        for copy in out:
            copy.wait()


def correlate(own, blobs, place, live, samples, half, norm_scale):
    slots = live.shape[1]
    width, depth = blobs.shape[1:]
    cosine, sine = lag_tables(samples)
    smem = pl.BlockSpec(memory_space=pltpu.SMEM)
    vmem = pl.BlockSpec(memory_space=pltpu.VMEM)
    anywhere = pl.BlockSpec(memory_space=pl.ANY)
    return pl.pallas_call(
        functools.partial(stack_kernel, norm_scale),
        out_shape=jax.ShapeDtypeStruct((slots, LAGS, half * width), jnp.float32),
        in_specs=[smem, smem, vmem, vmem, vmem, anywhere],
        out_specs=anywhere,
        scratch_shapes=[
            pltpu.VMEM((half, depth), jnp.float32),
            pltpu.VMEM((half * LAG_ROWS, depth), jnp.bfloat16),
            pltpu.VMEM((slots, width, depth), jnp.bfloat16),
            pltpu.VMEM((2, 4, LAGS, half * width), jnp.float32),
            pltpu.SemaphoreType.DMA((slots,)),
            pltpu.SemaphoreType.DMA((2, 4)),
        ],
        compiler_params=pltpu.CompilerParams(vmem_limit_bytes=48 * 2**20),
        cost_estimate=pl.CostEstimate(
            flops=2 * half * LAGS * depth * slots * width, bytes_accessed=8 * 2**20, transcendentals=0
        ),
    )(place, live, own, jnp.asarray(cosine), jnp.asarray(sine), blobs)


def places(reach):
    table = np.zeros((QUAD, 2 * reach + 1), np.int32)
    for position in range(QUAD):
        for slot in range(2 * reach + 1):
            other = position + slot - reach
            plane = other // QUAD
            if abs(plane) > 1:
                table[position, slot] = 12
                continue
            swap = (other % QUAD) ^ position
            table[position, slot] = 6 * (swap % 2) + 2 * (plane % 3) + swap // 2
    return table


def local(traces, partners):
    samples = traces.shape[2]
    slots = partners.shape[1]
    reach = (slots - 1) // 2
    segments = lax.axis_size("seg")
    blocks = lax.axis_size("chan")
    half = traces.shape[1] // segments
    assert segments == 2 and blocks % QUAD == 0 and reach == QUAD + 1
    swap = lambda by: [(i, i ^ by) for i in range(blocks)]
    shift = lambda by: [(i, i + by) for i in range(blocks) if 0 <= i + by < blocks]
    far = QUAD + 1
    corners = [(i, i + far) for i in range(QUAD - 1, blocks - far, QUAD)]
    corners += [(i, i - far) for i in range(2 * QUAD, blocks, QUAD)]

    white = spectra(traces[0])
    other = lax.ppermute(white, "seg", [(0, 1), (1, 0)])
    pair = jnp.concatenate([white, other], axis=1)
    quad = jnp.stack([pair, lax.ppermute(pair, "chan", swap(2))])
    corner = lax.ppermute(pair, "chan", corners)
    after = lax.ppermute(quad, "chan", shift(-QUAD))
    before = lax.ppermute(quad, "chan", shift(QUAD))
    mine = jnp.concatenate([quad, after, before], axis=0)
    sibling = lax.ppermute(mine, "chan", swap(1))
    blobs = jnp.concatenate([mine, sibling, corner[None]], axis=0)

    index = lax.axis_index("chan")
    place = jnp.asarray(places(reach))[index % QUAD]
    first = (lax.axis_index("seg") * half).astype(jnp.int32)
    place = jnp.concatenate([place, first[None]])
    norm_scale = (segments * BAND) ** (-0.5)
    return correlate(pair, blobs, place, partners, samples, half, norm_scale)[None]


def solution(mesh):
    placed = (P("seg", "chan", None), P("chan", None))
    return jax.shard_map(
        local, mesh=mesh, in_specs=placed, out_specs=P("chan", None, None, "seg"), check_vma=False
    )
```

time: 159 us -> 59.1 us (0.37)
  the two profiles are of different devices: /device:TPU:0 before, /device:TPU:3 now
where the time goes in v1:
time: 59.1 us; the launch traced here: 58.6 us
  waiting for transfers between devices  16.7 us (28%)
  starting transfers between devices  14.6 us (25%)
  Pallas kernels  13.7 us (23%)
  local copies, waits for them, and re-layouts  13.3 us (23%)
    pallas_call x1, Pallas kernels, correlate(): pl.pallas_call(functools.partial(stack_kernel, norm_scale), out_shape=jax...  12.1 us
    broadcast_in_dim x1, local copies, waits for them, and re-layouts, local(): correlate(pair, blobs, place, partners, samples, half, norm_scale)[None]  8.07 us
    ppermute x1, waiting for transfers between devices, local(): corner = lax.ppermute(pair, 'chan', corners)  5.21 us
    unnamed x20, local copies, waits for them, and re-layouts  4.51 us
    ppermute x1, starting transfers between devices, local(): sibling = lax.ppermute(mine, 'chan', swap(1))  4.47 us
    ppermute x1, starting transfers between devices, local(): corner = lax.ppermute(pair, 'chan', corners)  4.2 us
    ppermute x1, waiting for transfers between devices, local(): after = lax.ppermute(quad, 'chan', shift(-QUAD))  3.83 us
    ppermute x1, waiting for transfers between devices, local(): quad = jnp.stack([pair, lax.ppermute(pair, 'chan', swap(2))])  3.79 us
  transfers between devices with their start and end apart: 6, of which 5 were waited for; matrix products, arithmetic and copies ran while one was open for 2% of the time, Pallas kernels for 0%

profile of v1, /device:TPU:3, one launch (start us, length us, event | category | flops | bytes accessed | tf_op | source)
XLA Modules:
  0.0 58.6 jit_solution(10634037835444192381)
XLA Ops:
  0.0 1.0 %copy-done = bf16[1,64,4096]{2,1,0:T(8,128)(2,1)S(1)} copy-done((bf16[1,64,4096]{2,1,0:T(8,128)(2,1)S(1)}, bf16[1,64,4096]{2,1,0:T(8,128)(2,1)}, u32[]{:S(2)}) %copy-start) | copy-done | bytes 524312
  1.0 0.9 %copy-done.1 = bf16[256,512]{1,0:T(8,128)(2,1)S(1)} copy-done((bf16[256,512]{1,0:T(8,128)(2,1)S(1)}, bf16[256,512]{1,0:T(8,128)(2,1)}, u32[]{:S(2)}) %copy-start.1) | copy-done | bytes 262168
  2.0 0.9 %copy-done.2 = bf16[256,512]{1,0:T(8,128)(2,1)S(1)} copy-done((bf16[256,512]{1,0:T(8,128)(2,1)S(1)}, bf16[256,512]{1,0:T(8,128)(2,1)}, u32[]{:S(2)}) %copy-start.2) | copy-done | bytes 262168
  2.9 0.7 %copy-done.3 = f32[16,256]{1,0:T(8,128)S(1)} copy-done((f32[16,256]{1,0:T(8,128)S(1)}, f32[16,256]{1,0:T(8,128)}, u32[]{:S(2)}) %copy-start.3) | copy-done | bytes 16408
  3.7 0.7 %copy-done.4 = f32[16,256]{1,0:T(8,128)S(1)} copy-done((f32[16,256]{1,0:T(8,128)S(1)}, f32[16,256]{1,0:T(8,128)}, u32[]{:S(2)}) %copy-start.4) | copy-done | bytes 16408
  4.4 1.7 %shard_map.91 = bf16[64,512]{1,0:T(8,128)(2,1)S(1)} custom-call(bf16[64,4096]{1,0:T(8,128)(2,1)S(1)} %bitcast.12, bf16[256,512]{1,0:T(8,128)(2,1)S(1)} %copy-done.2, bf16[256,512]{1,0:T(8,128)(2,1)S(1)} %copy-done.1, f32[16,256]{1,0:T(8,128)S(1)} %copy-done.4, f32[16,256]{1,0:T(8,128)S(1)} %copy-done.3), custom_call_target="tpu_custom_call" | custom-call | tf_op jit(solution)/shard_map/pallas_call | solution.py:67
  6.1 1.3 %collective-permute-start = (bf16[64,512]{1,0:T(8,128)(2,1)S(1)}, bf16[64,512]{1,0:T(8,128)(2,1)S(1)}, u32[]{:S(2)}, u32[]{:S(2)}) collective-permute-start(bf16[64,512]{1,0:T(8,128)(2,1)S(1)} %shard_map.91), channel_id=1, source_target_pairs={{0,16},{16,0},{1,17},{17,1},{2,18},{18,2},{3,19},{19,3},{4,20},{20... | collective-permute-start | bytes 196616 | tf_op jit(solution)/shard_map/ppermute | solution.py:213
  7.4 1.9 %collective-permute-done = bf16[64,512]{1,0:T(8,128)(2,1)S(1)} collective-permute-done((bf16[64,512]{1,0:T(8,128)(2,1)S(1)}, bf16[64,512]{1,0:T(8,128)(2,1)S(1)}, u32[]{:S(2)}, u32[]{:S(2)}) %collective-permute-start) | collective-permute-done | bytes 65568 | tf_op jit(solution)/shard_map/ppermute | solution.py:213
  9.3 0.1 collective-permute-start.1
  9.4 3.8 %collective-permute-done.1 = bf16[64,1024]{1,0:T(8,128)(2,1)S(1)} collective-permute-done((bf16[64,1024]{1,0:T(8,128)(2,1)S(1)}, bf16[64,1024]{1,0:T(8,128)(2,1)S(1)}, u32[]{:S(2)}, u32[]{:S(2)}) %collective-permute-start.1) | collective-permute-done | bytes 131104 | tf_op jit(solution)/shard_map/ppermute | solution.py:215
  13.2 3.2 %collective-permute-start.3 = (bf16[2,64,1024]{2,1,0:T(8,128)(2,1)S(1)}, bf16[2,64,1024]{2,1,0:T(8,128)(2,1)S(1)}, u32[]{:S(2)}, u32[]{:S(2)}) collective-permute-start(bf16[2,64,1024]{2,1,0:T(8,128)(2,1)S(1)} %pad_maximum_fusion.1), channel_id=1, source_target_pairs={{0,4},{1,5},{2,6},{3,7},{4,8},{5,9},{6,10},{7,11},{8,12},{9,13},{1... | collective-permute-start | bytes 786440 | tf_op jit(solution)/shard_map/ppermute | solution.py:218
  16.4 1.3 %collective-permute-start.2 = (bf16[2,64,1024]{2,1,0:T(8,128)(2,1)S(1)}, bf16[2,64,1024]{2,1,0:T(8,128)(2,1)S(1)}, u32[]{:S(2)}, u32[]{:S(2)}) collective-permute-start(bf16[2,64,1024]{2,1,0:T(8,128)(2,1)S(1)} %pad_maximum_fusion.1), channel_id=1, source_target_pairs={{4,0},{5,1},{6,2},{7,3},{8,4},{9,5},{10,6},{11,7},{12,8},{13,9},{1... | collective-permute-start | bytes 786440 | tf_op jit(solution)/shard_map/ppermute | solution.py:217
  17.7 2.0 %collective-permute-done.3 = bf16[2,64,1024]{2,1,0:T(8,128)(2,1)S(1)} collective-permute-done((bf16[2,64,1024]{2,1,0:T(8,128)(2,1)S(1)}, bf16[2,64,1024]{2,1,0:T(8,128)(2,1)S(1)}, u32[]{:S(2)}, u32[]{:S(2)}) %collective-permute-start.3) | collective-permute-done | bytes 262176 | tf_op jit(solution)/shard_map/ppermute | solution.py:218
  19.7 3.8 %collective-permute-done.2 = bf16[2,64,1024]{2,1,0:T(8,128)(2,1)S(1)} collective-permute-done((bf16[2,64,1024]{2,1,0:T(8,128)(2,1)S(1)}, bf16[2,64,1024]{2,1,0:T(8,128)(2,1)S(1)}, u32[]{:S(2)}, u32[]{:S(2)}) %collective-permute-start.2) | collective-permute-done | bytes 262176 | tf_op jit(solution)/shard_map/ppermute | solution.py:217
  23.5 0.1 pad_maximum_fusion
  23.6 4.5 %collective-permute-start.4 = (bf16[6,64,1024]{2,1,0:T(8,128)(2,1)S(1)}, bf16[6,64,1024]{2,1,0:T(8,128)(2,1)S(1)}, u32[]{:S(2)}, u32[]{:S(2)}) collective-permute-start(bf16[6,64,1024]{2,1,0:T(8,128)(2,1)S(1)} %pad_maximum_fusion), channel_id=1, source_target_pairs={{0,1},{1,0},{2,3},{3,2},{4,5},{5,4},{6,7},{7,6},{8,9},{9,8},{10,11... | collective-permute-start | bytes 2359304 | tf_op jit(solution)/shard_map/ppermute | solution.py:220
  28.1 0.7 %dynamic-slice_bitcast_fusion = s32[11]{0:T(128)S(1)} fusion(s32[4,11]{1,0:T(4,128)} %constant.43.clone, s32[]{:T(128)S(6)} %select_n.11), kind=kLoop, calls=%fused_computation.10 | loop fusion | bytes 92 | tf_op jit(solution)/shard_map/squeeze | solution.py:224
  28.8 0.1 pad_add_fusion.place_ref
  28.9 4.2 %collective-permute-start.5 = (bf16[64,1024]{1,0:T(8,128)(2,1)S(1)}, bf16[64,1024]{1,0:T(8,128)(2,1)S(1)}, u32[]{:S(2)}, u32[]{:S(2)}) collective-permute-start(bf16[64,1024]{1,0:T(8,128)(2,1)S(1)} %get-tuple-element.6.own_ref), channel_id=1, source_target_pairs={{3,8},{7,12},{8,3},{12,7},{19,24},{23,28},{24,19},{28,23}} | collective-permute-start | bytes 393224 | tf_op jit(solution)/shard_map/ppermute | solution.py:216
  33.2 0.0 collective-permute-done.4
  33.2 0.1 constant_dynamic-update-slice_fusion
  33.3 5.2 %collective-permute-done.5 = bf16[64,1024]{1,0:T(8,128)(2,1)S(1)} collective-permute-done((bf16[64,1024]{1,0:T(8,128)(2,1)S(1)}, bf16[64,1024]{1,0:T(8,128)(2,1)S(1)}, u32[]{:S(2)}, u32[]{:S(2)}) %collective-permute-start.5) | collective-permute-done | bytes 131104 | tf_op jit(solution)/shard_map/ppermute | solution.py:216
  38.5 12.1 %shard_map.92 = f32[11,65,2048]{2,1,0:T(8,128)} custom-call(s32[12]{0:T(128)S(1)} %pad_add_fusion.place_ref, s32[1,11]{1,0:T(1,128)S(1)} %copy-done.5, bf16[64,1024]{1,0:T(8,128)(2,1)S(1)} %get-tuple-element.6.own_ref, f32[72,256]{1,0:T(8,128)S(1)} %copy-done.7, f32[72,256]{1,0:T(8,128)S(1)} %copy-done.6, ...), custom_call_target="tpu_custom_call" | custom-call | flops 2998927360 | bytes 8388608 | tf_op jit(solution)/shard_map/pallas_call | solution.py:164
  50.6 8.1 %copy.10 = f32[1,11,65,2048]{3,0,2,1:T(1,128)} copy(f32[1,11,65,2048]{3,2,1,0:T(8,128)} %bitcast.13) | data formatting | bytes 11714560 | tf_op jit(solution)/shard_map/broadcast_in_dim | solution.py:228
  (18 shorter events, 0.1 us)
Async XLA Ops:
  0.0 1.0 %copy-start = (bf16[1,64,4096]{2,1,0:T(8,128)(2,1)S(1)}, bf16[1,64,4096]{2,1,0:T(8,128)(2,1)}, u32[]{:S(2)}) copy-start(bf16[1,64,4096]{2,1,0:T(8,128)(2,1)} %param.9) | copy-start | bytes 1572868
  1.0 0.9 %copy-start.1 = (bf16[256,512]{1,0:T(8,128)(2,1)S(1)}, bf16[256,512]{1,0:T(8,128)(2,1)}, u32[]{:S(2)}) copy-start(bf16[256,512]{1,0:T(8,128)(2,1)} %constant.40.clone.low_ref) | copy-start | bytes 786436
  2.0 0.9 %copy-start.2 = (bf16[256,512]{1,0:T(8,128)(2,1)S(1)}, bf16[256,512]{1,0:T(8,128)(2,1)}, u32[]{:S(2)}) copy-start(bf16[256,512]{1,0:T(8,128)(2,1)} %constant.39.clone.high_ref) | copy-start | bytes 786436
  2.9 0.7 %copy-start.3 = (f32[16,256]{1,0:T(8,128)S(1)}, f32[16,256]{1,0:T(8,128)}, u32[]{:S(2)}) copy-start(f32[16,256]{1,0:T(8,128)} %constant.42.clone.sin_ref) | copy-start | bytes 49156
  3.7 0.7 %copy-start.4 = (f32[16,256]{1,0:T(8,128)S(1)}, f32[16,256]{1,0:T(8,128)}, u32[]{:S(2)}) copy-start(f32[16,256]{1,0:T(8,128)} %constant.41.clone.cos_ref) | copy-start | bytes 49156
  6.1 3.2 %collective-permute-start = (bf16[64,512]{1,0:T(8,128)(2,1)S(1)}, bf16[64,512]{1,0:T(8,128)(2,1)S(1)}, u32[]{:S(2)}, u32[]{:S(2)}) collective-permute-start(bf16[64,512]{1,0:T(8,128)(2,1)S(1)} %shard_map.91), channel_id=1, source_target_pairs={{0,16},{16,0},{1,17},{17,1},{2,18},{18,2},{3,19},{19,3},{4,20},{20... | collective-permute-start | bytes 196616 | tf_op jit(solution)/shard_map/ppermute | solution.py:213
  9.3 3.9 %collective-permute-start.1 = (bf16[64,1024]{1,0:T(8,128)(2,1)S(1)}, bf16[64,1024]{1,0:T(8,128)(2,1)S(1)}, u32[]{:S(2)}, u32[]{:S(2)}) collective-permute-start(bf16[64,1024]{1,0:T(8,128)(2,1)S(1)} %get-tuple-element.6.own_ref), channel_id=1, source_target_pairs={{0,2},{1,3},{2,0},{3,1},{4,6},{5,7},{6,4},{7,5},{8,10},{9,11},{10,... | collective-permute-start | bytes 393224 | tf_op jit(solution)/shard_map/ppermute | solution.py:215
  13.2 6.5 %collective-permute-start.3 = (bf16[2,64,1024]{2,1,0:T(8,128)(2,1)S(1)}, bf16[2,64,1024]{2,1,0:T(8,128)(2,1)S(1)}, u32[]{:S(2)}, u32[]{:S(2)}) collective-permute-start(bf16[2,64,1024]{2,1,0:T(8,128)(2,1)S(1)} %pad_maximum_fusion.1), channel_id=1, source_target_pairs={{0,4},{1,5},{2,6},{3,7},{4,8},{5,9},{6,10},{7,11},{8,12},{9,13},{1... | collective-permute-start | bytes 786440 | tf_op jit(solution)/shard_map/ppermute | solution.py:218
  16.4 7.1 %collective-permute-start.2 = (bf16[2,64,1024]{2,1,0:T(8,128)(2,1)S(1)}, bf16[2,64,1024]{2,1,0:T(8,128)(2,1)S(1)}, u32[]{:S(2)}, u32[]{:S(2)}) collective-permute-start(bf16[2,64,1024]{2,1,0:T(8,128)(2,1)S(1)} %pad_maximum_fusion.1), channel_id=1, source_target_pairs={{4,0},{5,1},{6,2},{7,3},{8,4},{9,5},{10,6},{11,7},{12,8},{13,9},{1... | collective-permute-start | bytes 786440 | tf_op jit(solution)/shard_map/ppermute | solution.py:217
  23.6 9.5 %collective-permute-start.4 = (bf16[6,64,1024]{2,1,0:T(8,128)(2,1)S(1)}, bf16[6,64,1024]{2,1,0:T(8,128)(2,1)S(1)}, u32[]{:S(2)}, u32[]{:S(2)}) collective-permute-start(bf16[6,64,1024]{2,1,0:T(8,128)(2,1)S(1)} %pad_maximum_fusion), channel_id=1, source_target_pairs={{0,1},{1,0},{2,3},{3,2},{4,5},{5,4},{6,7},{7,6},{8,9},{9,8},{10,11... | collective-permute-start | bytes 2359304 | tf_op jit(solution)/shard_map/ppermute | solution.py:220
  28.9 9.6 %copy-start.5 = (s32[1,11]{1,0:T(1,128)S(1)}, s32[1,11]{1,0:T(1,128)}, u32[]{:S(2)}) copy-start(s32[1,11]{1,0:T(1,128)} %live_ref.1) | copy-start | bytes 136
  28.9 9.6 %copy-start.6 = (f32[72,256]{1,0:T(8,128)S(1)}, f32[72,256]{1,0:T(8,128)}, u32[]{:S(2)}) copy-start(f32[72,256]{1,0:T(8,128)} %constant.45.clone.sin_ref) | copy-start | bytes 221188
  28.9 9.6 %copy-start.7 = (f32[72,256]{1,0:T(8,128)S(1)}, f32[72,256]{1,0:T(8,128)}, u32[]{:S(2)}) copy-start(f32[72,256]{1,0:T(8,128)} %constant.44.clone.cos_ref) | copy-start | bytes 221188
  28.9 9.6 %collective-permute-start.5 = (bf16[64,1024]{1,0:T(8,128)(2,1)S(1)}, bf16[64,1024]{1,0:T(8,128)(2,1)S(1)}, u32[]{:S(2)}, u32[]{:S(2)}) collective-permute-start(bf16[64,1024]{1,0:T(8,128)(2,1)S(1)} %get-tuple-element.6.own_ref), channel_id=1, source_target_pairs={{3,8},{7,12},{8,3},{12,7},{19,24},{23,28},{24,19},{28,23}} | collective-permute-start | bytes 393224 | tf_op jit(solution)/shard_map/ppermute | solution.py:216

commit v2 on v1

v2 whole, which is shorter than its diff:
```python
import functools
import math

import jax
import jax.numpy as jnp
import numpy as np
from jax import lax
from jax.experimental import pallas as pl
from jax.experimental.pallas import tpu as pltpu
from jax.sharding import PartitionSpec as P

BAND = 256
BAND_LO = 16
LAG = 32
LAGS = 2 * LAG + 1
REACH = 5
QUAD = 4
SPECTRUM_VMEM = 56 * 2**20
KERNEL_VMEM = 24 * 2**20

water_level = 0.5
epsilon = 1e-06


def split_table(samples, step):
    bins = np.arange(BAND) + BAND_LO
    angle = (np.arange(step)[:, None] * bins[None, :] % samples) * (2.0 * math.pi / samples)
    table = np.concatenate([np.cos(angle), -np.sin(angle)], axis=1).astype(np.float32)
    high = table.astype(jnp.bfloat16)
    low = (table - high.astype(np.float32)).astype(jnp.bfloat16)
    stretches = samples // step
    turn = (np.arange(stretches)[:, None] * step * bins[None, :] % samples) * (2.0 * math.pi / samples)
    return high, low, np.cos(turn).astype(np.float32), np.sin(turn).astype(np.float32)


def lag_tables(samples):
    bins = np.arange(BAND) + BAND_LO
    shifts = np.arange(LAGS) - LAG
    angle = (shifts[:, None] * bins[None, :] % samples) * (2.0 * math.pi / samples)
    return np.stack([np.cos(angle), np.sin(angle)]).astype(np.float32)


def spectrum_kernel(step, traces_hbm, table_hbm, turn_hbm, white_ref, traces, table, turn, sems):
    copies = [
        pltpu.make_async_copy(table_hbm, table, sems.at[0]),
        pltpu.make_async_copy(traces_hbm, traces, sems.at[1]),
        pltpu.make_async_copy(turn_hbm, turn, sems.at[2]),
    ]
    for copy in copies:
        copy.start()
    for copy in copies:
        copy.wait()
    real = imag = None
    for stretch in range(traces.shape[1] // step):
        part = traces[:, stretch * step : (stretch + 1) * step]
        y = jnp.dot(part, table[0], preferred_element_type=jnp.float32)
        y = y + jnp.dot(part, table[1], preferred_element_type=jnp.float32)
        y_real, y_imag = y[:, :BAND], y[:, BAND:]
        if stretch == 0:
            real, imag = y_real, y_imag
            continue
        cosine = turn[0, stretch : stretch + 1, :]
        sine = turn[1, stretch : stretch + 1, :]
        real = real + (y_real * cosine + y_imag * sine)
        imag = imag + (y_imag * cosine - y_real * sine)
    power = real * real + imag * imag
    level = jnp.mean(power, axis=1, keepdims=True)
    denom = jnp.sqrt(power + water_level * level + epsilon)
    white_ref[:, :BAND] = (real / denom).astype(jnp.bfloat16)
    white_ref[:, BAND:] = (imag / denom).astype(jnp.bfloat16)


def spectra(traces):
    channels, samples = traces.shape
    step = 256
    high, low, cosine, sine = split_table(samples, step)
    table, turn = np.stack([high, low]), np.stack([cosine, sine])
    anywhere = pl.BlockSpec(memory_space=pl.ANY)
    return pl.pallas_call(
        functools.partial(spectrum_kernel, step),
        out_shape=jax.ShapeDtypeStruct((channels, 2 * BAND), jnp.bfloat16),
        in_specs=[anywhere] * 3,
        out_specs=pl.BlockSpec(memory_space=pltpu.VMEM),
        scratch_shapes=[
            pltpu.VMEM(traces.shape, traces.dtype),
            pltpu.VMEM(table.shape, jnp.bfloat16),
            pltpu.VMEM(turn.shape, jnp.float32),
            pltpu.SemaphoreType.DMA((3,)),
        ],
        compiler_params=pltpu.CompilerParams(vmem_limit_bytes=SPECTRUM_VMEM),
    )(traces, jnp.asarray(table), jnp.asarray(turn))


def rows_kernel(pair_ref, lag_ref, rows_ref, stage, own):
    pairs = own.shape[1]
    first = pl.multiple_of(lax.axis_index("seg") * 2 * pairs, 2 * pairs)
    mine = pair_ref[pl.ds(first, 2 * pairs), :].astype(jnp.float32)
    for left in range(0, mine.shape[1], 128):
        stage[...] = mine[:, left : left + 128]
        for member in range(2):
            own[member, :, left : left + 128] = stage[pl.ds(member, pairs, stride=2), :]

    def turn(lag, carry):
        cosine = lag_ref[0, pl.ds(lag, 1), :]
        sine = lag_ref[1, pl.ds(lag, 1), :]
        at = pl.ds(pl.multiple_of(lag * pairs, pairs), pairs)
        for member in range(2):
            for left in range(0, own.shape[2], 2 * BAND):
                middle, right = left + BAND, left + 2 * BAND
                real, imag = own[member, :, left:middle], own[member, :, middle:right]
                rows_ref[member, at, left:middle] = (real * cosine - imag * sine).astype(jnp.bfloat16)
                rows_ref[member, at, middle:right] = (real * sine + imag * cosine).astype(jnp.bfloat16)
        return carry

    lax.fori_loop(0, LAGS, turn, 0, unroll=5)


def lag_rows(pair, samples, half):
    depth = pair.shape[1]
    vmem = pl.BlockSpec(memory_space=pltpu.VMEM)
    return pl.pallas_call(
        rows_kernel,
        out_shape=jax.ShapeDtypeStruct((2, LAGS * half // 2, depth), jnp.bfloat16),
        in_specs=[vmem] * 2,
        out_specs=vmem,
        scratch_shapes=[pltpu.VMEM((half, 128), jnp.float32), pltpu.VMEM((2, half // 2, depth), jnp.float32)],
        compiler_params=pltpu.CompilerParams(vmem_limit_bytes=KERNEL_VMEM),
        cost_estimate=pl.CostEstimate(flops=6 * half * LAGS * depth, bytes_accessed=2**20, transcendentals=0),
    )(pair, jnp.asarray(lag_tables(samples)))


def multiply(rows, partner, scale, tile):
    members = len(scale)
    width = partner.shape[0] // members
    even, odd = [
        lax.dot_general(rows[m], partner, (((1,), (1,)), ((), ())), preferred_element_type=jnp.float32)
        for m in range(2)
    ]
    lane = lax.broadcasted_iota(jnp.int32, (even.shape[0], 2 * width), 1)
    for n in range(0, members, 2):
        a, b = even[:, n * width : (n + 2) * width], odd[:, n * width : (n + 2) * width]
        if n + 1 == members:
            tile[n][...] = jnp.concatenate([a, b], axis=1) * scale[n]
            continue
        tile[n][...] = jnp.where(lane < width, a, pltpu.roll(b, width, 1)) * scale[n]
        tile[n + 1][...] = jnp.where(lane < width, pltpu.roll(a, width, 1), b) * scale[n + 1]


def position():
    place = lax.rem(lax.axis_index("chan"), QUAD)
    return place, REACH - place


def slot_of(place, plane, swap_x, swap_core):
    step_x = 2 - 4 * lax.div(place, 2)
    step_core = 1 - 2 * lax.rem(place, 2)
    return REACH + QUAD * plane + swap_x * step_x + swap_core * step_core


def near_kernel(rows_ref, scale_ref, quad_ref, sibling_ref, out_ref, window, tiles, sems):
    place, _ = position()
    width = quad_ref.shape[1]
    for core, ref in enumerate((quad_ref, sibling_ref)):
        for x in range(2):
            n = 2 * core + x
            window[n * width : (n + 1) * width] = ref[x]
    slots = [slot_of(place, 0, n % 2, n // 2) for n in range(QUAD)]
    scale = [scale_ref[pl.ds(slot, 1), :] for slot in slots]
    multiply([rows_ref[0], rows_ref[1]], window[...], scale, [tiles.at[n] for n in range(QUAD)])
    copies = [
        pltpu.make_async_copy(tiles.at[n], out_ref.at[slot], sems.at[n]) for n, slot in enumerate(slots)
    ]
    for copy in copies:
        copy.start()
    for copy in copies:
        copy.wait()


def far_kernel(rows_ref, scale_ref, after_ref, before_ref, sib_after_ref, sib_before_ref, corner_ref, near_ref,
               out_ref, window, tiles, sems):
    del near_ref
    place, first = position()
    width = corner_ref.shape[0]
    total = tiles.shape[0]

    def put(slot, valid, value):
        at = jnp.where(slot < first, slot, slot - QUAD)

        @pl.when(valid)
        def _():
            window[pl.ds(pl.multiple_of(at * width, width), width), :] = value()

    blobs = ((after_ref, 1, 0), (before_ref, -1, 0), (sib_after_ref, 1, 1), (sib_before_ref, -1, 1))
    for ref, plane, core in blobs:
        for x in range(2):
            slot = slot_of(place, plane, x, core)
            put(slot, (slot >= 0) & (slot <= 2 * REACH), lambda ref=ref, x=x: ref[x])
    put(jnp.where(place == 0, 0, 2 * REACH), (place == 0) | (place == QUAD - 1), lambda: corner_ref[...])

    copies = []
    for start in range(0, total, QUAD):
        members = range(start, min(start + QUAD, total))
        slots = [jnp.where(n < first, n, n + QUAD) for n in members]
        scale = [scale_ref[pl.ds(slot, 1), :] for slot in slots]
        partner = window[start * width : (start + len(members)) * width]
        multiply([rows_ref[0], rows_ref[1]], partner, scale, [tiles.at[n] for n in members])
        for n, slot in zip(members, slots):
            copy = pltpu.make_async_copy(tiles.at[n], out_ref.at[slot], sems.at[n])
            copy.start()
            copies.append(copy)
    for copy in copies:
        copy.wait()


def correlate(kernel, rows, scale, blobs, out, count):
    width, depth = blobs[0].shape[-2:]
    lines = rows.shape[1]
    vmem = pl.BlockSpec(memory_space=pltpu.VMEM)
    anywhere = pl.BlockSpec(memory_space=pl.ANY)
    extra = [] if out is None else [out]
    operands = [rows, scale, *blobs, *extra]
    return pl.pallas_call(
        kernel,
        out_shape=jax.ShapeDtypeStruct((scale.shape[0], lines, 2 * width), jnp.float32),
        in_specs=[vmem] * (2 + len(blobs)) + [anywhere] * len(extra),
        out_specs=anywhere,
        scratch_shapes=[
            pltpu.VMEM((count * width, depth), jnp.bfloat16),
            pltpu.VMEM((count, lines, 2 * width), jnp.float32),
            pltpu.SemaphoreType.DMA((count,)),
        ],
        input_output_aliases={len(operands) - 1: 0} if extra else {},
        compiler_params=pltpu.CompilerParams(vmem_limit_bytes=KERNEL_VMEM),
        cost_estimate=pl.CostEstimate(
            flops=4 * lines * depth * count * width, bytes_accessed=8 * count * lines * width, transcendentals=0
        ),
    )(*operands)


def local(traces, partners):
    samples = traces.shape[2]
    slots = partners.shape[1]
    segments = lax.axis_size("seg")
    blocks = lax.axis_size("chan")
    channels = traces.shape[1]
    half = channels // segments
    assert segments == 2 and blocks % QUAD == 0 and slots == 2 * REACH + 1
    swap = lambda by: [(i, i ^ by) for i in range(blocks)]
    shift = lambda by: [(i, i + by) for i in range(blocks) if 0 <= i + by < blocks]
    corners = [(i, i + REACH) for i in range(QUAD - 1, blocks - REACH, QUAD)]
    corners += [(i, i - REACH) for i in range(2 * QUAD, blocks, QUAD)]
    norm_scale = (segments * BAND) ** (-0.5)
    scale = jnp.where(partners[0] >= 0, norm_scale, 0.0).astype(jnp.float32)
    scale = jnp.broadcast_to(scale[:, None], (slots, 2 * channels))

    white = spectra(traces[0])
    other = lax.ppermute(white, "seg", [(0, 1), (1, 0)])
    pair = jnp.concatenate([white, other], axis=1)
    rows = lag_rows(pair, samples, half)
    quad = jnp.stack([pair, lax.ppermute(pair, "chan", swap(2))])
    corner = lax.ppermute(pair, "chan", corners)
    after = lax.ppermute(quad, "chan", shift(-QUAD))
    before = lax.ppermute(quad, "chan", shift(QUAD))
    out = correlate(near_kernel, rows, scale, [quad, lax.ppermute(quad, "chan", swap(1))], None, QUAD)
    sib_after = lax.ppermute(after, "chan", swap(1))
    sib_before = lax.ppermute(before, "chan", swap(1))
    blobs = [after, before, sib_after, sib_before, corner]
    out = correlate(far_kernel, rows, scale, blobs, out, slots - QUAD)
    return out.reshape(1, slots, LAGS, half * channels)


def solution(mesh):
    placed = (P("seg", "chan", None), P("chan", None))
    return jax.shard_map(
        local, mesh=mesh, in_specs=placed, out_specs=P("chan", None, None, "seg"), check_vma=False
    )
```

time: 59.1 us -> 37.4 us (0.63)
  the two profiles are of different devices: /device:TPU:3 before, /device:TPU:1 now
where the time goes in v2:
time: 37.4 us; the launch traced here: 37.2 us
  starting transfers between devices  18.6 us (50%)
  Pallas kernels  11.7 us (31%)
  waiting for transfers between devices  4.27 us (11%)
  other arithmetic  1.54 us (4%)
  local copies, waits for them, and re-layouts  0.98 us (3%)
    pallas_call x2, Pallas kernels, correlate(): pl.pallas_call(kernel, out_shape=jax.ShapeDtypeStruct((scale.shape[0], li...  6.93 us
    ppermute x1, starting transfers between devices, local(): sib_after = lax.ppermute(after, 'chan', swap(1))  4.4 us
    pallas_call x1, Pallas kernels, spectra(): pl.pallas_call(functools.partial(spectrum_kernel, step), out_shape=jax.Sh...  3.54 us
    ppermute x1, starting transfers between devices, local(): before = lax.ppermute(quad, 'chan', shift(QUAD))  3.44 us
    ppermute x1, starting transfers between devices, local(): lax.ppermute(quad, 'chan', swap(1))  3.32 us
    ppermute x1, waiting for transfers between devices, local(): quad = jnp.stack([pair, lax.ppermute(pair, 'chan', swap(2))])  2.39 us
    ppermute x1, starting transfers between devices, local(): other = lax.ppermute(white, 'seg', [(0, 1), (1, 0)])  2.14 us
    ppermute x1, waiting for transfers between devices, local(): other = lax.ppermute(white, 'seg', [(0, 1), (1, 0)])  1.87 us
  transfers between devices with their start and end apart: 8, of which 2 were waited for; matrix products, arithmetic and copies ran while one was open for 2% of the time, Pallas kernels for 11%

profile of v2, /device:TPU:1, one launch (start us, length us, event | category | flops | bytes accessed | tf_op | source)
XLA Modules:
  0.0 37.2 jit_solution(14399462146351187171)
XLA Ops:
  0.0 3.5 %shard_map.55 = bf16[64,512]{1,0:T(8,128)(2,1)} custom-call(bf16[64,4096]{1,0:T(8,128)(2,1)} %bitcast.7, bf16[2,256,512]{2,1,0:T(8,128)(2,1)} %constant.12.clone.table_hbm, f32[2,16,256]{2,1,0:T(8,128)} %constant.13.clone.turn_hbm), custom_call_target="tpu_custom_call" | custom-call | tf_op jit(solution)/shard_map/pallas_call | solution.py:79
  3.5 2.1 %collective-permute-start = (bf16[64,512]{1,0:T(8,128)(2,1)}, bf16[64,512]{1,0:T(8,128)(2,1)S(1)}, u32[]{:S(2)}, u32[]{:S(2)}) collective-permute-start(bf16[64,512]{1,0:T(8,128)(2,1)} %shard_map.55), channel_id=1, source_target_pairs={{0,16},{16,0},{1,17},{17,1},{2,18},{18,2},{3,19},{19,3},{4,20},{20... | collective-permute-start | bytes 196616 | tf_op jit(solution)/shard_map/ppermute | solution.py:257
  5.7 1.9 %collective-permute-done = bf16[64,512]{1,0:T(8,128)(2,1)S(1)} collective-permute-done((bf16[64,512]{1,0:T(8,128)(2,1)}, bf16[64,512]{1,0:T(8,128)(2,1)S(1)}, u32[]{:S(2)}, u32[]{:S(2)}) %collective-permute-start) | collective-permute-done | bytes 65568 | tf_op jit(solution)/shard_map/ppermute | solution.py:257
  7.5 0.9 %fusion.1 = (bf16[1,64,1024]{2,1,0:T(8,128)(2,1)S(1)}, bf16[64,1024]{1,0:T(8,128)(2,1)S(1)}) fusion(bf16[64,512]{1,0:T(8,128)(2,1)S(1)} %collective-permute-done, bf16[64,512]{1,0:T(8,128)(2,1)} %shard_map.55), kind=kLoop, calls=%fused_computation.4 | loop fusion | flops 262144 | bytes 393216 | tf_op jit(solution)/shard_map/stack | solution.py:260
  8.4 1.5 %collective-permute-start.1 = (bf16[64,1024]{1,0:T(8,128)(2,1)S(1)}, bf16[64,1024]{1,0:T(8,128)(2,1)S(1)}, u32[]{:S(2)}, u32[]{:S(2)}) collective-permute-start(bf16[64,1024]{1,0:T(8,128)(2,1)S(1)} %get-tuple-element.6.pair_ref), channel_id=1, source_target_pairs={{0,2},{1,3},{2,0},{3,1},{4,6},{5,7},{6,4},{7,5},{8,10},{9,11},{10,... | collective-permute-start | bytes 393224 | tf_op jit(solution)/shard_map/ppermute | solution.py:260
  9.9 2.4 %collective-permute-done.1 = bf16[64,1024]{1,0:T(8,128)(2,1)S(1)} collective-permute-done((bf16[64,1024]{1,0:T(8,128)(2,1)S(1)}, bf16[64,1024]{1,0:T(8,128)(2,1)S(1)}, u32[]{:S(2)}, u32[]{:S(2)}) %collective-permute-start.1) | collective-permute-done | bytes 131104 | tf_op jit(solution)/shard_map/ppermute | solution.py:260
  12.3 3.4 %collective-permute-start.3 = (bf16[2,64,1024]{2,1,0:T(8,128)(2,1)S(1)}, bf16[2,64,1024]{2,1,0:T(8,128)(2,1)S(1)}, u32[]{:S(2)}, u32[]{:S(2)}) collective-permute-start(bf16[2,64,1024]{2,1,0:T(8,128)(2,1)S(1)} %pad_maximum_fusion.quad_ref), channel_id=1, source_target_pairs={{0,4},{1,5},{2,6},{3,7},{4,8},{5,9},{6,10},{7,11},{8,12},{9,13},{1... | collective-permute-start | bytes 786440 | tf_op jit(solution)/shard_map/ppermute | solution.py:263
  15.8 1.3 %collective-permute-start.2 = (bf16[2,64,1024]{2,1,0:T(8,128)(2,1)S(1)}, bf16[2,64,1024]{2,1,0:T(8,128)(2,1)S(1)}, u32[]{:S(2)}, u32[]{:S(2)}) collective-permute-start(bf16[2,64,1024]{2,1,0:T(8,128)(2,1)S(1)} %pad_maximum_fusion.quad_ref), channel_id=1, source_target_pairs={{4,0},{5,1},{6,2},{7,3},{8,4},{9,5},{10,6},{11,7},{12,8},{13,9},{1... | collective-permute-start | bytes 786440 | tf_op jit(solution)/shard_map/ppermute | solution.py:262
  17.1 3.3 %collective-permute-start.7 = (bf16[2,64,1024]{2,1,0:T(8,128)(2,1)S(1)}, bf16[2,64,1024]{2,1,0:T(8,128)(2,1)S(1)}, u32[]{:S(2)}, u32[]{:S(2)}) collective-permute-start(bf16[2,64,1024]{2,1,0:T(8,128)(2,1)S(1)} %pad_maximum_fusion.quad_ref), channel_id=1, source_target_pairs={{0,1},{1,0},{2,3},{3,2},{4,5},{5,4},{6,7},{7,6},{8,9},{9,8},{10,11... | collective-permute-start | bytes 786440 | tf_op jit(solution)/shard_map/ppermute | solution.py:264
  20.4 0.7 %collective-permute-start.6 = (bf16[64,1024]{1,0:T(8,128)(2,1)S(1)}, bf16[64,1024]{1,0:T(8,128)(2,1)S(1)}, u32[]{:S(2)}, u32[]{:S(2)}) collective-permute-start(bf16[64,1024]{1,0:T(8,128)(2,1)S(1)} %get-tuple-element.6.pair_ref), channel_id=1, source_target_pairs={{3,8},{7,12},{8,3},{12,7},{19,24},{23,28},{24,19},{28,23}} | collective-permute-start | bytes 393224 | tf_op jit(solution)/shard_map/ppermute | solution.py:261
  21.1 0.0 collective-permute-done.3.before_ref
  21.1 1.8 %collective-permute-start.5 = (bf16[2,64,1024]{2,1,0:T(8,128)(2,1)S(1)}, bf16[2,64,1024]{2,1,0:T(8,128)(2,1)S(1)}, u32[]{:S(2)}, u32[]{:S(2)}) collective-permute-start(bf16[2,64,1024]{2,1,0:T(8,128)(2,1)S(1)} %collective-permute-done.3.before_ref), channel_id=1, source_target_pairs={{0,1},{1,0},{2,3},{3,2},{4,5},{5,4},{6,7},{7,6},{8,9},{9,8},{10,11... | collective-permute-start | bytes 786440 | tf_op jit(solution)/shard_map/ppermute | solution.py:266
  22.9 0.0 collective-permute-done.2.after_ref
  22.9 4.4 %collective-permute-start.4 = (bf16[2,64,1024]{2,1,0:T(8,128)(2,1)S(1)}, bf16[2,64,1024]{2,1,0:T(8,128)(2,1)S(1)}, u32[]{:S(2)}, u32[]{:S(2)}) collective-permute-start(bf16[2,64,1024]{2,1,0:T(8,128)(2,1)S(1)} %collective-permute-done.2.after_ref), channel_id=1, source_target_pairs={{0,1},{1,0},{2,3},{3,2},{4,5},{5,4},{6,7},{7,6},{8,9},{9,8},{10,11... | collective-permute-start | bytes 786440 | tf_op jit(solution)/shard_map/ppermute | solution.py:265
  27.3 0.7 %fusion = f32[11]{0:T(128)S(1)} fusion(s32[1,11]{1,0:T(1,128)} %param.6), kind=kLoop, calls=%fused_computation.3 | loop fusion | flops 22 | bytes 88 | tf_op jit(solution)/shard_map/jit(_where)/select_n | solution.py:253
  28.0 0.9 %copy-done = f32[2,65,256]{2,1,0:T(8,128)S(1)} copy-done((f32[2,65,256]{2,1,0:T(8,128)S(1)}, f32[2,65,256]{2,1,0:T(8,128)}, u32[]{:S(2)}) %copy-start) | copy-done | bytes 133144
  28.9 1.3 %shard_map.56.rows_ref = bf16[2,1040,1024]{2,1,0:T(8,128)(2,1)S(1)} custom-call(bf16[64,1024]{1,0:T(8,128)(2,1)S(1)} %get-tuple-element.6.pair_ref, f32[2,65,256]{2,1,0:T(8,128)S(1)} %copy-done), custom_call_target="tpu_custom_call" | custom-call | flops 12779520 | bytes 1048576 | tf_op jit(solution)/shard_map/pallas_call | solution.py:121
  30.1 0.0 collective-permute-done.7.sibling_ref
  30.1 0.1 broadcast_in_dim.16.scale_ref
  30.2 3.0 %shard_map.57.near_ref = f32[11,1040,128]{2,1,0:T(8,128)} custom-call(bf16[2,1040,1024]{2,1,0:T(8,128)(2,1)S(1)} %shard_map.56.rows_ref, f32[11,128]{1,0:T(8,128)S(1)} %broadcast_in_dim.16.scale_ref, bf16[2,64,1024]{2,1,0:T(8,128)(2,1)S(1)} %pad_maximum_fusion.quad_ref, bf16[2,64,1024]{2,1,0:T(8,128)(2,1)S(1)} %collective-permute-done.7.sibling_ref), custom_call_target="tpu_custom_call" | custom-call | flops 1090519040 | bytes 2129920 | tf_op jit(solution)/shard_map/pallas_call | solution.py:222
  33.2 0.0 collective-permute-done.6.corner_ref
  33.2 0.0 collective-permute-done.5.sib_before_ref
  33.2 0.0 collective-permute-done.4.sib_after_ref
  33.3 3.9 %shard_map.58 = f32[11,1040,128]{2,1,0:T(8,128)} custom-call(bf16[2,1040,1024]{2,1,0:T(8,128)(2,1)S(1)} %shard_map.56.rows_ref, f32[11,128]{1,0:T(8,128)S(1)} %broadcast_in_dim.16.scale_ref, bf16[2,64,1024]{2,1,0:T(8,128)(2,1)S(1)} %collective-permute-done.2.after_ref, ...), custom_call_target="tpu_custom_call", output_to_operand_aliasing={{}: (7, {})} | custom-call | flops 1908408320 | bytes 3727360 | tf_op jit(solution)/shard_map/pallas_call | solution.py:222
  (2 shorter events, 0.0 us)
Async XLA Ops:
  3.5 4.0 %collective-permute-start = (bf16[64,512]{1,0:T(8,128)(2,1)}, bf16[64,512]{1,0:T(8,128)(2,1)S(1)}, u32[]{:S(2)}, u32[]{:S(2)}) collective-permute-start(bf16[64,512]{1,0:T(8,128)(2,1)} %shard_map.55), channel_id=1, source_target_pairs={{0,16},{16,0},{1,17},{17,1},{2,18},{18,2},{3,19},{19,3},{4,20},{20... | collective-permute-start | bytes 196616 | tf_op jit(solution)/shard_map/ppermute | solution.py:257
  8.4 3.9 %collective-permute-start.1 = (bf16[64,1024]{1,0:T(8,128)(2,1)S(1)}, bf16[64,1024]{1,0:T(8,128)(2,1)S(1)}, u32[]{:S(2)}, u32[]{:S(2)}) collective-permute-start(bf16[64,1024]{1,0:T(8,128)(2,1)S(1)} %get-tuple-element.6.pair_ref), channel_id=1, source_target_pairs={{0,2},{1,3},{2,0},{3,1},{4,6},{5,7},{6,4},{7,5},{8,10},{9,11},{10,... | collective-permute-start | bytes 393224 | tf_op jit(solution)/shard_map/ppermute | solution.py:260
  12.3 8.7 %collective-permute-start.3 = (bf16[2,64,1024]{2,1,0:T(8,128)(2,1)S(1)}, bf16[2,64,1024]{2,1,0:T(8,128)(2,1)S(1)}, u32[]{:S(2)}, u32[]{:S(2)}) collective-permute-start(bf16[2,64,1024]{2,1,0:T(8,128)(2,1)S(1)} %pad_maximum_fusion.quad_ref), channel_id=1, source_target_pairs={{0,4},{1,5},{2,6},{3,7},{4,8},{5,9},{6,10},{7,11},{8,12},{9,13},{1... | collective-permute-start | bytes 786440 | tf_op jit(solution)/shard_map/ppermute | solution.py:263
  15.8 7.1 %collective-permute-start.2 = (bf16[2,64,1024]{2,1,0:T(8,128)(2,1)S(1)}, bf16[2,64,1024]{2,1,0:T(8,128)(2,1)S(1)}, u32[]{:S(2)}, u32[]{:S(2)}) collective-permute-start(bf16[2,64,1024]{2,1,0:T(8,128)(2,1)S(1)} %pad_maximum_fusion.quad_ref), channel_id=1, source_target_pairs={{4,0},{5,1},{6,2},{7,3},{8,4},{9,5},{10,6},{11,7},{12,8},{13,9},{1... | collective-permute-start | bytes 786440 | tf_op jit(solution)/shard_map/ppermute | solution.py:262
  17.1 13.1 %collective-permute-start.7 = (bf16[2,64,1024]{2,1,0:T(8,128)(2,1)S(1)}, bf16[2,64,1024]{2,1,0:T(8,128)(2,1)S(1)}, u32[]{:S(2)}, u32[]{:S(2)}) collective-permute-start(bf16[2,64,1024]{2,1,0:T(8,128)(2,1)S(1)} %pad_maximum_fusion.quad_ref), channel_id=1, source_target_pairs={{0,1},{1,0},{2,3},{3,2},{4,5},{5,4},{6,7},{7,6},{8,9},{9,8},{10,11... | collective-permute-start | bytes 786440 | tf_op jit(solution)/shard_map/ppermute | solution.py:264
  20.4 12.8 %collective-permute-start.6 = (bf16[64,1024]{1,0:T(8,128)(2,1)S(1)}, bf16[64,1024]{1,0:T(8,128)(2,1)S(1)}, u32[]{:S(2)}, u32[]{:S(2)}) collective-permute-start(bf16[64,1024]{1,0:T(8,128)(2,1)S(1)} %get-tuple-element.6.pair_ref), channel_id=1, source_target_pairs={{3,8},{7,12},{8,3},{12,7},{19,24},{23,28},{24,19},{28,23}} | collective-permute-start | bytes 393224 | tf_op jit(solution)/shard_map/ppermute | solution.py:261
  21.1 12.2 %collective-permute-start.5 = (bf16[2,64,1024]{2,1,0:T(8,128)(2,1)S(1)}, bf16[2,64,1024]{2,1,0:T(8,128)(2,1)S(1)}, u32[]{:S(2)}, u32[]{:S(2)}) collective-permute-start(bf16[2,64,1024]{2,1,0:T(8,128)(2,1)S(1)} %collective-permute-done.3.before_ref), channel_id=1, source_target_pairs={{0,1},{1,0},{2,3},{3,2},{4,5},{5,4},{6,7},{7,6},{8,9},{9,8},{10,11... | collective-permute-start | bytes 786440 | tf_op jit(solution)/shard_map/ppermute | solution.py:266
  22.9 10.4 %collective-permute-start.4 = (bf16[2,64,1024]{2,1,0:T(8,128)(2,1)S(1)}, bf16[2,64,1024]{2,1,0:T(8,128)(2,1)S(1)}, u32[]{:S(2)}, u32[]{:S(2)}) collective-permute-start(bf16[2,64,1024]{2,1,0:T(8,128)(2,1)S(1)} %collective-permute-done.2.after_ref), channel_id=1, source_target_pairs={{0,1},{1,0},{2,3},{3,2},{4,5},{5,4},{6,7},{7,6},{8,9},{9,8},{10,11... | collective-permute-start | bytes 786440 | tf_op jit(solution)/shard_map/ppermute | solution.py:265
  27.9 0.9 %copy-start = (f32[2,65,256]{2,1,0:T(8,128)S(1)}, f32[2,65,256]{2,1,0:T(8,128)}, u32[]{:S(2)}) copy-start(f32[2,65,256]{2,1,0:T(8,128)} %constant.14.clone.lag_ref) | copy-start | bytes 399364

commit v3 on v2

v3 whole, which is shorter than its diff:
```python
import functools
import math

import jax
import jax.numpy as jnp
import numpy as np
from jax import lax
from jax.experimental import pallas as pl
from jax.experimental.pallas import tpu as pltpu
from jax.sharding import PartitionSpec as P

BAND = 256
BAND_LO = 16
LAG = 32
LAGS = 2 * LAG + 1
REACH = 5
QUAD = 4
SPECTRUM_VMEM = 55040 * 2**10
KERNEL_VMEM = 24 * 2**20

water_level = 0.5
epsilon = 1e-06


def split_table(samples, step):
    bins = np.arange(BAND) + BAND_LO
    angle = (np.arange(step)[:, None] * bins[None, :] % samples) * (2.0 * math.pi / samples)
    table = np.concatenate([np.cos(angle), -np.sin(angle)], axis=1).astype(np.float32)
    high = table.astype(jnp.bfloat16)
    low = (table - high.astype(np.float32)).astype(jnp.bfloat16)
    return np.stack([high, low])


def spectrum_kernel(step, traces_hbm, table_hbm, white_ref, traces, table, sems):
    channels = white_ref.shape[0]
    stretches = traces.shape[0] // channels
    group = 4
    table_copy = pltpu.make_async_copy(table_hbm, table, sems.at[stretches])
    table_copy.start()
    copies = [
        pltpu.make_async_copy(
            traces_hbm.at[:, pl.ds(n * step, step)], traces.at[pl.ds(n * channels, channels)], sems.at[n]
        )
        for n in range(stretches)
    ]
    for copy in copies:
        copy.start()
    number = lax.broadcasted_iota(jnp.int32, (stretches, BAND), 0)
    bins = lax.broadcasted_iota(jnp.int32, (stretches, BAND), 1) + BAND_LO
    turn = lax.rem(number * bins, stretches).astype(jnp.float32) * (2.0 * math.pi / stretches)
    turn_cos, turn_sin = jnp.cos(turn), jnp.sin(turn)
    table_copy.wait()
    real = imag = None
    for start in range(0, stretches, group):
        for copy in copies[start : start + group]:
            copy.wait()
        part = traces[start * channels : (start + group) * channels]
        y = jnp.dot(part, table[0], preferred_element_type=jnp.float32)
        y = y + jnp.dot(part, table[1], preferred_element_type=jnp.float32)
        for n in range(group):
            y_real = y[n * channels : (n + 1) * channels, :BAND]
            y_imag = y[n * channels : (n + 1) * channels, BAND:]
            if start + n == 0:
                real, imag = y_real, y_imag
                continue
            cosine, sine = turn_cos[start + n : start + n + 1], turn_sin[start + n : start + n + 1]
            real = real + (y_real * cosine + y_imag * sine)
            imag = imag + (y_imag * cosine - y_real * sine)
    power = real * real + imag * imag
    level = jnp.mean(power, axis=1, keepdims=True)
    denom = jnp.sqrt(power + water_level * level + epsilon)
    white_ref[:, :BAND] = (real / denom).astype(jnp.bfloat16)
    white_ref[:, BAND:] = (imag / denom).astype(jnp.bfloat16)


def spectra(traces):
    channels, samples = traces.shape
    step = 256
    table = split_table(samples, step)
    hbm = pl.BlockSpec(memory_space=pltpu.HBM)
    return pl.pallas_call(
        functools.partial(spectrum_kernel, step),
        out_shape=jax.ShapeDtypeStruct((channels, 2 * BAND), jnp.bfloat16),
        in_specs=[hbm] * 2,
        out_specs=pl.BlockSpec(memory_space=pltpu.VMEM),
        scratch_shapes=[
            pltpu.VMEM((samples // step * channels, step), traces.dtype),
            pltpu.VMEM(table.shape, jnp.bfloat16),
            pltpu.SemaphoreType.DMA((samples // step + 1,)),
        ],
        compiler_params=pltpu.CompilerParams(vmem_limit_bytes=SPECTRUM_VMEM),
    )(traces, jnp.asarray(table))


def turn_rows(samples, pair_ref, rows_ref, stage, own, lag_cos, lag_sin):
    lag = lax.broadcasted_iota(jnp.int32, lag_cos.shape, 0)
    bins = lax.broadcasted_iota(jnp.int32, lag_cos.shape, 1) + BAND_LO
    angle = lax.rem((lag + (samples - LAG)) * bins, samples).astype(jnp.float32) * (2.0 * math.pi / samples)
    lag_cos[...] = jnp.cos(angle)
    lag_sin[...] = jnp.sin(angle)
    pairs = own.shape[1]
    first = pl.multiple_of(lax.axis_index("seg") * 2 * pairs, 2 * pairs)
    mine = pair_ref[0, pl.ds(first, 2 * pairs), :].astype(jnp.float32)
    for left in range(0, mine.shape[1], 128):
        stage[...] = mine[:, left : left + 128]
        for member in range(2):
            own[member, :, left : left + 128] = stage[pl.ds(member, pairs, stride=2), :]

    def turn(lag, carry):
        cosine, sine = lag_cos[pl.ds(lag, 1), :], lag_sin[pl.ds(lag, 1), :]
        at = pl.ds(pl.multiple_of(lag * pairs, pairs), pairs)
        for member in range(2):
            for left in range(0, own.shape[2], 2 * BAND):
                middle, right = left + BAND, left + 2 * BAND
                real, imag = own[member, :, left:middle], own[member, :, middle:right]
                rows_ref[member, at, left:middle] = (real * cosine - imag * sine).astype(jnp.bfloat16)
                rows_ref[member, at, middle:right] = (real * sine + imag * cosine).astype(jnp.bfloat16)
        return carry

    lax.fori_loop(0, LAGS, turn, 0, unroll=5)


def multiply(rows_ref, window, scale, tiles, done):
    members = len(scale)
    width = window.shape[0] // members
    lines = rows_ref.shape[1]
    bounds = [lines * cut // 13 // 16 * 16 for cut in (0, 6, 10)] + [lines]
    for number, (low, high) in enumerate(zip(bounds[:-1], bounds[1:])):
        even, odd = [
            lax.dot_general(
                rows_ref[m, low:high], window[...], (((1,), (1,)), ((), ())), preferred_element_type=jnp.float32
            )
            for m in range(2)
        ]
        lane = lax.broadcasted_iota(jnp.int32, (high - low, 2 * width), 1)
        for n in range(0, members, 2):
            a, b = even[:, n * width : (n + 2) * width], odd[:, n * width : (n + 2) * width]
            tiles[n, low:high] = jnp.where(lane < width, a, pltpu.roll(b, width, 1)) * scale[n]
            tiles[n + 1, low:high] = jnp.where(lane < width, pltpu.roll(a, width, 1), b) * scale[n + 1]
        done(number, low, high)


class Sender:
    def __init__(self, tiles, slots, out_ref, sems, checked):
        self.tiles, self.slots, self.out_ref, self.sems, self.checked = tiles, slots, out_ref, sems, checked
        self.sent = []

    def act(self, slot, action):
        if self.checked:
            pl.when((slot >= 0) & (slot <= 2 * REACH))(action)
        else:
            action()

    def send(self, number, low, high):
        for n, slot in enumerate(self.slots):
            copy = pltpu.make_async_copy(
                self.tiles.at[n, low:high],
                self.out_ref.at[slot, low:high],
                self.sems.at[number * len(self.slots) + n],
            )
            self.sent.append((slot, copy))
            self.act(slot, copy.start)

    def wait(self):
        for slot, copy in self.sent:
            self.act(slot, copy.wait)


def slot_of(plane, swap_x, swap_core):
    place = lax.rem(lax.axis_index("chan"), QUAD)
    step_x = 2 - 4 * lax.div(place, 2)
    step_core = 1 - 2 * lax.rem(place, 2)
    return REACH + QUAD * plane + swap_x * step_x + swap_core * step_core


def near_kernel(rows_ref, scale_ref, own_ref, sibling_ref, out_ref, window, tiles, sems):
    width = own_ref.shape[1]
    slots = []
    for core, ref in enumerate((own_ref, sibling_ref)):
        for x in range(2):
            n = len(slots)
            window[n * width : (n + 1) * width] = ref[x]
            slots.append(slot_of(0, x, core))
    scale = [scale_ref[pl.ds(slot, 1), :] for slot in slots]
    sender = Sender(tiles, slots, out_ref, sems, False)
    multiply(rows_ref, window, scale, tiles, sender.send)
    sender.wait()


def far_slots(core):
    chan = lax.axis_index("chan")
    place = lax.rem(chan, QUAD)
    ahead = 1 - 2 * lax.rem(lax.div(chan, QUAD), 2)
    slots, stands = [], []
    for plane in (ahead, -ahead):
        for x in range(2):
            slot = slot_of(plane, x, core)
            low = (place == 0) & (plane == 1)
            high = (place == QUAD - 1) & (plane == -1)
            if core == 0 and x == 1:
                stands.append((len(slots), low | high))
                slot = jnp.where(low, 0, jnp.where(high, 2 * REACH, slot))
            slots.append(slot)
    return slots, stands


def own_kernel(rows_ref, scale_ref, first_ref, second_ref, corner_ref, tiles_ref, window):
    width = first_ref.shape[1]
    slots, stands = far_slots(0)
    for n in range(QUAD):
        window[n * width : (n + 1) * width] = (first_ref, second_ref)[n // 2][n % 2]
    for n, stand in stands:

        @pl.when(stand)
        def _():
            window[n * width : (n + 1) * width] = corner_ref[...]

    scale = [scale_ref[pl.ds(jnp.clip(slot, 0, 2 * REACH), 1), :] for slot in slots]
    multiply(rows_ref, window, scale, tiles_ref, lambda *stretch: None)


def sibling_kernel(rows_ref, scale_ref, first_ref, second_ref, own_tiles_ref, near_ref, out_ref, window, tiles, sems,
                   own_sems):
    del near_ref
    width = first_ref.shape[1]
    own_sender = Sender(own_tiles_ref, far_slots(0)[0], out_ref, own_sems, True)
    own_sender.send(0, 0, own_tiles_ref.shape[1])
    slots, _ = far_slots(1)
    for n in range(QUAD):
        window[n * width : (n + 1) * width] = (first_ref, second_ref)[n // 2][n % 2]
    scale = [scale_ref[pl.ds(jnp.clip(slot, 0, 2 * REACH), 1), :] for slot in slots]
    sender = Sender(tiles, slots, out_ref, sems, True)
    multiply(rows_ref, window, scale, tiles, sender.send)
    own_sender.wait()
    sender.wait()


def lag_rows(quad, samples, half):
    depth = quad.shape[2]
    vmem = pl.BlockSpec(memory_space=pltpu.VMEM)
    return pl.pallas_call(
        functools.partial(turn_rows, samples),
        out_shape=jax.ShapeDtypeStruct((2, LAGS * half // 2, depth), jnp.bfloat16),
        in_specs=[vmem],
        out_specs=vmem,
        scratch_shapes=[
            pltpu.VMEM((half, 128), jnp.float32),
            pltpu.VMEM((2, half // 2, depth), jnp.float32),
            pltpu.VMEM((LAGS, BAND), jnp.float32),
            pltpu.VMEM((LAGS, BAND), jnp.float32),
        ],
        compiler_params=pltpu.CompilerParams(vmem_limit_bytes=KERNEL_VMEM),
        cost_estimate=pl.CostEstimate(flops=5*10**9, bytes_accessed=2**20, transcendentals=0),
    )(quad)


def correlate(kernel, operands, out=None, tiles_only=False):
    rows, scale, blobs = operands[:3]
    width, depth = blobs.shape[-2:]
    lines = rows.shape[1]
    vmem = pl.BlockSpec(memory_space=pltpu.VMEM)
    anywhere = pl.BlockSpec(memory_space=pl.ANY)
    extra = [] if out is None else [out]
    scratch = [pltpu.VMEM((QUAD * width, depth), jnp.bfloat16)]
    if not tiles_only:
        scratch += [pltpu.VMEM((QUAD, lines, 2 * width), jnp.float32), pltpu.SemaphoreType.DMA((3 * QUAD,))]
    if extra:
        scratch += [pltpu.SemaphoreType.DMA((QUAD,))]
    return pl.pallas_call(
        kernel,
        out_shape=jax.ShapeDtypeStruct((QUAD if tiles_only else scale.shape[0], lines, 2 * width), jnp.float32),
        in_specs=[vmem] * len(operands) + [anywhere] * len(extra),
        out_specs=vmem if tiles_only else anywhere,
        scratch_shapes=scratch,
        input_output_aliases={len(operands): 0} if extra else {},
        compiler_params=pltpu.CompilerParams(vmem_limit_bytes=KERNEL_VMEM),
        cost_estimate=pl.CostEstimate(
            flops=4 * lines * depth * QUAD * width, bytes_accessed=8 * QUAD * lines * width, transcendentals=0
        ),
    )(*operands, *extra)


def local(traces, partners):
    slots = partners.shape[1]
    segments = lax.axis_size("seg")
    blocks = lax.axis_size("chan")
    channels = traces.shape[1]
    half = channels // segments
    assert segments == 2 and blocks % QUAD == 0 and slots == 2 * REACH + 1
    plane_one = [(c, c ^ QUAD) for c in range(blocks)]
    plane_two = [(c, ((c + QUAD) ^ QUAD) - QUAD) for c in range(QUAD, blocks - QUAD)]
    sibling = [(c, c ^ 1) for c in range(blocks)]
    corners = [(c, c + REACH) for c in range(QUAD - 1, blocks - REACH, QUAD)]
    corners += [(c, c - REACH) for c in range(2 * QUAD, blocks, QUAD)]
    norm_scale = (segments * BAND) ** (-0.5)
    scale = jnp.where(partners[0] >= 0, norm_scale, 0.0).astype(jnp.float32)
    scale = jnp.broadcast_to(scale[:, None], (slots, 2 * channels))
    white = spectra(traces[0])
    corner = lax.ppermute(white, "chan", corners)
    other = lax.ppermute(white, "seg", [(0, 1), (1, 0)])
    across = lax.ppermute(white, "chan", [(c, c ^ 2) for c in range(blocks)])
    diagonal = [(s * blocks + c, (1 - s) * blocks + (c ^ 2)) for s in range(segments) for c in range(blocks)]
    diagonal = lax.ppermute(white, ("seg", "chan"), diagonal)
    pair = jnp.concatenate([white, other], axis=1)
    quad = jnp.stack([pair, jnp.concatenate([across, diagonal], axis=1)])
    quad, scale = lax.optimization_barrier((quad, scale))
    first = lax.ppermute(quad, "chan", plane_one)
    second = lax.ppermute(quad, "chan", plane_two)
    corner_other = lax.ppermute(corner, "seg", [(0, 1), (1, 0)])
    scale, corner, corner_other = lax.optimization_barrier((scale, corner, corner_other))
    near = quad
    corner = jnp.concatenate([corner, corner_other], axis=1)
    beside = lax.ppermute(near, "chan", sibling)
    rows = lag_rows(near, traces.shape[2], half)
    out = correlate(near_kernel, [rows, scale, near, beside])
    first, second, out = lax.optimization_barrier((first, second, out))
    sib_first = lax.ppermute(first, "chan", sibling)
    sib_second = lax.ppermute(second, "chan", sibling)
    tiles = correlate(own_kernel, [rows, scale, first, second, corner], tiles_only=True)
    out = correlate(sibling_kernel, [rows, scale, sib_first, sib_second, tiles], out)
    return out.reshape(1, slots, LAGS, half * channels)


def solution(mesh):
    placed = (P("seg", "chan", None), P("chan", None))
    return jax.shard_map(
        local, mesh=mesh, in_specs=placed, out_specs=P("chan", None, None, "seg"), check_vma=False
    )
```

time: 37.4 us -> 31.1 us (0.83)
  the two profiles are of different devices: /device:TPU:1 before, /device:TPU:0 now
where the time goes in v3:
time: 31.1 us; the launch traced here: 31 us
  starting transfers between devices  13.4 us (43%)
  Pallas kernels  10.9 us (35%)
  waiting for transfers between devices  5.77 us (19%)
  other arithmetic  0.71 us (2%)
    pallas_call x3, Pallas kernels, correlate(): pl.pallas_call(kernel, out_shape=jax.ShapeDtypeStruct((QUAD if tiles_only...  6.78 us
    ppermute x1, starting transfers between devices, local(): first = lax.ppermute(quad, 'chan', plane_one)  4.46 us
    ppermute x1, starting transfers between devices, local(): diagonal = lax.ppermute(white, ('seg', 'chan'), diagonal)  3.96 us
    ppermute x1, waiting for transfers between devices, local(): other = lax.ppermute(white, 'seg', [(0, 1), (1, 0)])  3.51 us
    pallas_call x1, Pallas kernels, spectra(): pl.pallas_call(functools.partial(spectrum_kernel, step), out_shape=jax.Sh...  2.55 us
    ppermute x1, waiting for transfers between devices, local(): corner_other = lax.ppermute(corner, 'seg', [(0, 1), (1, 0)])  2.22 us
    ppermute x1, starting transfers between devices, local(): beside = lax.ppermute(near, 'chan', sibling)  1.95 us
    pallas_call x1, Pallas kernels, lag_rows(): pl.pallas_call(functools.partial(turn_rows, samples), out_shape=jax.Shape...  1.53 us
  transfers between devices with their start and end apart: 10, of which 2 were waited for; matrix products, arithmetic and copies ran while one was open for 3% of the time, Pallas kernels for 18%

profile of v3, /device:TPU:0, one launch (start us, length us, event | category | flops | bytes accessed | tf_op | source)
XLA Modules:
  0.0 31.0 jit_solution(2697590278886761728)
XLA Ops:
  0.0 2.6 %shard_map.37 = bf16[64,512]{1,0:T(8,128)(2,1)S(1)} custom-call(bf16[64,4096]{1,0:T(8,128)(2,1)} %bitcast.8, bf16[2,256,512]{2,1,0:T(8,128)(2,1)} %constant.8.clone.table_hbm), custom_call_target="tpu_custom_call" | custom-call | tf_op jit(solution)/shard_map/pallas_call | solution.py:81
  2.6 0.7 %collective-permute-start.3 = (bf16[64,512]{1,0:T(8,128)(2,1)S(1)}, bf16[64,512]{1,0:T(8,128)(2,1)S(1)}, u32[]{:S(2)}, u32[]{:S(2)}) collective-permute-start(bf16[64,512]{1,0:T(8,128)(2,1)S(1)} %shard_map.37), channel_id=1, source_target_pairs={{3,8},{7,12},{8,3},{12,7},{19,24},{23,28},{24,19},{28,23}} | collective-permute-start | bytes 196616 | tf_op jit(solution)/shard_map/ppermute | solution.py:299
  3.2 4.0 %collective-permute-start.2 = (bf16[64,512]{1,0:T(8,128)(2,1)S(1)}, bf16[64,512]{1,0:T(8,128)(2,1)S(1)}, u32[]{:S(2)}, u32[]{:S(2)}) collective-permute-start(bf16[64,512]{1,0:T(8,128)(2,1)S(1)} %shard_map.37), channel_id=1, source_target_pairs={{0,18},{1,19},{2,16},{3,17},{4,22},{5,23},{6,20},{7,21},{8,26},{9,... | collective-permute-start | bytes 196616 | tf_op jit(solution)/shard_map/ppermute | solution.py:303
  7.2 0.5 %collective-permute-start.1 = (bf16[64,512]{1,0:T(8,128)(2,1)S(1)}, bf16[64,512]{1,0:T(8,128)(2,1)S(1)}, u32[]{:S(2)}, u32[]{:S(2)}) collective-permute-start(bf16[64,512]{1,0:T(8,128)(2,1)S(1)} %shard_map.37), channel_id=1, source_target_pairs={{0,2},{1,3},{2,0},{3,1},{4,6},{5,7},{6,4},{7,5},{8,10},{9,11},{10,... | collective-permute-start | bytes 196616 | tf_op jit(solution)/shard_map/ppermute | solution.py:301
  7.7 0.1 collective-permute-start
  7.8 0.7 %fusion = f32[11]{0:T(128)S(1)} fusion(s32[1,11]{1,0:T(1,128)} %param.4), kind=kLoop, calls=%fused_computation.5 | loop fusion | flops 22 | bytes 88 | tf_op jit(solution)/shard_map/jit(_where)/select_n | solution.py:296
  8.5 3.5 %collective-permute-done = bf16[64,512]{1,0:T(8,128)(2,1)S(1)} collective-permute-done((bf16[64,512]{1,0:T(8,128)(2,1)S(1)}, bf16[64,512]{1,0:T(8,128)(2,1)S(1)}, u32[]{:S(2)}, u32[]{:S(2)}) %collective-permute-start) | collective-permute-done | bytes 65568 | tf_op jit(solution)/shard_map/ppermute | solution.py:300
  12.0 0.0 collective-permute-done.2
  12.1 0.1 broadcast_in_dim.16.scale_ref
  12.2 2.0 %collective-permute-start.7 = (bf16[2,64,1024]{2,1,0:T(8,128)(2,1)S(1)}, bf16[2,64,1024]{2,1,0:T(8,128)(2,1)S(1)}, u32[]{:S(2)}, u32[]{:S(2)}) collective-permute-start(bf16[2,64,1024]{2,1,0:T(8,128)(2,1)S(1)} %pad_maximum_fusion.pair_ref.own_ref), channel_id=1, source_target_pairs={{0,1},{1,0},{2,3},{3,2},{4,5},{5,4},{6,7},{7,6},{8,9},{9,8},{10,11... | collective-permute-start | bytes 786440 | tf_op jit(solution)/shard_map/ppermute | solution.py:313
  14.1 0.7 %collective-permute-start.6 = (bf16[2,64,1024]{2,1,0:T(8,128)(2,1)S(1)}, bf16[2,64,1024]{2,1,0:T(8,128)(2,1)S(1)}, u32[]{:S(2)}, u32[]{:S(2)}) collective-permute-start(bf16[2,64,1024]{2,1,0:T(8,128)(2,1)S(1)} %pad_maximum_fusion.pair_ref.own_ref), channel_id=1, source_target_pairs={{4,8},{5,9},{6,10},{7,11},{8,4},{9,5},{10,6},{11,7},{20,24},{21,25... | collective-permute-start | bytes 786440 | tf_op jit(solution)/shard_map/ppermute | solution.py:308
  14.8 4.5 %collective-permute-start.5 = (bf16[2,64,1024]{2,1,0:T(8,128)(2,1)S(1)}, bf16[2,64,1024]{2,1,0:T(8,128)(2,1)S(1)}, u32[]{:S(2)}, u32[]{:S(2)}) collective-permute-start(bf16[2,64,1024]{2,1,0:T(8,128)(2,1)S(1)} %pad_maximum_fusion.pair_ref.own_ref), channel_id=1, source_target_pairs={{0,4},{1,5},{2,6},{3,7},{4,0},{5,1},{6,2},{7,3},{8,12},{9,13},{10,... | collective-permute-start | bytes 786440 | tf_op jit(solution)/shard_map/ppermute | solution.py:307
  19.3 0.0 collective-permute-done.3
  19.3 0.5 %collective-permute-start.4 = (bf16[64,512]{1,0:T(8,128)(2,1)S(1)}, bf16[64,512]{1,0:T(8,128)(2,1)S(1)}, u32[]{:S(2)}, u32[]{:S(2)}) collective-permute-start(bf16[64,512]{1,0:T(8,128)(2,1)S(1)} %collective-permute-done.3), channel_id=1, source_target_pairs={{0,16},{16,0},{1,17},{17,1},{2,18},{18,2},{3,19},{19,3},{4,20},{20... | collective-permute-start | bytes 196616 | tf_op jit(solution)/shard_map/ppermute | solution.py:309
  19.8 1.5 %shard_map.38.rows_ref = bf16[2,1040,1024]{2,1,0:T(8,128)(2,1)S(1)} custom-call(bf16[2,64,1024]{2,1,0:T(8,128)(2,1)S(1)} %pad_maximum_fusion.pair_ref.own_ref), custom_call_target="tpu_custom_call" | custom-call | flops 5000000000 | bytes 1048576 | tf_op jit(solution)/shard_map/pallas_call | solution.py:241
  21.3 2.2 %collective-permute-done.4 = bf16[64,512]{1,0:T(8,128)(2,1)S(1)} collective-permute-done((bf16[64,512]{1,0:T(8,128)(2,1)S(1)}, bf16[64,512]{1,0:T(8,128)(2,1)S(1)}, u32[]{:S(2)}, u32[]{:S(2)}) %collective-permute-start.4) | collective-permute-done | bytes 65568 | tf_op jit(solution)/shard_map/ppermute | solution.py:309
  23.5 0.0 collective-permute-done.7.sibling_ref
  23.5 2.4 %shard_map.39.near_ref = f32[11,1040,128]{2,1,0:T(8,128)} custom-call(bf16[2,1040,1024]{2,1,0:T(8,128)(2,1)S(1)} %shard_map.38.rows_ref, f32[11,128]{1,0:T(8,128)S(1)} %broadcast_in_dim.16.scale_ref, bf16[2,64,1024]{2,1,0:T(8,128)(2,1)S(1)} %pad_maximum_fusion.pair_ref.own_ref, bf16[2,64,1024]{2,1,0:T(8,128)(2,1)S(1)} %collective-permute-done.7.sibling_ref), custom_call_target="tpu_custom_call" | custom-call | flops 1090519040 | bytes 2129920 | tf_op jit(solution)/shard_map/pallas_call | solution.py:269
  25.9 0.0 collective-permute-done.5.first_ref
  25.9 0.1 collective-permute-start.8
  26.0 0.5 %collective-permute-start.9 = (bf16[2,64,1024]{2,1,0:T(8,128)(2,1)S(1)}, bf16[2,64,1024]{2,1,0:T(8,128)(2,1)S(1)}, u32[]{:S(2)}, u32[]{:S(2)}) collective-permute-start(bf16[2,64,1024]{2,1,0:T(8,128)(2,1)S(1)} %collective-permute-done.6.second_ref), channel_id=1, source_target_pairs={{0,1},{1,0},{2,3},{3,2},{4,5},{5,4},{6,7},{7,6},{8,9},{9,8},{10,11... | collective-permute-start | bytes 786440 | tf_op jit(solution)/shard_map/ppermute | solution.py:318
  26.5 1.5 %shard_map.40.own_tiles_ref = f32[4,1040,128]{2,1,0:T(8,128)S(1)} custom-call(bf16[2,1040,1024]{2,1,0:T(8,128)(2,1)S(1)} %shard_map.38.rows_ref, f32[11,128]{1,0:T(8,128)S(1)} %broadcast_in_dim.16.scale_ref, bf16[2,64,1024]{2,1,0:T(8,128)(2,1)S(1)} %collective-permute-done.5.first_ref, bf16[2,64,1024]{2,1,0:T(8,128)(2,1)S(1)} %collective-permute-done.6.second_ref, ...), custom_call_target="tpu_custom_call" | custom-call | flops 1090519040 | bytes 2129920 | tf_op jit(solution)/shard_map/pallas_call | solution.py:269
  28.1 0.0 collective-permute-done.9.second_ref
  28.1 2.9 %shard_map.41 = f32[11,1040,128]{2,1,0:T(8,128)} custom-call(bf16[2,1040,1024]{2,1,0:T(8,128)(2,1)S(1)} %shard_map.38.rows_ref, f32[11,128]{1,0:T(8,128)S(1)} %broadcast_in_dim.16.scale_ref, bf16[2,64,1024]{2,1,0:T(8,128)(2,1)S(1)} %collective-permute-done.8.first_ref, ...), custom_call_target="tpu_custom_call", output_to_operand_aliasing={{}: (5, {})} | custom-call | flops 1090519040 | bytes 2129920 | tf_op jit(solution)/shard_map/pallas_call | solution.py:269
  (7 shorter events, 0.1 us)
Async XLA Ops:
  2.6 16.7 %collective-permute-start.3 = (bf16[64,512]{1,0:T(8,128)(2,1)S(1)}, bf16[64,512]{1,0:T(8,128)(2,1)S(1)}, u32[]{:S(2)}, u32[]{:S(2)}) collective-permute-start(bf16[64,512]{1,0:T(8,128)(2,1)S(1)} %shard_map.37), channel_id=1, source_target_pairs={{3,8},{7,12},{8,3},{12,7},{19,24},{23,28},{24,19},{28,23}} | collective-permute-start | bytes 196616 | tf_op jit(solution)/shard_map/ppermute | solution.py:299
  3.2 8.8 %collective-permute-start.2 = (bf16[64,512]{1,0:T(8,128)(2,1)S(1)}, bf16[64,512]{1,0:T(8,128)(2,1)S(1)}, u32[]{:S(2)}, u32[]{:S(2)}) collective-permute-start(bf16[64,512]{1,0:T(8,128)(2,1)S(1)} %shard_map.37), channel_id=1, source_target_pairs={{0,18},{1,19},{2,16},{3,17},{4,22},{5,23},{6,20},{7,21},{8,26},{9,... | collective-permute-start | bytes 196616 | tf_op jit(solution)/shard_map/ppermute | solution.py:303
  7.2 4.8 %collective-permute-start.1 = (bf16[64,512]{1,0:T(8,128)(2,1)S(1)}, bf16[64,512]{1,0:T(8,128)(2,1)S(1)}, u32[]{:S(2)}, u32[]{:S(2)}) collective-permute-start(bf16[64,512]{1,0:T(8,128)(2,1)S(1)} %shard_map.37), channel_id=1, source_target_pairs={{0,2},{1,3},{2,0},{3,1},{4,6},{5,7},{6,4},{7,5},{8,10},{9,11},{10,... | collective-permute-start | bytes 196616 | tf_op jit(solution)/shard_map/ppermute | solution.py:301
  7.7 4.3 %collective-permute-start = (bf16[64,512]{1,0:T(8,128)(2,1)S(1)}, bf16[64,512]{1,0:T(8,128)(2,1)S(1)}, u32[]{:S(2)}, u32[]{:S(2)}) collective-permute-start(bf16[64,512]{1,0:T(8,128)(2,1)S(1)} %shard_map.37), channel_id=1, source_target_pairs={{0,16},{16,0},{1,17},{17,1},{2,18},{18,2},{3,19},{19,3},{4,20},{20... | collective-permute-start | bytes 196616 | tf_op jit(solution)/shard_map/ppermute | solution.py:300
  12.2 11.4 %collective-permute-start.7 = (bf16[2,64,1024]{2,1,0:T(8,128)(2,1)S(1)}, bf16[2,64,1024]{2,1,0:T(8,128)(2,1)S(1)}, u32[]{:S(2)}, u32[]{:S(2)}) collective-permute-start(bf16[2,64,1024]{2,1,0:T(8,128)(2,1)S(1)} %pad_maximum_fusion.pair_ref.own_ref), channel_id=1, source_target_pairs={{0,1},{1,0},{2,3},{3,2},{4,5},{5,4},{6,7},{7,6},{8,9},{9,8},{10,11... | collective-permute-start | bytes 786440 | tf_op jit(solution)/shard_map/ppermute | solution.py:313
  14.1 11.8 %collective-permute-start.6 = (bf16[2,64,1024]{2,1,0:T(8,128)(2,1)S(1)}, bf16[2,64,1024]{2,1,0:T(8,128)(2,1)S(1)}, u32[]{:S(2)}, u32[]{:S(2)}) collective-permute-start(bf16[2,64,1024]{2,1,0:T(8,128)(2,1)S(1)} %pad_maximum_fusion.pair_ref.own_ref), channel_id=1, source_target_pairs={{4,8},{5,9},{6,10},{7,11},{8,4},{9,5},{10,6},{11,7},{20,24},{21,25... | collective-permute-start | bytes 786440 | tf_op jit(solution)/shard_map/ppermute | solution.py:308
  14.8 11.1 %collective-permute-start.5 = (bf16[2,64,1024]{2,1,0:T(8,128)(2,1)S(1)}, bf16[2,64,1024]{2,1,0:T(8,128)(2,1)S(1)}, u32[]{:S(2)}, u32[]{:S(2)}) collective-permute-start(bf16[2,64,1024]{2,1,0:T(8,128)(2,1)S(1)} %pad_maximum_fusion.pair_ref.own_ref), channel_id=1, source_target_pairs={{0,4},{1,5},{2,6},{3,7},{4,0},{5,1},{6,2},{7,3},{8,12},{9,13},{10,... | collective-permute-start | bytes 786440 | tf_op jit(solution)/shard_map/ppermute | solution.py:307
  19.3 4.3 %collective-permute-start.4 = (bf16[64,512]{1,0:T(8,128)(2,1)S(1)}, bf16[64,512]{1,0:T(8,128)(2,1)S(1)}, u32[]{:S(2)}, u32[]{:S(2)}) collective-permute-start(bf16[64,512]{1,0:T(8,128)(2,1)S(1)} %collective-permute-done.3), channel_id=1, source_target_pairs={{0,16},{16,0},{1,17},{17,1},{2,18},{18,2},{3,19},{19,3},{4,20},{20... | collective-permute-start | bytes 196616 | tf_op jit(solution)/shard_map/ppermute | solution.py:309
  25.9 2.1 %collective-permute-start.8 = (bf16[2,64,1024]{2,1,0:T(8,128)(2,1)S(1)}, bf16[2,64,1024]{2,1,0:T(8,128)(2,1)S(1)}, u32[]{:S(2)}, u32[]{:S(2)}) collective-permute-start(bf16[2,64,1024]{2,1,0:T(8,128)(2,1)S(1)} %collective-permute-done.5.first_ref), channel_id=1, source_target_pairs={{0,1},{1,0},{2,3},{3,2},{4,5},{5,4},{6,7},{7,6},{8,9},{9,8},{10,11... | collective-permute-start | bytes 786440 | tf_op jit(solution)/shard_map/ppermute | solution.py:317
  26.0 2.1 %collective-permute-start.9 = (bf16[2,64,1024]{2,1,0:T(8,128)(2,1)S(1)}, bf16[2,64,1024]{2,1,0:T(8,128)(2,1)S(1)}, u32[]{:S(2)}, u32[]{:S(2)}) collective-permute-start(bf16[2,64,1024]{2,1,0:T(8,128)(2,1)S(1)} %collective-permute-done.6.second_ref), channel_id=1, source_target_pairs={{0,1},{1,0},{2,3},{3,2},{4,5},{5,4},{6,7},{7,6},{8,9},{9,8},{10,11... | collective-permute-start | bytes 786440 | tf_op jit(solution)/shard_map/ppermute | solution.py:318

commit v4 on v3

--- a/solution.py
+++ b/solution.py
@@ -92,7 +92,32 @@
     )(traces, jnp.asarray(table))
 
 
-def turn_rows(samples, pair_ref, rows_ref, stage, own, lag_cos, lag_sin):
+def quad_kernel(white_ref, other_ref, across_ref, diagonal_ref, quad_ref):
+    half = white_ref.shape[1]
+    quad_ref[0, :, :half] = white_ref[...]
+    quad_ref[0, :, half:] = other_ref[...]
+    quad_ref[1, :, :half] = across_ref[...]
+    quad_ref[1, :, half:] = diagonal_ref[...]
+
+
+def assemble(*quarters):
+    channels, depth = quarters[0].shape
+    vmem = pl.BlockSpec(memory_space=pltpu.VMEM)
+    return pl.pallas_call(
+        quad_kernel,
+        out_shape=jax.ShapeDtypeStruct((2, channels, 2 * depth), quarters[0].dtype),
+        in_specs=[vmem] * 4,
+        out_specs=vmem,
+        compiler_params=pltpu.CompilerParams(vmem_limit_bytes=2 * 2**20),
+        cost_estimate=pl.CostEstimate(flops=10**9, bytes_accessed=2**19, transcendentals=0),
+    )(*quarters)
+
+
+def rows_kernel(samples, norm_scale, pair_ref, partners_ref, rows_ref, scale_ref, stage, own, lag_cos, lag_sin):
+    slots = scale_ref.shape[0]
+    slot = lax.broadcasted_iota(jnp.int32, (slots, slots), 0) == lax.broadcasted_iota(jnp.int32, (slots, slots), 1)
+    factor = jnp.where(slot & (jnp.broadcast_to(partners_ref[...], (slots, slots)) >= 0), norm_scale, 0.0)
+    scale_ref[...] = jnp.broadcast_to(jnp.sum(factor, axis=1, keepdims=True), scale_ref.shape)
     lag = lax.broadcasted_iota(jnp.int32, lag_cos.shape, 0)
     bins = lax.broadcasted_iota(jnp.int32, lag_cos.shape, 1) + BAND_LO
     angle = lax.rem((lag + (samples - LAG)) * bins, samples).astype(jnp.float32) * (2.0 * math.pi / samples)
@@ -235,14 +260,17 @@
     sender.wait()
 
 
-def lag_rows(quad, samples, half):
-    depth = quad.shape[2]
+def lag_rows(quad, partners, samples, half, norm_scale):
+    width, depth = quad.shape[1:]
     vmem = pl.BlockSpec(memory_space=pltpu.VMEM)
     return pl.pallas_call(
-        functools.partial(turn_rows, samples),
-        out_shape=jax.ShapeDtypeStruct((2, LAGS * half // 2, depth), jnp.bfloat16),
-        in_specs=[vmem],
-        out_specs=vmem,
+        functools.partial(rows_kernel, samples, norm_scale),
+        out_shape=[
+            jax.ShapeDtypeStruct((2, LAGS * half // 2, depth), jnp.bfloat16),
+            jax.ShapeDtypeStruct((partners.shape[1], 2 * width), jnp.float32),
+        ],
+        in_specs=[vmem, vmem],
+        out_specs=[vmem, vmem],
         scratch_shapes=[
             pltpu.VMEM((half, 128), jnp.float32),
             pltpu.VMEM((2, half // 2, depth), jnp.float32),
@@ -250,8 +278,8 @@
             pltpu.VMEM((LAGS, BAND), jnp.float32),
         ],
         compiler_params=pltpu.CompilerParams(vmem_limit_bytes=KERNEL_VMEM),
-        cost_estimate=pl.CostEstimate(flops=5*10**9, bytes_accessed=2**20, transcendentals=0),
-    )(quad)
+        cost_estimate=pl.CostEstimate(flops=5 * 10**9, bytes_accessed=2**20, transcendentals=0),
+    )(quad, partners)
 
 
 def correlate(kernel, operands, out=None, tiles_only=False):
@@ -293,26 +321,21 @@
     corners = [(c, c + REACH) for c in range(QUAD - 1, blocks - REACH, QUAD)]
     corners += [(c, c - REACH) for c in range(2 * QUAD, blocks, QUAD)]
     norm_scale = (segments * BAND) ** (-0.5)
-    scale = jnp.where(partners[0] >= 0, norm_scale, 0.0).astype(jnp.float32)
-    scale = jnp.broadcast_to(scale[:, None], (slots, 2 * channels))
     white = spectra(traces[0])
     corner = lax.ppermute(white, "chan", corners)
     other = lax.ppermute(white, "seg", [(0, 1), (1, 0)])
     across = lax.ppermute(white, "chan", [(c, c ^ 2) for c in range(blocks)])
     diagonal = [(s * blocks + c, (1 - s) * blocks + (c ^ 2)) for s in range(segments) for c in range(blocks)]
     diagonal = lax.ppermute(white, ("seg", "chan"), diagonal)
-    pair = jnp.concatenate([white, other], axis=1)
-    quad = jnp.stack([pair, jnp.concatenate([across, diagonal], axis=1)])
-    quad, scale = lax.optimization_barrier((quad, scale))
+    quad = assemble(white, other, across, diagonal)
     first = lax.ppermute(quad, "chan", plane_one)
     second = lax.ppermute(quad, "chan", plane_two)
+    near, corner = lax.optimization_barrier((quad, corner))
     corner_other = lax.ppermute(corner, "seg", [(0, 1), (1, 0)])
-    scale, corner, corner_other = lax.optimization_barrier((scale, corner, corner_other))
-    near = quad
+    beside = lax.ppermute(quad, "chan", sibling)
+    rows, scale = lag_rows(near, partners, traces.shape[2], half, norm_scale)
+    out = correlate(near_kernel, [rows, scale, quad, beside])
     corner = jnp.concatenate([corner, corner_other], axis=1)
-    beside = lax.ppermute(near, "chan", sibling)
-    rows = lag_rows(near, traces.shape[2], half)
-    out = correlate(near_kernel, [rows, scale, near, beside])
     first, second, out = lax.optimization_barrier((first, second, out))
     sib_first = lax.ppermute(first, "chan", sibling)
     sib_second = lax.ppermute(second, "chan", sibling)

time: 31.1 us -> 28.4 us (0.913)
  starting transfers between devices: 13.4 us -> 11.6 us
  waiting for transfers between devices: 5.77 us -> 4.95 us
  other arithmetic: 0.71 us -> 0.01 us
  local copies, waits for them, and re-layouts: 0.07 us -> 0.65 us
    ppermute x1, waiting for transfers between devices: 3.51 us -> 0.54 us  [local(): other = lax.ppermute(white, 'seg', [(0, 1), (1, 0)])]
    ppermute x1, waiting for transfers between devices: 2.22 us -> 0.01 us  [local(): corner_other = lax.ppermute(corner, 'seg', [(0, 1), (1, 0)])]
    ppermute x1, starting transfers between devices: 1.95 us -> 0.07 us  [local(): beside = lax.ppermute(quad, 'chan', sibling)]
    ppermute x1, waiting for transfers between devices: 0.01 us -> 1.8 us  [local(): across = lax.ppermute(white, 'chan', [(c, c ^ 2) for c in range(blocks)])]
    ppermute x1, waiting for transfers between devices: 0.02 us -> 1.44 us  [local(): first = lax.ppermute(quad, 'chan', plane_one)]
    ppermute x1, waiting for transfers between devices: 0.01 us -> 1.16 us  [local(): diagonal = lax.ppermute(white, ('seg', 'chan'), diagonal)]
    select_n x1 -> x0, other arithmetic: 0.66 us -> none  [local(): scale = jnp.where(partners[0] >= 0, norm_scale, 0.0).astype(jnp.float32)]
    unnamed x0 -> x2, local copies, waits for them, and re-layouts: none -> 0.65 us
  transfers between devices with their start and end apart: 10 -> 10, of which waited for: 2 -> 4; matrix products, arithmetic and copies ran while one was open for 3% -> 0% of each run, Pallas kernels for 18% -> 19%
where the time goes in v4:
time: 28.4 us; the launch traced here: 28.2 us
  starting transfers between devices  11.6 us (41%)
  Pallas kernels  10.9 us (38%)
  waiting for transfers between devices  4.95 us (17%)
  local copies, waits for them, and re-layouts  0.65 us (2%)
    pallas_call x3, Pallas kernels, correlate(): pl.pallas_call(kernel, out_shape=jax.ShapeDtypeStruct((QUAD if tiles_only...  6.79 us
    ppermute x1, starting transfers between devices, local(): first = lax.ppermute(quad, 'chan', plane_one)  4.45 us
    ppermute x1, starting transfers between devices, local(): diagonal = lax.ppermute(white, ('seg', 'chan'), diagonal)  3.96 us
    pallas_call x1, Pallas kernels, spectra(): pl.pallas_call(functools.partial(spectrum_kernel, step), out_shape=jax.Sh...  2.55 us
    ppermute x1, waiting for transfers between devices, local(): across = lax.ppermute(white, 'chan', [(c, c ^ 2) for c in range(blocks)])  1.8 us
    pallas_call x1, Pallas kernels, lag_rows(): pl.pallas_call(functools.partial(rows_kernel, samples, norm_scale), out_s...  1.53 us
    ppermute x1, waiting for transfers between devices, local(): first = lax.ppermute(quad, 'chan', plane_one)  1.44 us
    ppermute x1, waiting for transfers between devices, local(): diagonal = lax.ppermute(white, ('seg', 'chan'), diagonal)  1.16 us
  transfers between devices with their start and end apart: 10, of which 4 were waited for; matrix products, arithmetic and copies ran while one was open for 0% of the time, Pallas kernels for 19%

profile of v4, /device:TPU:0, one launch (start us, length us, event | category | flops | bytes accessed | tf_op | source)
XLA Modules:
  0.0 28.2 jit_solution(17985212020064870263)
XLA Ops:
  0.0 2.6 %shard_map.37.white_ref = bf16[64,512]{1,0:T(8,128)(2,1)S(1)} custom-call(bf16[64,4096]{1,0:T(8,128)(2,1)} %bitcast.2, bf16[2,256,512]{2,1,0:T(8,128)(2,1)} %constant.2.clone.table_hbm), custom_call_target="tpu_custom_call" | custom-call | tf_op jit(solution)/shard_map/pallas_call | solution.py:81
  2.6 4.0 %collective-permute-start.2 = (bf16[64,512]{1,0:T(8,128)(2,1)S(1)}, bf16[64,512]{1,0:T(8,128)(2,1)S(1)}, u32[]{:S(2)}, u32[]{:S(2)}) collective-permute-start(bf16[64,512]{1,0:T(8,128)(2,1)S(1)} %shard_map.37.white_ref), channel_id=1, source_target_pairs={{0,18},{1,19},{2,16},{3,17},{4,22},{5,23},{6,20},{7,21},{8,26},{9,... | collective-permute-start | bytes 196616 | tf_op jit(solution)/shard_map/ppermute | solution.py:329
  6.5 0.5 %collective-permute-start.1 = (bf16[64,512]{1,0:T(8,128)(2,1)S(1)}, bf16[64,512]{1,0:T(8,128)(2,1)S(1)}, u32[]{:S(2)}, u32[]{:S(2)}) collective-permute-start(bf16[64,512]{1,0:T(8,128)(2,1)S(1)} %shard_map.37.white_ref), channel_id=1, source_target_pairs={{0,2},{1,3},{2,0},{3,1},{4,6},{5,7},{6,4},{7,5},{8,10},{9,11},{10,... | collective-permute-start | bytes 196616 | tf_op jit(solution)/shard_map/ppermute | solution.py:327
  7.1 0.1 collective-permute-start
  7.2 0.7 %collective-permute-start.3 = (bf16[64,512]{1,0:T(8,128)(2,1)S(1)}, bf16[64,512]{1,0:T(8,128)(2,1)S(1)}, u32[]{:S(2)}, u32[]{:S(2)}) collective-permute-start(bf16[64,512]{1,0:T(8,128)(2,1)S(1)} %shard_map.37.white_ref), channel_id=1, source_target_pairs={{3,8},{7,12},{8,3},{12,7},{19,24},{23,28},{24,19},{28,23}} | collective-permute-start | bytes 196616 | tf_op jit(solution)/shard_map/ppermute | solution.py:325
  7.8 1.2 %collective-permute-done.2.diagonal_ref = bf16[64,512]{1,0:T(8,128)(2,1)S(1)} collective-permute-done((bf16[64,512]{1,0:T(8,128)(2,1)S(1)}, bf16[64,512]{1,0:T(8,128)(2,1)S(1)}, u32[]{:S(2)}, u32[]{:S(2)}) %collective-permute-start.2) | collective-permute-done | bytes 65568 | tf_op jit(solution)/shard_map/ppermute | solution.py:329
  9.0 1.8 %collective-permute-done.1.across_ref = bf16[64,512]{1,0:T(8,128)(2,1)S(1)} collective-permute-done((bf16[64,512]{1,0:T(8,128)(2,1)S(1)}, bf16[64,512]{1,0:T(8,128)(2,1)S(1)}, u32[]{:S(2)}, u32[]{:S(2)}) %collective-permute-start.1) | collective-permute-done | bytes 65568 | tf_op jit(solution)/shard_map/ppermute | solution.py:327
  10.8 0.5 %collective-permute-done.other_ref = bf16[64,512]{1,0:T(8,128)(2,1)S(1)} collective-permute-done((bf16[64,512]{1,0:T(8,128)(2,1)S(1)}, bf16[64,512]{1,0:T(8,128)(2,1)S(1)}, u32[]{:S(2)}, u32[]{:S(2)}) %collective-permute-start) | collective-permute-done | bytes 65568 | tf_op jit(solution)/shard_map/ppermute | solution.py:326
  11.3 0.1 collective-permute-start.6
  11.4 0.7 %collective-permute-start.5 = (bf16[2,64,1024]{2,1,0:T(8,128)(2,1)S(1)}, bf16[2,64,1024]{2,1,0:T(8,128)(2,1)S(1)}, u32[]{:S(2)}, u32[]{:S(2)}) collective-permute-start(bf16[2,64,1024]{2,1,0:T(8,128)(2,1)S(1)} %shard_map.38.pair_ref.own_ref), channel_id=1, source_target_pairs={{4,8},{5,9},{6,10},{7,11},{8,4},{9,5},{10,6},{11,7},{20,24},{21,25... | collective-permute-start | bytes 786440 | tf_op jit(solution)/shard_map/ppermute | solution.py:332
  12.1 4.5 %collective-permute-start.4 = (bf16[2,64,1024]{2,1,0:T(8,128)(2,1)S(1)}, bf16[2,64,1024]{2,1,0:T(8,128)(2,1)S(1)}, u32[]{:S(2)}, u32[]{:S(2)}) collective-permute-start(bf16[2,64,1024]{2,1,0:T(8,128)(2,1)S(1)} %shard_map.38.pair_ref.own_ref), channel_id=1, source_target_pairs={{0,4},{1,5},{2,6},{3,7},{4,0},{5,1},{6,2},{7,3},{8,12},{9,13},{10,... | collective-permute-start | bytes 786440 | tf_op jit(solution)/shard_map/ppermute | solution.py:331
  16.6 0.0 collective-permute-done.3
  16.6 0.6 %collective-permute-start.9 = (bf16[64,512]{1,0:T(8,128)(2,1)S(1)}, bf16[64,512]{1,0:T(8,128)(2,1)S(1)}, u32[]{:S(2)}, u32[]{:S(2)}) collective-permute-start(bf16[64,512]{1,0:T(8,128)(2,1)S(1)} %collective-permute-done.3), channel_id=1, source_target_pairs={{0,16},{16,0},{1,17},{17,1},{2,18},{18,2},{3,19},{19,3},{4,20},{20... | collective-permute-start | bytes 196616 | tf_op jit(solution)/shard_map/ppermute | solution.py:334
  17.2 0.7 %copy-done = s32[1,11]{1,0:T(1,128)S(1)} copy-done((s32[1,11]{1,0:T(1,128)S(1)}, s32[1,11]{1,0:T(1,128)}, u32[]{:S(2)}) %copy-start) | copy-done | bytes 68
  17.9 1.5 %shard_map.39 = (bf16[2,1040,1024]{2,1,0:T(8,128)(2,1)S(1)}, f32[11,128]{1,0:T(8,128)S(1)}) custom-call(bf16[2,64,1024]{2,1,0:T(8,128)(2,1)S(1)} %shard_map.38.pair_ref.own_ref, s32[1,11]{1,0:T(1,128)S(1)} %copy-done), custom_call_target="tpu_custom_call" | custom-call | flops 5000000000 | bytes 1048576 | tf_op jit(solution)/shard_map/pallas_call | solution.py:266
  19.4 0.0 collective-permute-done.6.sibling_ref
  19.4 2.4 %shard_map.40.near_ref = f32[11,1040,128]{2,1,0:T(8,128)} custom-call(bf16[2,1040,1024]{2,1,0:T(8,128)(2,1)S(1)} %get-tuple-element.13.rows_ref, f32[11,128]{1,0:T(8,128)S(1)} %get-tuple-element.14.scale_ref, bf16[2,64,1024]{2,1,0:T(8,128)(2,1)S(1)} %shard_map.38.pair_ref.own_ref, bf16[2,64,1024]{2,1,0:T(8,128)(2,1)S(1)} %collective-permute-done.6.sibling_ref), custom_call_target="tpu_custom_call" | custom-call | flops 1090519040 | bytes 2129920 | tf_op jit(solution)/shard_map/pallas_call | solution.py:297
  21.8 0.0 collective-permute-done.5.second_ref
  21.8 1.4 %collective-permute-done.4.first_ref = bf16[2,64,1024]{2,1,0:T(8,128)(2,1)S(1)} collective-permute-done((bf16[2,64,1024]{2,1,0:T(8,128)(2,1)S(1)}, bf16[2,64,1024]{2,1,0:T(8,128)(2,1)S(1)}, u32[]{:S(2)}, u32[]{:S(2)}) %collective-permute-start.4) | collective-permute-done | bytes 262176 | tf_op jit(solution)/shard_map/ppermute | solution.py:331
  23.2 0.0 collective-permute-start.7
  23.2 0.5 %collective-permute-start.8 = (bf16[2,64,1024]{2,1,0:T(8,128)(2,1)S(1)}, bf16[2,64,1024]{2,1,0:T(8,128)(2,1)S(1)}, u32[]{:S(2)}, u32[]{:S(2)}) collective-permute-start(bf16[2,64,1024]{2,1,0:T(8,128)(2,1)S(1)} %collective-permute-done.5.second_ref), channel_id=1, source_target_pairs={{0,1},{1,0},{2,3},{3,2},{4,5},{5,4},{6,7},{7,6},{8,9},{9,8},{10,11... | collective-permute-start | bytes 786440 | tf_op jit(solution)/shard_map/ppermute | solution.py:341
  23.8 1.5 %shard_map.41.own_tiles_ref = f32[4,1040,128]{2,1,0:T(8,128)S(1)} custom-call(bf16[2,1040,1024]{2,1,0:T(8,128)(2,1)S(1)} %get-tuple-element.13.rows_ref, f32[11,128]{1,0:T(8,128)S(1)} %get-tuple-element.14.scale_ref, bf16[2,64,1024]{2,1,0:T(8,128)(2,1)S(1)} %collective-permute-done.4.first_ref, bf16[2,64,1024]{2,1,0:T(8,128)(2,1)S(1)} %collective-permute-done.5.second_ref, ...), custom_call_target="tpu_custom_call" | custom-call | flops 1090519040 | bytes 2129920 | tf_op jit(solution)/shard_map/pallas_call | solution.py:297
  25.3 0.0 collective-permute-done.7.first_ref
  25.3 2.9 %shard_map.42 = f32[11,1040,128]{2,1,0:T(8,128)} custom-call(bf16[2,1040,1024]{2,1,0:T(8,128)(2,1)S(1)} %get-tuple-element.13.rows_ref, f32[11,128]{1,0:T(8,128)S(1)} %get-tuple-element.14.scale_ref, bf16[2,64,1024]{2,1,0:T(8,128)(2,1)S(1)} %collective-permute-done.7.first_ref, ...), custom_call_target="tpu_custom_call", output_to_operand_aliasing={{}: (5, {})} | custom-call | flops 1090519040 | bytes 2129920 | tf_op jit(solution)/shard_map/pallas_call | solution.py:297
  (5 shorter events, 0.0 us)
Async XLA Ops:
  2.6 6.4 %collective-permute-start.2 = (bf16[64,512]{1,0:T(8,128)(2,1)S(1)}, bf16[64,512]{1,0:T(8,128)(2,1)S(1)}, u32[]{:S(2)}, u32[]{:S(2)}) collective-permute-start(bf16[64,512]{1,0:T(8,128)(2,1)S(1)} %shard_map.37.white_ref), channel_id=1, source_target_pairs={{0,18},{1,19},{2,16},{3,17},{4,22},{5,23},{6,20},{7,21},{8,26},{9,... | collective-permute-start | bytes 196616 | tf_op jit(solution)/shard_map/ppermute | solution.py:329
  6.5 4.3 %collective-permute-start.1 = (bf16[64,512]{1,0:T(8,128)(2,1)S(1)}, bf16[64,512]{1,0:T(8,128)(2,1)S(1)}, u32[]{:S(2)}, u32[]{:S(2)}) collective-permute-start(bf16[64,512]{1,0:T(8,128)(2,1)S(1)} %shard_map.37.white_ref), channel_id=1, source_target_pairs={{0,2},{1,3},{2,0},{3,1},{4,6},{5,7},{6,4},{7,5},{8,10},{9,11},{10,... | collective-permute-start | bytes 196616 | tf_op jit(solution)/shard_map/ppermute | solution.py:327
  7.1 4.3 %collective-permute-start = (bf16[64,512]{1,0:T(8,128)(2,1)S(1)}, bf16[64,512]{1,0:T(8,128)(2,1)S(1)}, u32[]{:S(2)}, u32[]{:S(2)}) collective-permute-start(bf16[64,512]{1,0:T(8,128)(2,1)S(1)} %shard_map.37.white_ref), channel_id=1, source_target_pairs={{0,16},{16,0},{1,17},{17,1},{2,18},{18,2},{3,19},{19,3},{4,20},{20... | collective-permute-start | bytes 196616 | tf_op jit(solution)/shard_map/ppermute | solution.py:326
  7.2 9.4 %collective-permute-start.3 = (bf16[64,512]{1,0:T(8,128)(2,1)S(1)}, bf16[64,512]{1,0:T(8,128)(2,1)S(1)}, u32[]{:S(2)}, u32[]{:S(2)}) collective-permute-start(bf16[64,512]{1,0:T(8,128)(2,1)S(1)} %shard_map.37.white_ref), channel_id=1, source_target_pairs={{3,8},{7,12},{8,3},{12,7},{19,24},{23,28},{24,19},{28,23}} | collective-permute-start | bytes 196616 | tf_op jit(solution)/shard_map/ppermute | solution.py:325
  11.3 8.1 %collective-permute-start.6 = (bf16[2,64,1024]{2,1,0:T(8,128)(2,1)S(1)}, bf16[2,64,1024]{2,1,0:T(8,128)(2,1)S(1)}, u32[]{:S(2)}, u32[]{:S(2)}) collective-permute-start(bf16[2,64,1024]{2,1,0:T(8,128)(2,1)S(1)} %shard_map.38.pair_ref.own_ref), channel_id=1, source_target_pairs={{0,1},{1,0},{2,3},{3,2},{4,5},{5,4},{6,7},{7,6},{8,9},{9,8},{10,11... | collective-permute-start | bytes 786440 | tf_op jit(solution)/shard_map/ppermute | solution.py:335
  11.4 10.4 %collective-permute-start.5 = (bf16[2,64,1024]{2,1,0:T(8,128)(2,1)S(1)}, bf16[2,64,1024]{2,1,0:T(8,128)(2,1)S(1)}, u32[]{:S(2)}, u32[]{:S(2)}) collective-permute-start(bf16[2,64,1024]{2,1,0:T(8,128)(2,1)S(1)} %shard_map.38.pair_ref.own_ref), channel_id=1, source_target_pairs={{4,8},{5,9},{6,10},{7,11},{8,4},{9,5},{10,6},{11,7},{20,24},{21,25... | collective-permute-start | bytes 786440 | tf_op jit(solution)/shard_map/ppermute | solution.py:332
  12.1 11.1 %collective-permute-start.4 = (bf16[2,64,1024]{2,1,0:T(8,128)(2,1)S(1)}, bf16[2,64,1024]{2,1,0:T(8,128)(2,1)S(1)}, u32[]{:S(2)}, u32[]{:S(2)}) collective-permute-start(bf16[2,64,1024]{2,1,0:T(8,128)(2,1)S(1)} %shard_map.38.pair_ref.own_ref), channel_id=1, source_target_pairs={{0,4},{1,5},{2,6},{3,7},{4,0},{5,1},{6,2},{7,3},{8,12},{9,13},{10,... | collective-permute-start | bytes 786440 | tf_op jit(solution)/shard_map/ppermute | solution.py:331
  16.6 7.2 %collective-permute-start.9 = (bf16[64,512]{1,0:T(8,128)(2,1)S(1)}, bf16[64,512]{1,0:T(8,128)(2,1)S(1)}, u32[]{:S(2)}, u32[]{:S(2)}) collective-permute-start(bf16[64,512]{1,0:T(8,128)(2,1)S(1)} %collective-permute-done.3), channel_id=1, source_target_pairs={{0,16},{16,0},{1,17},{17,1},{2,18},{18,2},{3,19},{19,3},{4,20},{20... | collective-permute-start | bytes 196616 | tf_op jit(solution)/shard_map/ppermute | solution.py:334
  17.2 0.7 %copy-start = (s32[1,11]{1,0:T(1,128)S(1)}, s32[1,11]{1,0:T(1,128)}, u32[]{:S(2)}) copy-start(s32[1,11]{1,0:T(1,128)} %partners_ref.1) | copy-start | bytes 136
  23.2 2.1 %collective-permute-start.7 = (bf16[2,64,1024]{2,1,0:T(8,128)(2,1)S(1)}, bf16[2,64,1024]{2,1,0:T(8,128)(2,1)S(1)}, u32[]{:S(2)}, u32[]{:S(2)}) collective-permute-start(bf16[2,64,1024]{2,1,0:T(8,128)(2,1)S(1)} %collective-permute-done.4.first_ref), channel_id=1, source_target_pairs={{0,1},{1,0},{2,3},{3,2},{4,5},{5,4},{6,7},{7,6},{8,9},{9,8},{10,11... | collective-permute-start | bytes 786440 | tf_op jit(solution)/shard_map/ppermute | solution.py:340
  23.2 2.1 %collective-permute-start.8 = (bf16[2,64,1024]{2,1,0:T(8,128)(2,1)S(1)}, bf16[2,64,1024]{2,1,0:T(8,128)(2,1)S(1)}, u32[]{:S(2)}, u32[]{:S(2)}) collective-permute-start(bf16[2,64,1024]{2,1,0:T(8,128)(2,1)S(1)} %collective-permute-done.5.second_ref), channel_id=1, source_target_pairs={{0,1},{1,0},{2,3},{3,2},{4,5},{5,4},{6,7},{7,6},{8,9},{9,8},{10,11... | collective-permute-start | bytes 786440 | tf_op jit(solution)/shard_map/ppermute | solution.py:341

commit v5 on v4

--- a/solution.py
+++ b/solution.py
@@ -215,7 +215,7 @@
 def far_slots(core):
     chan = lax.axis_index("chan")
     place = lax.rem(chan, QUAD)
-    ahead = 1 - 2 * lax.rem(lax.div(chan, QUAD), 2)
+    ahead = 2 * lax.rem(lax.div(chan, QUAD), 2) - 1
     slots, stands = [], []
     for plane in (ahead, -ahead):
         for x in range(2):
@@ -315,8 +315,8 @@
     channels = traces.shape[1]
     half = channels // segments
     assert segments == 2 and blocks % QUAD == 0 and slots == 2 * REACH + 1
-    plane_one = [(c, c ^ QUAD) for c in range(blocks)]
-    plane_two = [(c, ((c + QUAD) ^ QUAD) - QUAD) for c in range(QUAD, blocks - QUAD)]
+    plane_two = [(c, c ^ QUAD) for c in range(blocks)]
+    plane_one = [(c, ((c + QUAD) ^ QUAD) - QUAD) for c in range(QUAD, blocks - QUAD)]
     sibling = [(c, c ^ 1) for c in range(blocks)]
     corners = [(c, c + REACH) for c in range(QUAD - 1, blocks - REACH, QUAD)]
     corners += [(c, c - REACH) for c in range(2 * QUAD, blocks, QUAD)]
@@ -332,7 +332,7 @@
     second = lax.ppermute(quad, "chan", plane_two)
     near, corner = lax.optimization_barrier((quad, corner))
     corner_other = lax.ppermute(corner, "seg", [(0, 1), (1, 0)])
-    beside = lax.ppermute(quad, "chan", sibling)
+    beside = lax.ppermute(near, "chan", sibling)
     rows, scale = lag_rows(near, partners, traces.shape[2], half, norm_scale)
     out = correlate(near_kernel, [rows, scale, quad, beside])
     corner = jnp.concatenate([corner, corner_other], axis=1)

time: 28.4 us -> 26.4 us (0.930)
  the two profiles are of different devices: /device:TPU:0 before, /device:TPU:15 now
where the time goes in v5:
time: 26.4 us; the launch traced here: 26.2 us
  starting transfers between devices  13.8 us (52%)
  Pallas kernels  10.8 us (41%)
  waiting for transfers between devices  0.81 us (3%)
  local copies, waits for them, and re-layouts  0.65 us (2%)
    pallas_call x3, Pallas kernels, correlate(): pl.pallas_call(kernel, out_shape=jax.ShapeDtypeStruct((QUAD if tiles_only...  6.73 us
    ppermute x1, starting transfers between devices, local(): corner = lax.ppermute(white, 'chan', corners)  5.58 us
    pallas_call x1, Pallas kernels, spectra(): pl.pallas_call(functools.partial(spectrum_kernel, step), out_shape=jax.Sh...  2.56 us
    ppermute x1, starting transfers between devices, local(): beside = lax.ppermute(near, 'chan', sibling)  2.41 us
    ppermute x1, starting transfers between devices, local(): first = lax.ppermute(quad, 'chan', plane_one)  1.91 us
    pallas_call x1, Pallas kernels, lag_rows(): pl.pallas_call(functools.partial(rows_kernel, samples, norm_scale), out_s...  1.53 us
    ppermute x1, starting transfers between devices, local(): other = lax.ppermute(white, 'seg', [(0, 1), (1, 0)])  1.24 us
    ppermute x1, starting transfers between devices, local(): across = lax.ppermute(white, 'chan', [(c, c ^ 2) for c in range(blocks)])  1.21 us
  transfers between devices with their start and end apart: 10, of which 2 were waited for; matrix products, arithmetic and copies ran while one was open for 0% of the time, Pallas kernels for 21%

profile of v5, /device:TPU:15, one launch (start us, length us, event | category | flops | bytes accessed | tf_op | source)
XLA Modules:
  0.0 26.2 jit_solution(18155728411086593312)
XLA Ops:
  0.0 2.6 %shard_map.37.white_ref = bf16[64,512]{1,0:T(8,128)(2,1)S(1)} custom-call(bf16[64,4096]{1,0:T(8,128)(2,1)} %bitcast.2, bf16[2,256,512]{2,1,0:T(8,128)(2,1)} %constant.2.clone.table_hbm), custom_call_target="tpu_custom_call" | custom-call | tf_op jit(solution)/shard_map/pallas_call | solution.py:81
  2.6 0.3 %collective-permute-start.2 = (bf16[64,512]{1,0:T(8,128)(2,1)S(1)}, bf16[64,512]{1,0:T(8,128)(2,1)S(1)}, u32[]{:S(2)}, u32[]{:S(2)}) collective-permute-start(bf16[64,512]{1,0:T(8,128)(2,1)S(1)} %shard_map.37.white_ref), channel_id=1, source_target_pairs={{0,18},{1,19},{2,16},{3,17},{4,22},{5,23},{6,20},{7,21},{8,26},{9,... | collective-permute-start | bytes 196616 | tf_op jit(solution)/shard_map/ppermute | solution.py:329
  2.8 1.2 %collective-permute-start.1 = (bf16[64,512]{1,0:T(8,128)(2,1)S(1)}, bf16[64,512]{1,0:T(8,128)(2,1)S(1)}, u32[]{:S(2)}, u32[]{:S(2)}) collective-permute-start(bf16[64,512]{1,0:T(8,128)(2,1)S(1)} %shard_map.37.white_ref), channel_id=1, source_target_pairs={{0,2},{1,3},{2,0},{3,1},{4,6},{5,7},{6,4},{7,5},{8,10},{9,11},{10,... | collective-permute-start | bytes 196616 | tf_op jit(solution)/shard_map/ppermute | solution.py:327
  4.0 1.2 %collective-permute-start = (bf16[64,512]{1,0:T(8,128)(2,1)S(1)}, bf16[64,512]{1,0:T(8,128)(2,1)S(1)}, u32[]{:S(2)}, u32[]{:S(2)}) collective-permute-start(bf16[64,512]{1,0:T(8,128)(2,1)S(1)} %shard_map.37.white_ref), channel_id=1, source_target_pairs={{0,16},{16,0},{1,17},{17,1},{2,18},{18,2},{3,19},{19,3},{4,20},{20... | collective-permute-start | bytes 196616 | tf_op jit(solution)/shard_map/ppermute | solution.py:326
  5.3 5.6 %collective-permute-start.3 = (bf16[64,512]{1,0:T(8,128)(2,1)S(1)}, bf16[64,512]{1,0:T(8,128)(2,1)S(1)}, u32[]{:S(2)}, u32[]{:S(2)}) collective-permute-start(bf16[64,512]{1,0:T(8,128)(2,1)S(1)} %shard_map.37.white_ref), channel_id=1, source_target_pairs={{3,8},{7,12},{8,3},{12,7},{19,24},{23,28},{24,19},{28,23}} | collective-permute-start | bytes 196616 | tf_op jit(solution)/shard_map/ppermute | solution.py:325
  10.9 0.0 collective-permute-done.2.diagonal_ref
  10.9 0.0 collective-permute-done.1.across_ref
  10.9 0.0 collective-permute-done.other_ref
  10.9 0.2 collective-permute-start.5
  11.2 1.9 %collective-permute-start.4 = (bf16[2,64,1024]{2,1,0:T(8,128)(2,1)S(1)}, bf16[2,64,1024]{2,1,0:T(8,128)(2,1)S(1)}, u32[]{:S(2)}, u32[]{:S(2)}) collective-permute-start(bf16[2,64,1024]{2,1,0:T(8,128)(2,1)S(1)} %shard_map.38.pair_ref.own_ref), channel_id=1, source_target_pairs={{4,8},{5,9},{6,10},{7,11},{8,4},{9,5},{10,6},{11,7},{20,24},{21,25... | collective-permute-start | bytes 786440 | tf_op jit(solution)/shard_map/ppermute | solution.py:331
  13.1 0.4 %collective-permute-done.3 = bf16[64,512]{1,0:T(8,128)(2,1)S(1)} collective-permute-done((bf16[64,512]{1,0:T(8,128)(2,1)S(1)}, bf16[64,512]{1,0:T(8,128)(2,1)S(1)}, u32[]{:S(2)}, u32[]{:S(2)}) %collective-permute-start.3) | collective-permute-done | bytes 65568 | tf_op jit(solution)/shard_map/ppermute | solution.py:325
  13.4 0.4 %collective-permute-start.9 = (bf16[64,512]{1,0:T(8,128)(2,1)S(1)}, bf16[64,512]{1,0:T(8,128)(2,1)S(1)}, u32[]{:S(2)}, u32[]{:S(2)}) collective-permute-start(bf16[64,512]{1,0:T(8,128)(2,1)S(1)} %collective-permute-done.3), channel_id=1, source_target_pairs={{0,16},{16,0},{1,17},{17,1},{2,18},{18,2},{3,19},{19,3},{4,20},{20... | collective-permute-start | bytes 196616 | tf_op jit(solution)/shard_map/ppermute | solution.py:334
  13.9 2.4 %collective-permute-start.6 = (bf16[2,64,1024]{2,1,0:T(8,128)(2,1)S(1)}, bf16[2,64,1024]{2,1,0:T(8,128)(2,1)S(1)}, u32[]{:S(2)}, u32[]{:S(2)}) collective-permute-start(bf16[2,64,1024]{2,1,0:T(8,128)(2,1)S(1)} %shard_map.38.pair_ref.own_ref), channel_id=1, source_target_pairs={{0,1},{1,0},{2,3},{3,2},{4,5},{5,4},{6,7},{7,6},{8,9},{9,8},{10,11... | collective-permute-start | bytes 786440 | tf_op jit(solution)/shard_map/ppermute | solution.py:335
  16.3 0.7 %copy-done = s32[1,11]{1,0:T(1,128)S(1)} copy-done((s32[1,11]{1,0:T(1,128)S(1)}, s32[1,11]{1,0:T(1,128)}, u32[]{:S(2)}) %copy-start) | copy-done | bytes 68
  16.9 1.5 %shard_map.39 = (bf16[2,1040,1024]{2,1,0:T(8,128)(2,1)S(1)}, f32[11,128]{1,0:T(8,128)S(1)}) custom-call(bf16[2,64,1024]{2,1,0:T(8,128)(2,1)S(1)} %shard_map.38.pair_ref.own_ref, s32[1,11]{1,0:T(1,128)S(1)} %copy-done), custom_call_target="tpu_custom_call" | custom-call | flops 5000000000 | bytes 1048576 | tf_op jit(solution)/shard_map/pallas_call | solution.py:266
  18.5 0.0 collective-permute-done.6.sibling_ref
  18.5 2.4 %shard_map.40.near_ref = f32[11,1040,128]{2,1,0:T(8,128)} custom-call(bf16[2,1040,1024]{2,1,0:T(8,128)(2,1)S(1)} %get-tuple-element.13.rows_ref, f32[11,128]{1,0:T(8,128)S(1)} %get-tuple-element.14.scale_ref, bf16[2,64,1024]{2,1,0:T(8,128)(2,1)S(1)} %shard_map.38.pair_ref.own_ref, bf16[2,64,1024]{2,1,0:T(8,128)(2,1)S(1)} %collective-permute-done.6.sibling_ref), custom_call_target="tpu_custom_call" | custom-call | flops 1090519040 | bytes 2129920 | tf_op jit(solution)/shard_map/pallas_call | solution.py:297
  20.9 0.0 collective-permute-done.5.second_ref
  20.9 0.4 %collective-permute-done.4.first_ref = bf16[2,64,1024]{2,1,0:T(8,128)(2,1)S(1)} collective-permute-done((bf16[2,64,1024]{2,1,0:T(8,128)(2,1)S(1)}, bf16[2,64,1024]{2,1,0:T(8,128)(2,1)S(1)}, u32[]{:S(2)}, u32[]{:S(2)}) %collective-permute-start.4) | collective-permute-done | bytes 262176 | tf_op jit(solution)/shard_map/ppermute | solution.py:331
  21.3 0.5 %collective-permute-start.7 = (bf16[2,64,1024]{2,1,0:T(8,128)(2,1)S(1)}, bf16[2,64,1024]{2,1,0:T(8,128)(2,1)S(1)}, u32[]{:S(2)}, u32[]{:S(2)}) collective-permute-start(bf16[2,64,1024]{2,1,0:T(8,128)(2,1)S(1)} %collective-permute-done.4.first_ref), channel_id=1, source_target_pairs={{0,1},{1,0},{2,3},{3,2},{4,5},{5,4},{6,7},{7,6},{8,9},{9,8},{10,11... | collective-permute-start | bytes 786440 | tf_op jit(solution)/shard_map/ppermute | solution.py:340
  21.8 0.0 collective-permute-start.8
  21.8 0.0 collective-permute-done.9
  21.8 1.5 %shard_map.41.own_tiles_ref = f32[4,1040,128]{2,1,0:T(8,128)S(1)} custom-call(bf16[2,1040,1024]{2,1,0:T(8,128)(2,1)S(1)} %get-tuple-element.13.rows_ref, f32[11,128]{1,0:T(8,128)S(1)} %get-tuple-element.14.scale_ref, bf16[2,64,1024]{2,1,0:T(8,128)(2,1)S(1)} %collective-permute-done.4.first_ref, bf16[2,64,1024]{2,1,0:T(8,128)(2,1)S(1)} %collective-permute-done.5.second_ref, ...), custom_call_target="tpu_custom_call" | custom-call | flops 1090519040 | bytes 2129920 | tf_op jit(solution)/shard_map/pallas_call | solution.py:297
  23.4 2.8 %shard_map.42 = f32[11,1040,128]{2,1,0:T(8,128)} custom-call(bf16[2,1040,1024]{2,1,0:T(8,128)(2,1)S(1)} %get-tuple-element.13.rows_ref, f32[11,128]{1,0:T(8,128)S(1)} %get-tuple-element.14.scale_ref, bf16[2,64,1024]{2,1,0:T(8,128)(2,1)S(1)} %collective-permute-done.7.first_ref, ...), custom_call_target="tpu_custom_call", output_to_operand_aliasing={{}: (5, {})} | custom-call | flops 1090519040 | bytes 2129920 | tf_op jit(solution)/shard_map/pallas_call | solution.py:297
  (5 shorter events, 0.0 us)
Async XLA Ops:
  2.6 8.3 %collective-permute-start.2 = (bf16[64,512]{1,0:T(8,128)(2,1)S(1)}, bf16[64,512]{1,0:T(8,128)(2,1)S(1)}, u32[]{:S(2)}, u32[]{:S(2)}) collective-permute-start(bf16[64,512]{1,0:T(8,128)(2,1)S(1)} %shard_map.37.white_ref), channel_id=1, source_target_pairs={{0,18},{1,19},{2,16},{3,17},{4,22},{5,23},{6,20},{7,21},{8,26},{9,... | collective-permute-start | bytes 196616 | tf_op jit(solution)/shard_map/ppermute | solution.py:329
  2.8 8.1 %collective-permute-start.1 = (bf16[64,512]{1,0:T(8,128)(2,1)S(1)}, bf16[64,512]{1,0:T(8,128)(2,1)S(1)}, u32[]{:S(2)}, u32[]{:S(2)}) collective-permute-start(bf16[64,512]{1,0:T(8,128)(2,1)S(1)} %shard_map.37.white_ref), channel_id=1, source_target_pairs={{0,2},{1,3},{2,0},{3,1},{4,6},{5,7},{6,4},{7,5},{8,10},{9,11},{10,... | collective-permute-start | bytes 196616 | tf_op jit(solution)/shard_map/ppermute | solution.py:327
  4.0 6.8 %collective-permute-start = (bf16[64,512]{1,0:T(8,128)(2,1)S(1)}, bf16[64,512]{1,0:T(8,128)(2,1)S(1)}, u32[]{:S(2)}, u32[]{:S(2)}) collective-permute-start(bf16[64,512]{1,0:T(8,128)(2,1)S(1)} %shard_map.37.white_ref), channel_id=1, source_target_pairs={{0,16},{16,0},{1,17},{17,1},{2,18},{18,2},{3,19},{19,3},{4,20},{20... | collective-permute-start | bytes 196616 | tf_op jit(solution)/shard_map/ppermute | solution.py:326
  5.3 8.2 %collective-permute-start.3 = (bf16[64,512]{1,0:T(8,128)(2,1)S(1)}, bf16[64,512]{1,0:T(8,128)(2,1)S(1)}, u32[]{:S(2)}, u32[]{:S(2)}) collective-permute-start(bf16[64,512]{1,0:T(8,128)(2,1)S(1)} %shard_map.37.white_ref), channel_id=1, source_target_pairs={{3,8},{7,12},{8,3},{12,7},{19,24},{23,28},{24,19},{28,23}} | collective-permute-start | bytes 196616 | tf_op jit(solution)/shard_map/ppermute | solution.py:325
  10.9 9.9 %collective-permute-start.5 = (bf16[2,64,1024]{2,1,0:T(8,128)(2,1)S(1)}, bf16[2,64,1024]{2,1,0:T(8,128)(2,1)S(1)}, u32[]{:S(2)}, u32[]{:S(2)}) collective-permute-start(bf16[2,64,1024]{2,1,0:T(8,128)(2,1)S(1)} %shard_map.38.pair_ref.own_ref), channel_id=1, source_target_pairs={{0,4},{1,5},{2,6},{3,7},{4,0},{5,1},{6,2},{7,3},{8,12},{9,13},{10,... | collective-permute-start | bytes 786440 | tf_op jit(solution)/shard_map/ppermute | solution.py:332
  11.2 10.1 %collective-permute-start.4 = (bf16[2,64,1024]{2,1,0:T(8,128)(2,1)S(1)}, bf16[2,64,1024]{2,1,0:T(8,128)(2,1)S(1)}, u32[]{:S(2)}, u32[]{:S(2)}) collective-permute-start(bf16[2,64,1024]{2,1,0:T(8,128)(2,1)S(1)} %shard_map.38.pair_ref.own_ref), channel_id=1, source_target_pairs={{4,8},{5,9},{6,10},{7,11},{8,4},{9,5},{10,6},{11,7},{20,24},{21,25... | collective-permute-start | bytes 786440 | tf_op jit(solution)/shard_map/ppermute | solution.py:331
  13.4 8.4 %collective-permute-start.9 = (bf16[64,512]{1,0:T(8,128)(2,1)S(1)}, bf16[64,512]{1,0:T(8,128)(2,1)S(1)}, u32[]{:S(2)}, u32[]{:S(2)}) collective-permute-start(bf16[64,512]{1,0:T(8,128)(2,1)S(1)} %collective-permute-done.3), channel_id=1, source_target_pairs={{0,16},{16,0},{1,17},{17,1},{2,18},{18,2},{3,19},{19,3},{4,20},{20... | collective-permute-start | bytes 196616 | tf_op jit(solution)/shard_map/ppermute | solution.py:334
  13.9 4.6 %collective-permute-start.6 = (bf16[2,64,1024]{2,1,0:T(8,128)(2,1)S(1)}, bf16[2,64,1024]{2,1,0:T(8,128)(2,1)S(1)}, u32[]{:S(2)}, u32[]{:S(2)}) collective-permute-start(bf16[2,64,1024]{2,1,0:T(8,128)(2,1)S(1)} %shard_map.38.pair_ref.own_ref), channel_id=1, source_target_pairs={{0,1},{1,0},{2,3},{3,2},{4,5},{5,4},{6,7},{7,6},{8,9},{9,8},{10,11... | collective-permute-start | bytes 786440 | tf_op jit(solution)/shard_map/ppermute | solution.py:335
  16.3 0.7 %copy-start = (s32[1,11]{1,0:T(1,128)S(1)}, s32[1,11]{1,0:T(1,128)}, u32[]{:S(2)}) copy-start(s32[1,11]{1,0:T(1,128)} %partners_ref.1) | copy-start | bytes 136
  21.3 2.1 %collective-permute-start.7 = (bf16[2,64,1024]{2,1,0:T(8,128)(2,1)S(1)}, bf16[2,64,1024]{2,1,0:T(8,128)(2,1)S(1)}, u32[]{:S(2)}, u32[]{:S(2)}) collective-permute-start(bf16[2,64,1024]{2,1,0:T(8,128)(2,1)S(1)} %collective-permute-done.4.first_ref), channel_id=1, source_target_pairs={{0,1},{1,0},{2,3},{3,2},{4,5},{5,4},{6,7},{7,6},{8,9},{9,8},{10,11... | collective-permute-start | bytes 786440 | tf_op jit(solution)/shard_map/ppermute | solution.py:340
  21.8 1.6 %collective-permute-start.8 = (bf16[2,64,1024]{2,1,0:T(8,128)(2,1)S(1)}, bf16[2,64,1024]{2,1,0:T(8,128)(2,1)S(1)}, u32[]{:S(2)}, u32[]{:S(2)}) collective-permute-start(bf16[2,64,1024]{2,1,0:T(8,128)(2,1)S(1)} %collective-permute-done.5.second_ref), channel_id=1, source_target_pairs={{0,1},{1,0},{2,3},{3,2},{4,5},{5,4},{6,7},{7,6},{8,9},{9,8},{10,11... | collective-permute-start | bytes 786440 | tf_op jit(solution)/shard_map/ppermute | solution.py:341

commit v6 on v5

--- a/solution.py
+++ b/solution.py
@@ -34,7 +34,7 @@
 def spectrum_kernel(step, traces_hbm, table_hbm, white_ref, traces, table, sems):
     channels = white_ref.shape[0]
     stretches = traces.shape[0] // channels
-    group = 4
+    group = stretches
     table_copy = pltpu.make_async_copy(table_hbm, table, sems.at[stretches])
     table_copy.start()
     copies = [
@@ -88,6 +88,7 @@
             pltpu.VMEM(table.shape, jnp.bfloat16),
             pltpu.SemaphoreType.DMA((samples // step + 1,)),
         ],
+        cost_estimate=pl.CostEstimate(flops=10**9, bytes_accessed=2**20, transcendentals=0),
         compiler_params=pltpu.CompilerParams(vmem_limit_bytes=SPECTRUM_VMEM),
     )(traces, jnp.asarray(table))
 

time: 26.4 us -> 25.9 us (0.981)
  waiting for transfers between devices: 0.81 us -> 1.47 us
  local copies, waits for them, and re-layouts: 0.65 us -> 0.01 us
  Pallas kernels: 10.8 us -> 10.4 us
    ppermute x1, waiting for transfers between devices: 0.42 us -> 1.08 us  [local(): first = lax.ppermute(quad, 'chan', plane_one)]
    unnamed x2, local copies, waits for them, and re-layouts: 0.65 us -> 0.01 us
    pallas_call x1, Pallas kernels: 2.56 us -> 2.11 us  [spectra(): pl.pallas_call(functools.partial(spectrum_kernel, step), out_shape=jax.Sh...]
where the time goes in v6:
time: 25.9 us; the launch traced here: 25.8 us
  starting transfers between devices  13.8 us (53%)
  Pallas kernels  10.4 us (40%)
  waiting for transfers between devices  1.47 us (6%)
    pallas_call x3, Pallas kernels, correlate(): pl.pallas_call(kernel, out_shape=jax.ShapeDtypeStruct((QUAD if tiles_only...  6.73 us
    ppermute x1, starting transfers between devices, local(): corner = lax.ppermute(white, 'chan', corners)  5.58 us
    ppermute x1, starting transfers between devices, local(): beside = lax.ppermute(near, 'chan', sibling)  2.41 us
    pallas_call x1, Pallas kernels, spectra(): pl.pallas_call(functools.partial(spectrum_kernel, step), out_shape=jax.Sh...  2.11 us
    ppermute x1, starting transfers between devices, local(): first = lax.ppermute(quad, 'chan', plane_one)  1.91 us
    pallas_call x1, Pallas kernels, lag_rows(): pl.pallas_call(functools.partial(rows_kernel, samples, norm_scale), out_s...  1.53 us
    ppermute x1, starting transfers between devices, local(): other = lax.ppermute(white, 'seg', [(0, 1), (1, 0)])  1.24 us
    ppermute x1, starting transfers between devices, local(): across = lax.ppermute(white, 'chan', [(c, c ^ 2) for c in range(blocks)])  1.21 us
  transfers between devices with their start and end apart: 10, of which 2 were waited for; matrix products, arithmetic and copies ran while one was open for 0% of the time, Pallas kernels for 21%

profile of v6, /device:TPU:15, one launch (start us, length us, event | category | flops | bytes accessed | tf_op | source)
XLA Modules:
  0.0 25.8 jit_solution(4245849248455369304)
XLA Ops:
  0.0 2.1 %shard_map.37.white_ref = bf16[64,512]{1,0:T(8,128)(2,1)S(1)} custom-call(bf16[64,4096]{1,0:T(8,128)(2,1)} %bitcast.2, bf16[2,256,512]{2,1,0:T(8,128)(2,1)} %constant.2.clone.table_hbm), custom_call_target="tpu_custom_call" | custom-call | flops 1000000000 | bytes 1048576 | tf_op jit(solution)/shard_map/pallas_call | solution.py:81
  2.1 0.3 %collective-permute-start.2 = (bf16[64,512]{1,0:T(8,128)(2,1)S(1)}, bf16[64,512]{1,0:T(8,128)(2,1)S(1)}, u32[]{:S(2)}, u32[]{:S(2)}) collective-permute-start(bf16[64,512]{1,0:T(8,128)(2,1)S(1)} %shard_map.37.white_ref), channel_id=1, source_target_pairs={{0,18},{1,19},{2,16},{3,17},{4,22},{5,23},{6,20},{7,21},{8,26},{9,... | collective-permute-start | bytes 196616 | tf_op jit(solution)/shard_map/ppermute | solution.py:330
  2.4 1.2 %collective-permute-start.1 = (bf16[64,512]{1,0:T(8,128)(2,1)S(1)}, bf16[64,512]{1,0:T(8,128)(2,1)S(1)}, u32[]{:S(2)}, u32[]{:S(2)}) collective-permute-start(bf16[64,512]{1,0:T(8,128)(2,1)S(1)} %shard_map.37.white_ref), channel_id=1, source_target_pairs={{0,2},{1,3},{2,0},{3,1},{4,6},{5,7},{6,4},{7,5},{8,10},{9,11},{10,... | collective-permute-start | bytes 196616 | tf_op jit(solution)/shard_map/ppermute | solution.py:328
  3.6 1.2 %collective-permute-start = (bf16[64,512]{1,0:T(8,128)(2,1)S(1)}, bf16[64,512]{1,0:T(8,128)(2,1)S(1)}, u32[]{:S(2)}, u32[]{:S(2)}) collective-permute-start(bf16[64,512]{1,0:T(8,128)(2,1)S(1)} %shard_map.37.white_ref), channel_id=1, source_target_pairs={{0,16},{16,0},{1,17},{17,1},{2,18},{18,2},{3,19},{19,3},{4,20},{20... | collective-permute-start | bytes 196616 | tf_op jit(solution)/shard_map/ppermute | solution.py:327
  4.8 5.6 %collective-permute-start.3 = (bf16[64,512]{1,0:T(8,128)(2,1)S(1)}, bf16[64,512]{1,0:T(8,128)(2,1)S(1)}, u32[]{:S(2)}, u32[]{:S(2)}) collective-permute-start(bf16[64,512]{1,0:T(8,128)(2,1)S(1)} %shard_map.37.white_ref), channel_id=1, source_target_pairs={{3,8},{7,12},{8,3},{12,7},{19,24},{23,28},{24,19},{28,23}} | collective-permute-start | bytes 196616 | tf_op jit(solution)/shard_map/ppermute | solution.py:326
  10.4 0.0 collective-permute-done.2.diagonal_ref
  10.4 0.0 collective-permute-done.1.across_ref
  10.4 0.0 collective-permute-done.other_ref
  10.5 0.2 collective-permute-start.5
  10.7 1.9 %collective-permute-start.4 = (bf16[2,64,1024]{2,1,0:T(8,128)(2,1)S(1)}, bf16[2,64,1024]{2,1,0:T(8,128)(2,1)S(1)}, u32[]{:S(2)}, u32[]{:S(2)}) collective-permute-start(bf16[2,64,1024]{2,1,0:T(8,128)(2,1)S(1)} %shard_map.38.pair_ref.own_ref), channel_id=1, source_target_pairs={{4,8},{5,9},{6,10},{7,11},{8,4},{9,5},{10,6},{11,7},{20,24},{21,25... | collective-permute-start | bytes 786440 | tf_op jit(solution)/shard_map/ppermute | solution.py:332
  12.6 0.4 %collective-permute-done.3 = bf16[64,512]{1,0:T(8,128)(2,1)S(1)} collective-permute-done((bf16[64,512]{1,0:T(8,128)(2,1)S(1)}, bf16[64,512]{1,0:T(8,128)(2,1)S(1)}, u32[]{:S(2)}, u32[]{:S(2)}) %collective-permute-start.3) | collective-permute-done | bytes 65568 | tf_op jit(solution)/shard_map/ppermute | solution.py:326
  13.0 0.4 %collective-permute-start.9 = (bf16[64,512]{1,0:T(8,128)(2,1)S(1)}, bf16[64,512]{1,0:T(8,128)(2,1)S(1)}, u32[]{:S(2)}, u32[]{:S(2)}) collective-permute-start(bf16[64,512]{1,0:T(8,128)(2,1)S(1)} %collective-permute-done.3), channel_id=1, source_target_pairs={{0,16},{16,0},{1,17},{17,1},{2,18},{18,2},{3,19},{19,3},{4,20},{20... | collective-permute-start | bytes 196616 | tf_op jit(solution)/shard_map/ppermute | solution.py:335
  13.4 2.4 %collective-permute-start.6 = (bf16[2,64,1024]{2,1,0:T(8,128)(2,1)S(1)}, bf16[2,64,1024]{2,1,0:T(8,128)(2,1)S(1)}, u32[]{:S(2)}, u32[]{:S(2)}) collective-permute-start(bf16[2,64,1024]{2,1,0:T(8,128)(2,1)S(1)} %shard_map.38.pair_ref.own_ref), channel_id=1, source_target_pairs={{0,1},{1,0},{2,3},{3,2},{4,5},{5,4},{6,7},{7,6},{8,9},{9,8},{10,11... | collective-permute-start | bytes 786440 | tf_op jit(solution)/shard_map/ppermute | solution.py:336
  15.8 1.5 %shard_map.39 = (bf16[2,1040,1024]{2,1,0:T(8,128)(2,1)S(1)}, f32[11,128]{1,0:T(8,128)S(1)}) custom-call(bf16[2,64,1024]{2,1,0:T(8,128)(2,1)S(1)} %shard_map.38.pair_ref.own_ref, s32[1,11]{1,0:T(1,128)S(1)} %copy-done), custom_call_target="tpu_custom_call" | custom-call | flops 5000000000 | bytes 1048576 | tf_op jit(solution)/shard_map/pallas_call | solution.py:267
  17.4 0.0 collective-permute-done.6.sibling_ref
  17.4 2.4 %shard_map.40.near_ref = f32[11,1040,128]{2,1,0:T(8,128)} custom-call(bf16[2,1040,1024]{2,1,0:T(8,128)(2,1)S(1)} %get-tuple-element.13.rows_ref, f32[11,128]{1,0:T(8,128)S(1)} %get-tuple-element.14.scale_ref, bf16[2,64,1024]{2,1,0:T(8,128)(2,1)S(1)} %shard_map.38.pair_ref.own_ref, bf16[2,64,1024]{2,1,0:T(8,128)(2,1)S(1)} %collective-permute-done.6.sibling_ref), custom_call_target="tpu_custom_call" | custom-call | flops 1090519040 | bytes 2129920 | tf_op jit(solution)/shard_map/pallas_call | solution.py:298
  19.8 0.0 collective-permute-done.5.second_ref
  19.8 1.1 %collective-permute-done.4.first_ref = bf16[2,64,1024]{2,1,0:T(8,128)(2,1)S(1)} collective-permute-done((bf16[2,64,1024]{2,1,0:T(8,128)(2,1)S(1)}, bf16[2,64,1024]{2,1,0:T(8,128)(2,1)S(1)}, u32[]{:S(2)}, u32[]{:S(2)}) %collective-permute-start.4) | collective-permute-done | bytes 262176 | tf_op jit(solution)/shard_map/ppermute | solution.py:332
  20.9 0.5 %collective-permute-start.7 = (bf16[2,64,1024]{2,1,0:T(8,128)(2,1)S(1)}, bf16[2,64,1024]{2,1,0:T(8,128)(2,1)S(1)}, u32[]{:S(2)}, u32[]{:S(2)}) collective-permute-start(bf16[2,64,1024]{2,1,0:T(8,128)(2,1)S(1)} %collective-permute-done.4.first_ref), channel_id=1, source_target_pairs={{0,1},{1,0},{2,3},{3,2},{4,5},{5,4},{6,7},{7,6},{8,9},{9,8},{10,11... | collective-permute-start | bytes 786440 | tf_op jit(solution)/shard_map/ppermute | solution.py:341
  21.3 0.0 collective-permute-start.8
  21.4 0.0 collective-permute-done.9
  21.4 1.5 %shard_map.41.own_tiles_ref = f32[4,1040,128]{2,1,0:T(8,128)S(1)} custom-call(bf16[2,1040,1024]{2,1,0:T(8,128)(2,1)S(1)} %get-tuple-element.13.rows_ref, f32[11,128]{1,0:T(8,128)S(1)} %get-tuple-element.14.scale_ref, bf16[2,64,1024]{2,1,0:T(8,128)(2,1)S(1)} %collective-permute-done.4.first_ref, bf16[2,64,1024]{2,1,0:T(8,128)(2,1)S(1)} %collective-permute-done.5.second_ref, ...), custom_call_target="tpu_custom_call" | custom-call | flops 1090519040 | bytes 2129920 | tf_op jit(solution)/shard_map/pallas_call | solution.py:298
  22.9 0.0 collective-permute-done.7.first_ref
  22.9 2.8 %shard_map.42 = f32[11,1040,128]{2,1,0:T(8,128)} custom-call(bf16[2,1040,1024]{2,1,0:T(8,128)(2,1)S(1)} %get-tuple-element.13.rows_ref, f32[11,128]{1,0:T(8,128)S(1)} %get-tuple-element.14.scale_ref, bf16[2,64,1024]{2,1,0:T(8,128)(2,1)S(1)} %collective-permute-done.7.first_ref, ...), custom_call_target="tpu_custom_call", output_to_operand_aliasing={{}: (5, {})} | custom-call | flops 1090519040 | bytes 2129920 | tf_op jit(solution)/shard_map/pallas_call | solution.py:298
  (5 shorter events, 0.0 us)
Async XLA Ops:
  0.0 15.8 %copy-start = (s32[1,11]{1,0:T(1,128)S(1)}, s32[1,11]{1,0:T(1,128)}, u32[]{:S(2)}) copy-start(s32[1,11]{1,0:T(1,128)} %partners_ref.1) | copy-start | bytes 136
  2.1 8.3 %collective-permute-start.2 = (bf16[64,512]{1,0:T(8,128)(2,1)S(1)}, bf16[64,512]{1,0:T(8,128)(2,1)S(1)}, u32[]{:S(2)}, u32[]{:S(2)}) collective-permute-start(bf16[64,512]{1,0:T(8,128)(2,1)S(1)} %shard_map.37.white_ref), channel_id=1, source_target_pairs={{0,18},{1,19},{2,16},{3,17},{4,22},{5,23},{6,20},{7,21},{8,26},{9,... | collective-permute-start | bytes 196616 | tf_op jit(solution)/shard_map/ppermute | solution.py:330
  2.4 8.1 %collective-permute-start.1 = (bf16[64,512]{1,0:T(8,128)(2,1)S(1)}, bf16[64,512]{1,0:T(8,128)(2,1)S(1)}, u32[]{:S(2)}, u32[]{:S(2)}) collective-permute-start(bf16[64,512]{1,0:T(8,128)(2,1)S(1)} %shard_map.37.white_ref), channel_id=1, source_target_pairs={{0,2},{1,3},{2,0},{3,1},{4,6},{5,7},{6,4},{7,5},{8,10},{9,11},{10,... | collective-permute-start | bytes 196616 | tf_op jit(solution)/shard_map/ppermute | solution.py:328
  3.6 6.9 %collective-permute-start = (bf16[64,512]{1,0:T(8,128)(2,1)S(1)}, bf16[64,512]{1,0:T(8,128)(2,1)S(1)}, u32[]{:S(2)}, u32[]{:S(2)}) collective-permute-start(bf16[64,512]{1,0:T(8,128)(2,1)S(1)} %shard_map.37.white_ref), channel_id=1, source_target_pairs={{0,16},{16,0},{1,17},{17,1},{2,18},{18,2},{3,19},{19,3},{4,20},{20... | collective-permute-start | bytes 196616 | tf_op jit(solution)/shard_map/ppermute | solution.py:327
  4.8 8.2 %collective-permute-start.3 = (bf16[64,512]{1,0:T(8,128)(2,1)S(1)}, bf16[64,512]{1,0:T(8,128)(2,1)S(1)}, u32[]{:S(2)}, u32[]{:S(2)}) collective-permute-start(bf16[64,512]{1,0:T(8,128)(2,1)S(1)} %shard_map.37.white_ref), channel_id=1, source_target_pairs={{3,8},{7,12},{8,3},{12,7},{19,24},{23,28},{24,19},{28,23}} | collective-permute-start | bytes 196616 | tf_op jit(solution)/shard_map/ppermute | solution.py:326
  10.5 9.3 %collective-permute-start.5 = (bf16[2,64,1024]{2,1,0:T(8,128)(2,1)S(1)}, bf16[2,64,1024]{2,1,0:T(8,128)(2,1)S(1)}, u32[]{:S(2)}, u32[]{:S(2)}) collective-permute-start(bf16[2,64,1024]{2,1,0:T(8,128)(2,1)S(1)} %shard_map.38.pair_ref.own_ref), channel_id=1, source_target_pairs={{0,4},{1,5},{2,6},{3,7},{4,0},{5,1},{6,2},{7,3},{8,12},{9,13},{10,... | collective-permute-start | bytes 786440 | tf_op jit(solution)/shard_map/ppermute | solution.py:333
  10.7 10.1 %collective-permute-start.4 = (bf16[2,64,1024]{2,1,0:T(8,128)(2,1)S(1)}, bf16[2,64,1024]{2,1,0:T(8,128)(2,1)S(1)}, u32[]{:S(2)}, u32[]{:S(2)}) collective-permute-start(bf16[2,64,1024]{2,1,0:T(8,128)(2,1)S(1)} %shard_map.38.pair_ref.own_ref), channel_id=1, source_target_pairs={{4,8},{5,9},{6,10},{7,11},{8,4},{9,5},{10,6},{11,7},{20,24},{21,25... | collective-permute-start | bytes 786440 | tf_op jit(solution)/shard_map/ppermute | solution.py:332
  13.0 8.4 %collective-permute-start.9 = (bf16[64,512]{1,0:T(8,128)(2,1)S(1)}, bf16[64,512]{1,0:T(8,128)(2,1)S(1)}, u32[]{:S(2)}, u32[]{:S(2)}) collective-permute-start(bf16[64,512]{1,0:T(8,128)(2,1)S(1)} %collective-permute-done.3), channel_id=1, source_target_pairs={{0,16},{16,0},{1,17},{17,1},{2,18},{18,2},{3,19},{19,3},{4,20},{20... | collective-permute-start | bytes 196616 | tf_op jit(solution)/shard_map/ppermute | solution.py:335
  13.4 4.0 %collective-permute-start.6 = (bf16[2,64,1024]{2,1,0:T(8,128)(2,1)S(1)}, bf16[2,64,1024]{2,1,0:T(8,128)(2,1)S(1)}, u32[]{:S(2)}, u32[]{:S(2)}) collective-permute-start(bf16[2,64,1024]{2,1,0:T(8,128)(2,1)S(1)} %shard_map.38.pair_ref.own_ref), channel_id=1, source_target_pairs={{0,1},{1,0},{2,3},{3,2},{4,5},{5,4},{6,7},{7,6},{8,9},{9,8},{10,11... | collective-permute-start | bytes 786440 | tf_op jit(solution)/shard_map/ppermute | solution.py:336
  20.9 2.1 %collective-permute-start.7 = (bf16[2,64,1024]{2,1,0:T(8,128)(2,1)S(1)}, bf16[2,64,1024]{2,1,0:T(8,128)(2,1)S(1)}, u32[]{:S(2)}, u32[]{:S(2)}) collective-permute-start(bf16[2,64,1024]{2,1,0:T(8,128)(2,1)S(1)} %collective-permute-done.4.first_ref), channel_id=1, source_target_pairs={{0,1},{1,0},{2,3},{3,2},{4,5},{5,4},{6,7},{7,6},{8,9},{9,8},{10,11... | collective-permute-start | bytes 786440 | tf_op jit(solution)/shard_map/ppermute | solution.py:341
  21.3 1.6 %collective-permute-start.8 = (bf16[2,64,1024]{2,1,0:T(8,128)(2,1)S(1)}, bf16[2,64,1024]{2,1,0:T(8,128)(2,1)S(1)}, u32[]{:S(2)}, u32[]{:S(2)}) collective-permute-start(bf16[2,64,1024]{2,1,0:T(8,128)(2,1)S(1)} %collective-permute-done.5.second_ref), channel_id=1, source_target_pairs={{0,1},{1,0},{2,3},{3,2},{4,5},{5,4},{6,7},{7,6},{8,9},{9,8},{10,11... | collective-permute-start | bytes 786440 | tf_op jit(solution)/shard_map/ppermute | solution.py:342

commit v7 on v6

--- a/solution.py
+++ b/solution.py
@@ -167,29 +167,32 @@
 
 
 class Sender:
-    def __init__(self, tiles, slots, out_ref, sems, checked):
-        self.tiles, self.slots, self.out_ref, self.sems, self.checked = tiles, slots, out_ref, sems, checked
+    def __init__(self, tiles, slots, out_ref, sems, last=None):
+        self.tiles, self.slots, self.out_ref, self.sems, self.last = tiles, slots, out_ref, sems, last
+        self.steady = len(slots) if last is None else len(slots) - 1
         self.sent = []
 
-    def act(self, slot, action):
-        if self.checked:
-            pl.when((slot >= 0) & (slot <= 2 * REACH))(action)
-        else:
-            action()
+    def copy(self, number, n, low, high):
+        return pltpu.make_async_copy(
+            self.tiles.at[n, low:high],
+            self.out_ref.at[self.slots[n], low:high],
+            self.sems.at[number * len(self.slots) + n],
+        )
 
     def send(self, number, low, high):
-        for n, slot in enumerate(self.slots):
-            copy = pltpu.make_async_copy(
-                self.tiles.at[n, low:high],
-                self.out_ref.at[slot, low:high],
-                self.sems.at[number * len(self.slots) + n],
-            )
-            self.sent.append((slot, copy))
-            self.act(slot, copy.start)
+        for n in range(self.steady):
+            copy = self.copy(number, n, low, high)
+            self.sent.append(copy)
+            copy.start()
+
+    def send_last(self):
+        pl.when(self.last)(self.copy(0, self.steady, 0, self.tiles.shape[1]).start)
 
     def wait(self):
-        for slot, copy in self.sent:
-            self.act(slot, copy.wait)
+        for copy in self.sent:
+            copy.wait()
+        if self.last is not None:
+            pl.when(self.last)(self.copy(0, self.steady, 0, self.tiles.shape[1]).wait)
 
 
 def slot_of(plane, swap_x, swap_core):
@@ -208,7 +211,7 @@
             window[n * width : (n + 1) * width] = ref[x]
             slots.append(slot_of(0, x, core))
     scale = [scale_ref[pl.ds(slot, 1), :] for slot in slots]
-    sender = Sender(tiles, slots, out_ref, sems, False)
+    sender = Sender(tiles, slots, out_ref, sems)
     multiply(rows_ref, window, scale, tiles, sender.send)
     sender.wait()
 
@@ -217,46 +220,54 @@
     chan = lax.axis_index("chan")
     place = lax.rem(chan, QUAD)
     ahead = 2 * lax.rem(lax.div(chan, QUAD), 2) - 1
-    slots, stands = [], []
-    for plane in (ahead, -ahead):
-        for x in range(2):
-            slot = slot_of(plane, x, core)
-            low = (place == 0) & (plane == 1)
-            high = (place == QUAD - 1) & (plane == -1)
-            if core == 0 and x == 1:
-                stands.append((len(slots), low | high))
-                slot = jnp.where(low, 0, jnp.where(high, 2 * REACH, slot))
-            slots.append(slot)
-    return slots, stands
+    side = 1 - 2 * lax.div(place, 2)
+    at_end = (place == 0) | (place == QUAD - 1)
+    slots = [slot_of(ahead, 0, core), slot_of(-ahead, 0, core), slot_of(-side, 1, core)]
+    if core == 0:
+        slots.append(jnp.where(place == 0, 0, 2 * REACH))
+        return slots, at_end
+    slots.append(jnp.clip(slot_of(side, 1, core), 0, 2 * REACH))
+    return slots, jnp.logical_not(at_end)
+
+
+def load_far(first_ref, second_ref, window):
+    chan = lax.axis_index("chan")
+    width = first_ref.shape[1]
+    ahead = 2 * lax.rem(lax.div(chan, QUAD), 2) - 1
+    side = 1 - 2 * lax.div(lax.rem(chan, QUAD), 2)
+    place = jnp.where(ahead == side, 3, 2)
+    window[:width] = first_ref[0]
+    window[width : 2 * width] = second_ref[0]
+    window[pl.ds(pl.multiple_of(place * width, width), width), :] = first_ref[1]
+    window[pl.ds(pl.multiple_of((5 - place) * width, width), width), :] = second_ref[1]
 
 
 def own_kernel(rows_ref, scale_ref, first_ref, second_ref, corner_ref, tiles_ref, window):
     width = first_ref.shape[1]
-    slots, stands = far_slots(0)
-    for n in range(QUAD):
-        window[n * width : (n + 1) * width] = (first_ref, second_ref)[n // 2][n % 2]
-    for n, stand in stands:
-
-        @pl.when(stand)
-        def _():
-            window[n * width : (n + 1) * width] = corner_ref[...]
-
-    scale = [scale_ref[pl.ds(jnp.clip(slot, 0, 2 * REACH), 1), :] for slot in slots]
+    slots, last = far_slots(0)
+    load_far(first_ref, second_ref, window)
+
+    @pl.when(last)
+    def _():
+        window[3 * width :] = corner_ref[...]
+
+    scale = [scale_ref[pl.ds(slot, 1), :] for slot in slots]
     multiply(rows_ref, window, scale, tiles_ref, lambda *stretch: None)
 
 
 def sibling_kernel(rows_ref, scale_ref, first_ref, second_ref, own_tiles_ref, near_ref, out_ref, window, tiles, sems,
                    own_sems):
     del near_ref
-    width = first_ref.shape[1]
-    own_sender = Sender(own_tiles_ref, far_slots(0)[0], out_ref, own_sems, True)
+    own_slots, own_last = far_slots(0)
+    own_sender = Sender(own_tiles_ref, own_slots, out_ref, own_sems, own_last)
     own_sender.send(0, 0, own_tiles_ref.shape[1])
-    slots, _ = far_slots(1)
-    for n in range(QUAD):
-        window[n * width : (n + 1) * width] = (first_ref, second_ref)[n // 2][n % 2]
-    scale = [scale_ref[pl.ds(jnp.clip(slot, 0, 2 * REACH), 1), :] for slot in slots]
-    sender = Sender(tiles, slots, out_ref, sems, True)
+    own_sender.send_last()
+    slots, last = far_slots(1)
+    load_far(first_ref, second_ref, window)
+    scale = [scale_ref[pl.ds(slot, 1), :] for slot in slots]
+    sender = Sender(tiles, slots, out_ref, sems, last)
     multiply(rows_ref, window, scale, tiles, sender.send)
+    sender.send_last()
     own_sender.wait()
     sender.wait()
 

time: 25.9 us -> 25.5 us (0.985)
  Pallas kernels: 10.4 us -> 9.93 us
    pallas_call x3, Pallas kernels: 6.73 us -> 6.27 us  [correlate(): pl.pallas_call(kernel, out_shape=jax.ShapeDtypeStruct((QUAD if tiles_only...]
  transfers between devices with their start and end apart: 10 -> 10, of which waited for: 2 -> 2; matrix products, arithmetic and copies ran while one was open for 0% -> 0% of each run, Pallas kernels for 21% -> 22%
where the time goes in v7:
time: 25.5 us; the launch traced here: 25.3 us
  starting transfers between devices  13.8 us (54%)
  Pallas kernels  9.93 us (39%)
  waiting for transfers between devices  1.47 us (6%)
    pallas_call x3, Pallas kernels, correlate(): pl.pallas_call(kernel, out_shape=jax.ShapeDtypeStruct((QUAD if tiles_only...  6.27 us
    ppermute x1, starting transfers between devices, local(): corner = lax.ppermute(white, 'chan', corners)  5.58 us
    ppermute x1, starting transfers between devices, local(): beside = lax.ppermute(near, 'chan', sibling)  2.41 us
    pallas_call x1, Pallas kernels, spectra(): pl.pallas_call(functools.partial(spectrum_kernel, step), out_shape=jax.Sh...  2.11 us
    ppermute x1, starting transfers between devices, local(): first = lax.ppermute(quad, 'chan', plane_one)  1.91 us
    pallas_call x1, Pallas kernels, lag_rows(): pl.pallas_call(functools.partial(rows_kernel, samples, norm_scale), out_s...  1.53 us
    ppermute x1, starting transfers between devices, local(): other = lax.ppermute(white, 'seg', [(0, 1), (1, 0)])  1.24 us
    ppermute x1, starting transfers between devices, local(): across = lax.ppermute(white, 'chan', [(c, c ^ 2) for c in range(blocks)])  1.21 us
  transfers between devices with their start and end apart: 10, of which 2 were waited for; matrix products, arithmetic and copies ran while one was open for 0% of the time, Pallas kernels for 22%

profile of v7, /device:TPU:15, one launch (start us, length us, event | category | flops | bytes accessed | tf_op | source)
XLA Modules:
  0.0 25.3 jit_solution(8671720997068251549)
XLA Ops:
  0.0 2.1 %shard_map.37.white_ref = bf16[64,512]{1,0:T(8,128)(2,1)S(1)} custom-call(bf16[64,4096]{1,0:T(8,128)(2,1)} %bitcast.2, bf16[2,256,512]{2,1,0:T(8,128)(2,1)} %constant.2.clone.table_hbm), custom_call_target="tpu_custom_call" | custom-call | flops 1000000000 | bytes 1048576 | tf_op jit(solution)/shard_map/pallas_call | solution.py:81
  2.1 0.3 %collective-permute-start.2 = (bf16[64,512]{1,0:T(8,128)(2,1)S(1)}, bf16[64,512]{1,0:T(8,128)(2,1)S(1)}, u32[]{:S(2)}, u32[]{:S(2)}) collective-permute-start(bf16[64,512]{1,0:T(8,128)(2,1)S(1)} %shard_map.37.white_ref), channel_id=1, source_target_pairs={{0,18},{1,19},{2,16},{3,17},{4,22},{5,23},{6,20},{7,21},{8,26},{9,... | collective-permute-start | bytes 196616 | tf_op jit(solution)/shard_map/ppermute | solution.py:341
  2.4 1.2 %collective-permute-start.1 = (bf16[64,512]{1,0:T(8,128)(2,1)S(1)}, bf16[64,512]{1,0:T(8,128)(2,1)S(1)}, u32[]{:S(2)}, u32[]{:S(2)}) collective-permute-start(bf16[64,512]{1,0:T(8,128)(2,1)S(1)} %shard_map.37.white_ref), channel_id=1, source_target_pairs={{0,2},{1,3},{2,0},{3,1},{4,6},{5,7},{6,4},{7,5},{8,10},{9,11},{10,... | collective-permute-start | bytes 196616 | tf_op jit(solution)/shard_map/ppermute | solution.py:339
  3.6 1.2 %collective-permute-start = (bf16[64,512]{1,0:T(8,128)(2,1)S(1)}, bf16[64,512]{1,0:T(8,128)(2,1)S(1)}, u32[]{:S(2)}, u32[]{:S(2)}) collective-permute-start(bf16[64,512]{1,0:T(8,128)(2,1)S(1)} %shard_map.37.white_ref), channel_id=1, source_target_pairs={{0,16},{16,0},{1,17},{17,1},{2,18},{18,2},{3,19},{19,3},{4,20},{20... | collective-permute-start | bytes 196616 | tf_op jit(solution)/shard_map/ppermute | solution.py:338
  4.8 5.6 %collective-permute-start.3 = (bf16[64,512]{1,0:T(8,128)(2,1)S(1)}, bf16[64,512]{1,0:T(8,128)(2,1)S(1)}, u32[]{:S(2)}, u32[]{:S(2)}) collective-permute-start(bf16[64,512]{1,0:T(8,128)(2,1)S(1)} %shard_map.37.white_ref), channel_id=1, source_target_pairs={{3,8},{7,12},{8,3},{12,7},{19,24},{23,28},{24,19},{28,23}} | collective-permute-start | bytes 196616 | tf_op jit(solution)/shard_map/ppermute | solution.py:337
  10.4 0.0 collective-permute-done.2.diagonal_ref
  10.4 0.0 collective-permute-done.1.across_ref
  10.4 0.0 collective-permute-done.other_ref
  10.5 0.2 collective-permute-start.5
  10.7 1.9 %collective-permute-start.4 = (bf16[2,64,1024]{2,1,0:T(8,128)(2,1)S(1)}, bf16[2,64,1024]{2,1,0:T(8,128)(2,1)S(1)}, u32[]{:S(2)}, u32[]{:S(2)}) collective-permute-start(bf16[2,64,1024]{2,1,0:T(8,128)(2,1)S(1)} %shard_map.38.pair_ref.own_ref), channel_id=1, source_target_pairs={{4,8},{5,9},{6,10},{7,11},{8,4},{9,5},{10,6},{11,7},{20,24},{21,25... | collective-permute-start | bytes 786440 | tf_op jit(solution)/shard_map/ppermute | solution.py:343
  12.6 0.4 %collective-permute-done.3 = bf16[64,512]{1,0:T(8,128)(2,1)S(1)} collective-permute-done((bf16[64,512]{1,0:T(8,128)(2,1)S(1)}, bf16[64,512]{1,0:T(8,128)(2,1)S(1)}, u32[]{:S(2)}, u32[]{:S(2)}) %collective-permute-start.3) | collective-permute-done | bytes 65568 | tf_op jit(solution)/shard_map/ppermute | solution.py:337
  13.0 0.4 %collective-permute-start.9 = (bf16[64,512]{1,0:T(8,128)(2,1)S(1)}, bf16[64,512]{1,0:T(8,128)(2,1)S(1)}, u32[]{:S(2)}, u32[]{:S(2)}) collective-permute-start(bf16[64,512]{1,0:T(8,128)(2,1)S(1)} %collective-permute-done.3), channel_id=1, source_target_pairs={{0,16},{16,0},{1,17},{17,1},{2,18},{18,2},{3,19},{19,3},{4,20},{20... | collective-permute-start | bytes 196616 | tf_op jit(solution)/shard_map/ppermute | solution.py:346
  13.4 2.4 %collective-permute-start.6 = (bf16[2,64,1024]{2,1,0:T(8,128)(2,1)S(1)}, bf16[2,64,1024]{2,1,0:T(8,128)(2,1)S(1)}, u32[]{:S(2)}, u32[]{:S(2)}) collective-permute-start(bf16[2,64,1024]{2,1,0:T(8,128)(2,1)S(1)} %shard_map.38.pair_ref.own_ref), channel_id=1, source_target_pairs={{0,1},{1,0},{2,3},{3,2},{4,5},{5,4},{6,7},{7,6},{8,9},{9,8},{10,11... | collective-permute-start | bytes 786440 | tf_op jit(solution)/shard_map/ppermute | solution.py:347
  15.8 1.5 %shard_map.39 = (bf16[2,1040,1024]{2,1,0:T(8,128)(2,1)S(1)}, f32[11,128]{1,0:T(8,128)S(1)}) custom-call(bf16[2,64,1024]{2,1,0:T(8,128)(2,1)S(1)} %shard_map.38.pair_ref.own_ref, s32[1,11]{1,0:T(1,128)S(1)} %copy-done), custom_call_target="tpu_custom_call" | custom-call | flops 5000000000 | bytes 1048576 | tf_op jit(solution)/shard_map/pallas_call | solution.py:278
  17.4 0.0 collective-permute-done.6.sibling_ref
  17.4 2.4 %shard_map.40.near_ref = f32[11,1040,128]{2,1,0:T(8,128)} custom-call(bf16[2,1040,1024]{2,1,0:T(8,128)(2,1)S(1)} %get-tuple-element.13.rows_ref, f32[11,128]{1,0:T(8,128)S(1)} %get-tuple-element.14.scale_ref, bf16[2,64,1024]{2,1,0:T(8,128)(2,1)S(1)} %shard_map.38.pair_ref.own_ref, bf16[2,64,1024]{2,1,0:T(8,128)(2,1)S(1)} %collective-permute-done.6.sibling_ref), custom_call_target="tpu_custom_call" | custom-call | flops 1090519040 | bytes 2129920 | tf_op jit(solution)/shard_map/pallas_call | solution.py:309
  19.8 0.0 collective-permute-done.5.second_ref
  19.8 1.1 %collective-permute-done.4.first_ref = bf16[2,64,1024]{2,1,0:T(8,128)(2,1)S(1)} collective-permute-done((bf16[2,64,1024]{2,1,0:T(8,128)(2,1)S(1)}, bf16[2,64,1024]{2,1,0:T(8,128)(2,1)S(1)}, u32[]{:S(2)}, u32[]{:S(2)}) %collective-permute-start.4) | collective-permute-done | bytes 262176 | tf_op jit(solution)/shard_map/ppermute | solution.py:343
  20.9 0.5 %collective-permute-start.7 = (bf16[2,64,1024]{2,1,0:T(8,128)(2,1)S(1)}, bf16[2,64,1024]{2,1,0:T(8,128)(2,1)S(1)}, u32[]{:S(2)}, u32[]{:S(2)}) collective-permute-start(bf16[2,64,1024]{2,1,0:T(8,128)(2,1)S(1)} %collective-permute-done.4.first_ref), channel_id=1, source_target_pairs={{0,1},{1,0},{2,3},{3,2},{4,5},{5,4},{6,7},{7,6},{8,9},{9,8},{10,11... | collective-permute-start | bytes 786440 | tf_op jit(solution)/shard_map/ppermute | solution.py:352
  21.3 0.0 collective-permute-start.8
  21.4 1.5 %shard_map.41.own_tiles_ref = f32[4,1040,128]{2,1,0:T(8,128)S(1)} custom-call(bf16[2,1040,1024]{2,1,0:T(8,128)(2,1)S(1)} %get-tuple-element.13.rows_ref, f32[11,128]{1,0:T(8,128)S(1)} %get-tuple-element.14.scale_ref, bf16[2,64,1024]{2,1,0:T(8,128)(2,1)S(1)} %collective-permute-done.4.first_ref, bf16[2,64,1024]{2,1,0:T(8,128)(2,1)S(1)} %collective-permute-done.5.second_ref, ...), custom_call_target="tpu_custom_call" | custom-call | flops 1090519040 | bytes 2129920 | tf_op jit(solution)/shard_map/pallas_call | solution.py:309
  22.9 0.0 collective-permute-done.7.first_ref
  22.9 0.0 collective-permute-done.8.second_ref
  23.0 2.4 %shard_map.42 = f32[11,1040,128]{2,1,0:T(8,128)} custom-call(bf16[2,1040,1024]{2,1,0:T(8,128)(2,1)S(1)} %get-tuple-element.13.rows_ref, f32[11,128]{1,0:T(8,128)S(1)} %get-tuple-element.14.scale_ref, bf16[2,64,1024]{2,1,0:T(8,128)(2,1)S(1)} %collective-permute-done.7.first_ref, ...), custom_call_target="tpu_custom_call", output_to_operand_aliasing={{}: (5, {})} | custom-call | flops 1090519040 | bytes 2129920 | tf_op jit(solution)/shard_map/pallas_call | solution.py:309
  (5 shorter events, 0.0 us)
Async XLA Ops:
  0.0 15.8 %copy-start = (s32[1,11]{1,0:T(1,128)S(1)}, s32[1,11]{1,0:T(1,128)}, u32[]{:S(2)}) copy-start(s32[1,11]{1,0:T(1,128)} %partners_ref.1) | copy-start | bytes 136
  2.1 8.3 %collective-permute-start.2 = (bf16[64,512]{1,0:T(8,128)(2,1)S(1)}, bf16[64,512]{1,0:T(8,128)(2,1)S(1)}, u32[]{:S(2)}, u32[]{:S(2)}) collective-permute-start(bf16[64,512]{1,0:T(8,128)(2,1)S(1)} %shard_map.37.white_ref), channel_id=1, source_target_pairs={{0,18},{1,19},{2,16},{3,17},{4,22},{5,23},{6,20},{7,21},{8,26},{9,... | collective-permute-start | bytes 196616 | tf_op jit(solution)/shard_map/ppermute | solution.py:341
  2.4 8.1 %collective-permute-start.1 = (bf16[64,512]{1,0:T(8,128)(2,1)S(1)}, bf16[64,512]{1,0:T(8,128)(2,1)S(1)}, u32[]{:S(2)}, u32[]{:S(2)}) collective-permute-start(bf16[64,512]{1,0:T(8,128)(2,1)S(1)} %shard_map.37.white_ref), channel_id=1, source_target_pairs={{0,2},{1,3},{2,0},{3,1},{4,6},{5,7},{6,4},{7,5},{8,10},{9,11},{10,... | collective-permute-start | bytes 196616 | tf_op jit(solution)/shard_map/ppermute | solution.py:339
  3.6 6.9 %collective-permute-start = (bf16[64,512]{1,0:T(8,128)(2,1)S(1)}, bf16[64,512]{1,0:T(8,128)(2,1)S(1)}, u32[]{:S(2)}, u32[]{:S(2)}) collective-permute-start(bf16[64,512]{1,0:T(8,128)(2,1)S(1)} %shard_map.37.white_ref), channel_id=1, source_target_pairs={{0,16},{16,0},{1,17},{17,1},{2,18},{18,2},{3,19},{19,3},{4,20},{20... | collective-permute-start | bytes 196616 | tf_op jit(solution)/shard_map/ppermute | solution.py:338
  4.8 8.2 %collective-permute-start.3 = (bf16[64,512]{1,0:T(8,128)(2,1)S(1)}, bf16[64,512]{1,0:T(8,128)(2,1)S(1)}, u32[]{:S(2)}, u32[]{:S(2)}) collective-permute-start(bf16[64,512]{1,0:T(8,128)(2,1)S(1)} %shard_map.37.white_ref), channel_id=1, source_target_pairs={{3,8},{7,12},{8,3},{12,7},{19,24},{23,28},{24,19},{28,23}} | collective-permute-start | bytes 196616 | tf_op jit(solution)/shard_map/ppermute | solution.py:337
  10.5 9.3 %collective-permute-start.5 = (bf16[2,64,1024]{2,1,0:T(8,128)(2,1)S(1)}, bf16[2,64,1024]{2,1,0:T(8,128)(2,1)S(1)}, u32[]{:S(2)}, u32[]{:S(2)}) collective-permute-start(bf16[2,64,1024]{2,1,0:T(8,128)(2,1)S(1)} %shard_map.38.pair_ref.own_ref), channel_id=1, source_target_pairs={{0,4},{1,5},{2,6},{3,7},{4,0},{5,1},{6,2},{7,3},{8,12},{9,13},{10,... | collective-permute-start | bytes 786440 | tf_op jit(solution)/shard_map/ppermute | solution.py:344
  10.7 10.1 %collective-permute-start.4 = (bf16[2,64,1024]{2,1,0:T(8,128)(2,1)S(1)}, bf16[2,64,1024]{2,1,0:T(8,128)(2,1)S(1)}, u32[]{:S(2)}, u32[]{:S(2)}) collective-permute-start(bf16[2,64,1024]{2,1,0:T(8,128)(2,1)S(1)} %shard_map.38.pair_ref.own_ref), channel_id=1, source_target_pairs={{4,8},{5,9},{6,10},{7,11},{8,4},{9,5},{10,6},{11,7},{20,24},{21,25... | collective-permute-start | bytes 786440 | tf_op jit(solution)/shard_map/ppermute | solution.py:343
  13.0 8.4 %collective-permute-start.9 = (bf16[64,512]{1,0:T(8,128)(2,1)S(1)}, bf16[64,512]{1,0:T(8,128)(2,1)S(1)}, u32[]{:S(2)}, u32[]{:S(2)}) collective-permute-start(bf16[64,512]{1,0:T(8,128)(2,1)S(1)} %collective-permute-done.3), channel_id=1, source_target_pairs={{0,16},{16,0},{1,17},{17,1},{2,18},{18,2},{3,19},{19,3},{4,20},{20... | collective-permute-start | bytes 196616 | tf_op jit(solution)/shard_map/ppermute | solution.py:346
  13.4 4.0 %collective-permute-start.6 = (bf16[2,64,1024]{2,1,0:T(8,128)(2,1)S(1)}, bf16[2,64,1024]{2,1,0:T(8,128)(2,1)S(1)}, u32[]{:S(2)}, u32[]{:S(2)}) collective-permute-start(bf16[2,64,1024]{2,1,0:T(8,128)(2,1)S(1)} %shard_map.38.pair_ref.own_ref), channel_id=1, source_target_pairs={{0,1},{1,0},{2,3},{3,2},{4,5},{5,4},{6,7},{7,6},{8,9},{9,8},{10,11... | collective-permute-start | bytes 786440 | tf_op jit(solution)/shard_map/ppermute | solution.py:347
  20.9 2.1 %collective-permute-start.7 = (bf16[2,64,1024]{2,1,0:T(8,128)(2,1)S(1)}, bf16[2,64,1024]{2,1,0:T(8,128)(2,1)S(1)}, u32[]{:S(2)}, u32[]{:S(2)}) collective-permute-start(bf16[2,64,1024]{2,1,0:T(8,128)(2,1)S(1)} %collective-permute-done.4.first_ref), channel_id=1, source_target_pairs={{0,1},{1,0},{2,3},{3,2},{4,5},{5,4},{6,7},{7,6},{8,9},{9,8},{10,11... | collective-permute-start | bytes 786440 | tf_op jit(solution)/shard_map/ppermute | solution.py:352
  21.3 1.6 %collective-permute-start.8 = (bf16[2,64,1024]{2,1,0:T(8,128)(2,1)S(1)}, bf16[2,64,1024]{2,1,0:T(8,128)(2,1)S(1)}, u32[]{:S(2)}, u32[]{:S(2)}) collective-permute-start(bf16[2,64,1024]{2,1,0:T(8,128)(2,1)S(1)} %collective-permute-done.5.second_ref), channel_id=1, source_target_pairs={{0,1},{1,0},{2,3},{3,2},{4,5},{5,4},{6,7},{7,6},{8,9},{9,8},{10,11... | collective-permute-start | bytes 786440 | tf_op jit(solution)/shard_map/ppermute | solution.py:353

commit v8 on v7

--- a/solution.py
+++ b/solution.py
@@ -167,32 +167,23 @@
 
 
 class Sender:
-    def __init__(self, tiles, slots, out_ref, sems, last=None):
-        self.tiles, self.slots, self.out_ref, self.sems, self.last = tiles, slots, out_ref, sems, last
-        self.steady = len(slots) if last is None else len(slots) - 1
+    def __init__(self, tiles, slots, out_ref, sems):
+        self.tiles, self.slots, self.out_ref, self.sems = tiles, slots, out_ref, sems
         self.sent = []
 
-    def copy(self, number, n, low, high):
-        return pltpu.make_async_copy(
-            self.tiles.at[n, low:high],
-            self.out_ref.at[self.slots[n], low:high],
-            self.sems.at[number * len(self.slots) + n],
-        )
-
     def send(self, number, low, high):
-        for n in range(self.steady):
-            copy = self.copy(number, n, low, high)
+        for n, slot in enumerate(self.slots):
+            copy = pltpu.make_async_copy(
+                self.tiles.at[n, low:high],
+                self.out_ref.at[slot, low:high],
+                self.sems.at[number * len(self.slots) + n],
+            )
             self.sent.append(copy)
             copy.start()
-
-    def send_last(self):
-        pl.when(self.last)(self.copy(0, self.steady, 0, self.tiles.shape[1]).start)
 
     def wait(self):
         for copy in self.sent:
             copy.wait()
-        if self.last is not None:
-            pl.when(self.last)(self.copy(0, self.steady, 0, self.tiles.shape[1]).wait)
 
 
 def slot_of(plane, swap_x, swap_core):
@@ -221,13 +212,11 @@
     place = lax.rem(chan, QUAD)
     ahead = 2 * lax.rem(lax.div(chan, QUAD), 2) - 1
     side = 1 - 2 * lax.div(place, 2)
-    at_end = (place == 0) | (place == QUAD - 1)
-    slots = [slot_of(ahead, 0, core), slot_of(-ahead, 0, core), slot_of(-side, 1, core)]
-    if core == 0:
-        slots.append(jnp.where(place == 0, 0, 2 * REACH))
-        return slots, at_end
-    slots.append(jnp.clip(slot_of(side, 1, core), 0, 2 * REACH))
-    return slots, jnp.logical_not(at_end)
+    last = jnp.clip(slot_of(side, 1, core), 0, 2 * REACH)
+    if core == 1:
+        last = jnp.where(place == 0, 0, jnp.where(place == QUAD - 1, 2 * REACH, last))
+    slots = [slot_of(ahead, 0, core), slot_of(-ahead, 0, core), slot_of(-side, 1, core), last]
+    return slots, (place == 0) | (place == QUAD - 1)
 
 
 def load_far(first_ref, second_ref, window):
@@ -242,32 +231,28 @@
     window[pl.ds(pl.multiple_of((5 - place) * width, width), width), :] = second_ref[1]
 
 
-def own_kernel(rows_ref, scale_ref, first_ref, second_ref, corner_ref, tiles_ref, window):
-    width = first_ref.shape[1]
-    slots, last = far_slots(0)
+def own_kernel(rows_ref, scale_ref, first_ref, second_ref, tiles_ref, window):
+    slots, _ = far_slots(0)
     load_far(first_ref, second_ref, window)
-
-    @pl.when(last)
-    def _():
-        window[3 * width :] = corner_ref[...]
-
     scale = [scale_ref[pl.ds(slot, 1), :] for slot in slots]
     multiply(rows_ref, window, scale, tiles_ref, lambda *stretch: None)
 
 
-def sibling_kernel(rows_ref, scale_ref, first_ref, second_ref, own_tiles_ref, near_ref, out_ref, window, tiles, sems,
-                   own_sems):
+def sibling_kernel(rows_ref, scale_ref, first_ref, second_ref, corner_ref, own_tiles_ref, near_ref, out_ref, window, tiles,
+                   sems, own_sems):
     del near_ref
-    own_slots, own_last = far_slots(0)
-    own_sender = Sender(own_tiles_ref, own_slots, out_ref, own_sems, own_last)
+    own_sender = Sender(own_tiles_ref, far_slots(0)[0][:3], out_ref, own_sems)
     own_sender.send(0, 0, own_tiles_ref.shape[1])
-    own_sender.send_last()
-    slots, last = far_slots(1)
+    slots, stands = far_slots(1)
     load_far(first_ref, second_ref, window)
+
+    @pl.when(stands)
+    def _():
+        window[3 * first_ref.shape[1] :] = corner_ref[...]
+
     scale = [scale_ref[pl.ds(slot, 1), :] for slot in slots]
-    sender = Sender(tiles, slots, out_ref, sems, last)
+    sender = Sender(tiles, slots, out_ref, sems)
     multiply(rows_ref, window, scale, tiles, sender.send)
-    sender.send_last()
     own_sender.wait()
     sender.wait()
 
@@ -351,8 +336,8 @@
     first, second, out = lax.optimization_barrier((first, second, out))
     sib_first = lax.ppermute(first, "chan", sibling)
     sib_second = lax.ppermute(second, "chan", sibling)
-    tiles = correlate(own_kernel, [rows, scale, first, second, corner], tiles_only=True)
-    out = correlate(sibling_kernel, [rows, scale, sib_first, sib_second, tiles], out)
+    tiles = correlate(own_kernel, [rows, scale, first, second], tiles_only=True)
+    out = correlate(sibling_kernel, [rows, scale, sib_first, sib_second, corner, tiles], out)
     return out.reshape(1, slots, LAGS, half * channels)
 
 

time: 25.5 us -> 25.5 us (level)
  transfers between devices with their start and end apart: 10 -> 10, of which waited for: 2 -> 2; matrix products, arithmetic and copies ran while one was open for 0% -> 0% of each run, Pallas kernels for 22% -> 21%
where the time goes in v8:
time: 25.5 us; the launch traced here: 25.4 us
  starting transfers between devices  13.8 us (54%)
  Pallas kernels  9.98 us (39%)
  waiting for transfers between devices  1.47 us (6%)
    pallas_call x3, Pallas kernels, correlate(): pl.pallas_call(kernel, out_shape=jax.ShapeDtypeStruct((QUAD if tiles_only...  6.32 us
    ppermute x1, starting transfers between devices, local(): corner = lax.ppermute(white, 'chan', corners)  5.58 us
    ppermute x1, starting transfers between devices, local(): beside = lax.ppermute(near, 'chan', sibling)  2.41 us
    pallas_call x1, Pallas kernels, spectra(): pl.pallas_call(functools.partial(spectrum_kernel, step), out_shape=jax.Sh...  2.11 us
    ppermute x1, starting transfers between devices, local(): first = lax.ppermute(quad, 'chan', plane_one)  1.91 us
    pallas_call x1, Pallas kernels, lag_rows(): pl.pallas_call(functools.partial(rows_kernel, samples, norm_scale), out_s...  1.53 us
    ppermute x1, starting transfers between devices, local(): other = lax.ppermute(white, 'seg', [(0, 1), (1, 0)])  1.24 us
    ppermute x1, starting transfers between devices, local(): across = lax.ppermute(white, 'chan', [(c, c ^ 2) for c in range(blocks)])  1.21 us
  transfers between devices with their start and end apart: 10, of which 2 were waited for; matrix products, arithmetic and copies ran while one was open for 0% of the time, Pallas kernels for 21%

profile of v8, /device:TPU:15, one launch (start us, length us, event | category | flops | bytes accessed | tf_op | source)
XLA Modules:
  0.0 25.4 jit_solution(3899061646765198402)
XLA Ops:
  0.0 2.1 %shard_map.37.white_ref = bf16[64,512]{1,0:T(8,128)(2,1)S(1)} custom-call(bf16[64,4096]{1,0:T(8,128)(2,1)} %bitcast.2, bf16[2,256,512]{2,1,0:T(8,128)(2,1)} %constant.2.clone.table_hbm), custom_call_target="tpu_custom_call" | custom-call | flops 1000000000 | bytes 1048576 | tf_op jit(solution)/shard_map/pallas_call | solution.py:81
  2.1 0.3 %collective-permute-start.2 = (bf16[64,512]{1,0:T(8,128)(2,1)S(1)}, bf16[64,512]{1,0:T(8,128)(2,1)S(1)}, u32[]{:S(2)}, u32[]{:S(2)}) collective-permute-start(bf16[64,512]{1,0:T(8,128)(2,1)S(1)} %shard_map.37.white_ref), channel_id=1, source_target_pairs={{0,18},{1,19},{2,16},{3,17},{4,22},{5,23},{6,20},{7,21},{8,26},{9,... | collective-permute-start | bytes 196616 | tf_op jit(solution)/shard_map/ppermute | solution.py:326
  2.4 1.2 %collective-permute-start.1 = (bf16[64,512]{1,0:T(8,128)(2,1)S(1)}, bf16[64,512]{1,0:T(8,128)(2,1)S(1)}, u32[]{:S(2)}, u32[]{:S(2)}) collective-permute-start(bf16[64,512]{1,0:T(8,128)(2,1)S(1)} %shard_map.37.white_ref), channel_id=1, source_target_pairs={{0,2},{1,3},{2,0},{3,1},{4,6},{5,7},{6,4},{7,5},{8,10},{9,11},{10,... | collective-permute-start | bytes 196616 | tf_op jit(solution)/shard_map/ppermute | solution.py:324
  3.6 1.2 %collective-permute-start = (bf16[64,512]{1,0:T(8,128)(2,1)S(1)}, bf16[64,512]{1,0:T(8,128)(2,1)S(1)}, u32[]{:S(2)}, u32[]{:S(2)}) collective-permute-start(bf16[64,512]{1,0:T(8,128)(2,1)S(1)} %shard_map.37.white_ref), channel_id=1, source_target_pairs={{0,16},{16,0},{1,17},{17,1},{2,18},{18,2},{3,19},{19,3},{4,20},{20... | collective-permute-start | bytes 196616 | tf_op jit(solution)/shard_map/ppermute | solution.py:323
  4.8 5.6 %collective-permute-start.3 = (bf16[64,512]{1,0:T(8,128)(2,1)S(1)}, bf16[64,512]{1,0:T(8,128)(2,1)S(1)}, u32[]{:S(2)}, u32[]{:S(2)}) collective-permute-start(bf16[64,512]{1,0:T(8,128)(2,1)S(1)} %shard_map.37.white_ref), channel_id=1, source_target_pairs={{3,8},{7,12},{8,3},{12,7},{19,24},{23,28},{24,19},{28,23}} | collective-permute-start | bytes 196616 | tf_op jit(solution)/shard_map/ppermute | solution.py:322
  10.4 0.0 collective-permute-done.2.diagonal_ref
  10.4 0.0 collective-permute-done.1.across_ref
  10.4 0.0 collective-permute-done.other_ref
  10.5 0.2 collective-permute-start.5
  10.7 1.9 %collective-permute-start.4 = (bf16[2,64,1024]{2,1,0:T(8,128)(2,1)S(1)}, bf16[2,64,1024]{2,1,0:T(8,128)(2,1)S(1)}, u32[]{:S(2)}, u32[]{:S(2)}) collective-permute-start(bf16[2,64,1024]{2,1,0:T(8,128)(2,1)S(1)} %shard_map.38.pair_ref.own_ref), channel_id=1, source_target_pairs={{4,8},{5,9},{6,10},{7,11},{8,4},{9,5},{10,6},{11,7},{20,24},{21,25... | collective-permute-start | bytes 786440 | tf_op jit(solution)/shard_map/ppermute | solution.py:328
  12.6 0.4 %collective-permute-done.3 = bf16[64,512]{1,0:T(8,128)(2,1)S(1)} collective-permute-done((bf16[64,512]{1,0:T(8,128)(2,1)S(1)}, bf16[64,512]{1,0:T(8,128)(2,1)S(1)}, u32[]{:S(2)}, u32[]{:S(2)}) %collective-permute-start.3) | collective-permute-done | bytes 65568 | tf_op jit(solution)/shard_map/ppermute | solution.py:322
  13.0 0.4 %collective-permute-start.9 = (bf16[64,512]{1,0:T(8,128)(2,1)S(1)}, bf16[64,512]{1,0:T(8,128)(2,1)S(1)}, u32[]{:S(2)}, u32[]{:S(2)}) collective-permute-start(bf16[64,512]{1,0:T(8,128)(2,1)S(1)} %collective-permute-done.3), channel_id=1, source_target_pairs={{0,16},{16,0},{1,17},{17,1},{2,18},{18,2},{3,19},{19,3},{4,20},{20... | collective-permute-start | bytes 196616 | tf_op jit(solution)/shard_map/ppermute | solution.py:331
  13.4 2.4 %collective-permute-start.6 = (bf16[2,64,1024]{2,1,0:T(8,128)(2,1)S(1)}, bf16[2,64,1024]{2,1,0:T(8,128)(2,1)S(1)}, u32[]{:S(2)}, u32[]{:S(2)}) collective-permute-start(bf16[2,64,1024]{2,1,0:T(8,128)(2,1)S(1)} %shard_map.38.pair_ref.own_ref), channel_id=1, source_target_pairs={{0,1},{1,0},{2,3},{3,2},{4,5},{5,4},{6,7},{7,6},{8,9},{9,8},{10,11... | collective-permute-start | bytes 786440 | tf_op jit(solution)/shard_map/ppermute | solution.py:332
  15.8 1.5 %shard_map.39 = (bf16[2,1040,1024]{2,1,0:T(8,128)(2,1)S(1)}, f32[11,128]{1,0:T(8,128)S(1)}) custom-call(bf16[2,64,1024]{2,1,0:T(8,128)(2,1)S(1)} %shard_map.38.pair_ref.own_ref, s32[1,11]{1,0:T(1,128)S(1)} %copy-done), custom_call_target="tpu_custom_call" | custom-call | flops 5000000000 | bytes 1048576 | tf_op jit(solution)/shard_map/pallas_call | solution.py:263
  17.4 0.0 collective-permute-done.6.sibling_ref
  17.4 2.4 %shard_map.40.near_ref = f32[11,1040,128]{2,1,0:T(8,128)} custom-call(bf16[2,1040,1024]{2,1,0:T(8,128)(2,1)S(1)} %get-tuple-element.13.rows_ref, f32[11,128]{1,0:T(8,128)S(1)} %get-tuple-element.14.scale_ref, bf16[2,64,1024]{2,1,0:T(8,128)(2,1)S(1)} %shard_map.38.pair_ref.own_ref, bf16[2,64,1024]{2,1,0:T(8,128)(2,1)S(1)} %collective-permute-done.6.sibling_ref), custom_call_target="tpu_custom_call" | custom-call | flops 1090519040 | bytes 2129920 | tf_op jit(solution)/shard_map/pallas_call | solution.py:294
  19.8 0.0 collective-permute-done.5.second_ref
  19.8 1.1 %collective-permute-done.4.first_ref = bf16[2,64,1024]{2,1,0:T(8,128)(2,1)S(1)} collective-permute-done((bf16[2,64,1024]{2,1,0:T(8,128)(2,1)S(1)}, bf16[2,64,1024]{2,1,0:T(8,128)(2,1)S(1)}, u32[]{:S(2)}, u32[]{:S(2)}) %collective-permute-start.4) | collective-permute-done | bytes 262176 | tf_op jit(solution)/shard_map/ppermute | solution.py:328
  20.9 0.5 %collective-permute-start.7 = (bf16[2,64,1024]{2,1,0:T(8,128)(2,1)S(1)}, bf16[2,64,1024]{2,1,0:T(8,128)(2,1)S(1)}, u32[]{:S(2)}, u32[]{:S(2)}) collective-permute-start(bf16[2,64,1024]{2,1,0:T(8,128)(2,1)S(1)} %collective-permute-done.4.first_ref), channel_id=1, source_target_pairs={{0,1},{1,0},{2,3},{3,2},{4,5},{5,4},{6,7},{7,6},{8,9},{9,8},{10,11... | collective-permute-start | bytes 786440 | tf_op jit(solution)/shard_map/ppermute | solution.py:337
  21.3 0.0 collective-permute-start.8
  21.4 0.0 collective-permute-done.9
  21.4 1.5 %shard_map.41.own_tiles_ref = f32[4,1040,128]{2,1,0:T(8,128)S(1)} custom-call(bf16[2,1040,1024]{2,1,0:T(8,128)(2,1)S(1)} %get-tuple-element.13.rows_ref, f32[11,128]{1,0:T(8,128)S(1)} %get-tuple-element.14.scale_ref, bf16[2,64,1024]{2,1,0:T(8,128)(2,1)S(1)} %collective-permute-done.4.first_ref, bf16[2,64,1024]{2,1,0:T(8,128)(2,1)S(1)} %collective-permute-done.5.second_ref), custom_call_target="tpu_custom_call" | custom-call | flops 1090519040 | bytes 2129920 | tf_op jit(solution)/shard_map/pallas_call | solution.py:294
  22.9 0.0 collective-permute-done.8.second_ref
  22.9 2.5 %shard_map.42 = f32[11,1040,128]{2,1,0:T(8,128)} custom-call(bf16[2,1040,1024]{2,1,0:T(8,128)(2,1)S(1)} %get-tuple-element.13.rows_ref, f32[11,128]{1,0:T(8,128)S(1)} %get-tuple-element.14.scale_ref, bf16[2,64,1024]{2,1,0:T(8,128)(2,1)S(1)} %collective-permute-done.7.first_ref, ...), custom_call_target="tpu_custom_call", output_to_operand_aliasing={{}: (6, {})} | custom-call | flops 1090519040 | bytes 2129920 | tf_op jit(solution)/shard_map/pallas_call | solution.py:294
  (5 shorter events, 0.0 us)
Async XLA Ops:
  0.0 15.8 %copy-start = (s32[1,11]{1,0:T(1,128)S(1)}, s32[1,11]{1,0:T(1,128)}, u32[]{:S(2)}) copy-start(s32[1,11]{1,0:T(1,128)} %partners_ref.1) | copy-start | bytes 136
  2.1 8.3 %collective-permute-start.2 = (bf16[64,512]{1,0:T(8,128)(2,1)S(1)}, bf16[64,512]{1,0:T(8,128)(2,1)S(1)}, u32[]{:S(2)}, u32[]{:S(2)}) collective-permute-start(bf16[64,512]{1,0:T(8,128)(2,1)S(1)} %shard_map.37.white_ref), channel_id=1, source_target_pairs={{0,18},{1,19},{2,16},{3,17},{4,22},{5,23},{6,20},{7,21},{8,26},{9,... | collective-permute-start | bytes 196616 | tf_op jit(solution)/shard_map/ppermute | solution.py:326
  2.4 8.1 %collective-permute-start.1 = (bf16[64,512]{1,0:T(8,128)(2,1)S(1)}, bf16[64,512]{1,0:T(8,128)(2,1)S(1)}, u32[]{:S(2)}, u32[]{:S(2)}) collective-permute-start(bf16[64,512]{1,0:T(8,128)(2,1)S(1)} %shard_map.37.white_ref), channel_id=1, source_target_pairs={{0,2},{1,3},{2,0},{3,1},{4,6},{5,7},{6,4},{7,5},{8,10},{9,11},{10,... | collective-permute-start | bytes 196616 | tf_op jit(solution)/shard_map/ppermute | solution.py:324
  3.6 6.9 %collective-permute-start = (bf16[64,512]{1,0:T(8,128)(2,1)S(1)}, bf16[64,512]{1,0:T(8,128)(2,1)S(1)}, u32[]{:S(2)}, u32[]{:S(2)}) collective-permute-start(bf16[64,512]{1,0:T(8,128)(2,1)S(1)} %shard_map.37.white_ref), channel_id=1, source_target_pairs={{0,16},{16,0},{1,17},{17,1},{2,18},{18,2},{3,19},{19,3},{4,20},{20... | collective-permute-start | bytes 196616 | tf_op jit(solution)/shard_map/ppermute | solution.py:323
  4.8 8.2 %collective-permute-start.3 = (bf16[64,512]{1,0:T(8,128)(2,1)S(1)}, bf16[64,512]{1,0:T(8,128)(2,1)S(1)}, u32[]{:S(2)}, u32[]{:S(2)}) collective-permute-start(bf16[64,512]{1,0:T(8,128)(2,1)S(1)} %shard_map.37.white_ref), channel_id=1, source_target_pairs={{3,8},{7,12},{8,3},{12,7},{19,24},{23,28},{24,19},{28,23}} | collective-permute-start | bytes 196616 | tf_op jit(solution)/shard_map/ppermute | solution.py:322
  10.5 9.3 %collective-permute-start.5 = (bf16[2,64,1024]{2,1,0:T(8,128)(2,1)S(1)}, bf16[2,64,1024]{2,1,0:T(8,128)(2,1)S(1)}, u32[]{:S(2)}, u32[]{:S(2)}) collective-permute-start(bf16[2,64,1024]{2,1,0:T(8,128)(2,1)S(1)} %shard_map.38.pair_ref.own_ref), channel_id=1, source_target_pairs={{0,4},{1,5},{2,6},{3,7},{4,0},{5,1},{6,2},{7,3},{8,12},{9,13},{10,... | collective-permute-start | bytes 786440 | tf_op jit(solution)/shard_map/ppermute | solution.py:329
  10.7 10.1 %collective-permute-start.4 = (bf16[2,64,1024]{2,1,0:T(8,128)(2,1)S(1)}, bf16[2,64,1024]{2,1,0:T(8,128)(2,1)S(1)}, u32[]{:S(2)}, u32[]{:S(2)}) collective-permute-start(bf16[2,64,1024]{2,1,0:T(8,128)(2,1)S(1)} %shard_map.38.pair_ref.own_ref), channel_id=1, source_target_pairs={{4,8},{5,9},{6,10},{7,11},{8,4},{9,5},{10,6},{11,7},{20,24},{21,25... | collective-permute-start | bytes 786440 | tf_op jit(solution)/shard_map/ppermute | solution.py:328
  13.0 8.4 %collective-permute-start.9 = (bf16[64,512]{1,0:T(8,128)(2,1)S(1)}, bf16[64,512]{1,0:T(8,128)(2,1)S(1)}, u32[]{:S(2)}, u32[]{:S(2)}) collective-permute-start(bf16[64,512]{1,0:T(8,128)(2,1)S(1)} %collective-permute-done.3), channel_id=1, source_target_pairs={{0,16},{16,0},{1,17},{17,1},{2,18},{18,2},{3,19},{19,3},{4,20},{20... | collective-permute-start | bytes 196616 | tf_op jit(solution)/shard_map/ppermute | solution.py:331
  13.4 4.0 %collective-permute-start.6 = (bf16[2,64,1024]{2,1,0:T(8,128)(2,1)S(1)}, bf16[2,64,1024]{2,1,0:T(8,128)(2,1)S(1)}, u32[]{:S(2)}, u32[]{:S(2)}) collective-permute-start(bf16[2,64,1024]{2,1,0:T(8,128)(2,1)S(1)} %shard_map.38.pair_ref.own_ref), channel_id=1, source_target_pairs={{0,1},{1,0},{2,3},{3,2},{4,5},{5,4},{6,7},{7,6},{8,9},{9,8},{10,11... | collective-permute-start | bytes 786440 | tf_op jit(solution)/shard_map/ppermute | solution.py:332
  20.9 2.0 %collective-permute-start.7 = (bf16[2,64,1024]{2,1,0:T(8,128)(2,1)S(1)}, bf16[2,64,1024]{2,1,0:T(8,128)(2,1)S(1)}, u32[]{:S(2)}, u32[]{:S(2)}) collective-permute-start(bf16[2,64,1024]{2,1,0:T(8,128)(2,1)S(1)} %collective-permute-done.4.first_ref), channel_id=1, source_target_pairs={{0,1},{1,0},{2,3},{3,2},{4,5},{5,4},{6,7},{7,6},{8,9},{9,8},{10,11... | collective-permute-start | bytes 786440 | tf_op jit(solution)/shard_map/ppermute | solution.py:337
  21.3 1.6 %collective-permute-start.8 = (bf16[2,64,1024]{2,1,0:T(8,128)(2,1)S(1)}, bf16[2,64,1024]{2,1,0:T(8,128)(2,1)S(1)}, u32[]{:S(2)}, u32[]{:S(2)}) collective-permute-start(bf16[2,64,1024]{2,1,0:T(8,128)(2,1)S(1)} %collective-permute-done.5.second_ref), channel_id=1, source_target_pairs={{0,1},{1,0},{2,3},{3,2},{4,5},{5,4},{6,7},{7,6},{8,9},{9,8},{10,11... | collective-permute-start | bytes 786440 | tf_op jit(solution)/shard_map/ppermute | solution.py:338

commit v9 on v8

--- a/solution.py
+++ b/solution.py
@@ -328,9 +328,10 @@
     first = lax.ppermute(quad, "chan", plane_one)
     second = lax.ppermute(quad, "chan", plane_two)
     near, corner = lax.optimization_barrier((quad, corner))
-    corner_other = lax.ppermute(corner, "seg", [(0, 1), (1, 0)])
     beside = lax.ppermute(near, "chan", sibling)
     rows, scale = lag_rows(near, partners, traces.shape[2], half, norm_scale)
+    rows, corner = lax.optimization_barrier((rows, corner))
+    corner_other = lax.ppermute(corner, "seg", [(0, 1), (1, 0)])
     out = correlate(near_kernel, [rows, scale, quad, beside])
     corner = jnp.concatenate([corner, corner_other], axis=1)
     first, second, out = lax.optimization_barrier((first, second, out))

time: 25.5 us -> 25.5 us (level)
    ppermute x1, starting transfers between devices: 2.41 us -> 1.32 us  [local(): beside = lax.ppermute(near, 'chan', sibling)]
    ppermute x1, starting transfers between devices: 0.42 us -> 1.3 us  [local(): corner_other = lax.ppermute(corner, 'seg', [(0, 1), (1, 0)])]
where the time goes in v9:
time: 25.5 us; the launch traced here: 25.4 us
  starting transfers between devices  13.6 us (53%)
  Pallas kernels  9.98 us (39%)
  waiting for transfers between devices  1.69 us (7%)
    pallas_call x3, Pallas kernels, correlate(): pl.pallas_call(kernel, out_shape=jax.ShapeDtypeStruct((QUAD if tiles_only...  6.31 us
    ppermute x1, starting transfers between devices, local(): corner = lax.ppermute(white, 'chan', corners)  5.58 us
    pallas_call x1, Pallas kernels, spectra(): pl.pallas_call(functools.partial(spectrum_kernel, step), out_shape=jax.Sh...  2.11 us
    ppermute x1, starting transfers between devices, local(): first = lax.ppermute(quad, 'chan', plane_one)  1.91 us
    pallas_call x1, Pallas kernels, lag_rows(): pl.pallas_call(functools.partial(rows_kernel, samples, norm_scale), out_s...  1.53 us
    ppermute x1, starting transfers between devices, local(): beside = lax.ppermute(near, 'chan', sibling)  1.32 us
    ppermute x1, waiting for transfers between devices, local(): first = lax.ppermute(quad, 'chan', plane_one)  1.3 us
    ppermute x1, starting transfers between devices, local(): corner_other = lax.ppermute(corner, 'seg', [(0, 1), (1, 0)])  1.3 us
  transfers between devices with their start and end apart: 10, of which 2 were waited for; matrix products, arithmetic and copies ran while one was open for 0% of the time, Pallas kernels for 21%

profile of v9, /device:TPU:15, one launch (start us, length us, event | category | flops | bytes accessed | tf_op | source)
XLA Modules:
  0.0 25.4 jit_solution(3975605334380040262)
XLA Ops:
  0.0 2.1 %shard_map.37.white_ref = bf16[64,512]{1,0:T(8,128)(2,1)S(1)} custom-call(bf16[64,4096]{1,0:T(8,128)(2,1)} %bitcast.2, bf16[2,256,512]{2,1,0:T(8,128)(2,1)} %constant.2.clone.table_hbm), custom_call_target="tpu_custom_call" | custom-call | flops 1000000000 | bytes 1048576 | tf_op jit(solution)/shard_map/pallas_call | solution.py:81
  2.1 0.3 %collective-permute-start.2 = (bf16[64,512]{1,0:T(8,128)(2,1)S(1)}, bf16[64,512]{1,0:T(8,128)(2,1)S(1)}, u32[]{:S(2)}, u32[]{:S(2)}) collective-permute-start(bf16[64,512]{1,0:T(8,128)(2,1)S(1)} %shard_map.37.white_ref), channel_id=1, source_target_pairs={{0,18},{1,19},{2,16},{3,17},{4,22},{5,23},{6,20},{7,21},{8,26},{9,... | collective-permute-start | bytes 196616 | tf_op jit(solution)/shard_map/ppermute | solution.py:326
  2.4 1.2 %collective-permute-start.1 = (bf16[64,512]{1,0:T(8,128)(2,1)S(1)}, bf16[64,512]{1,0:T(8,128)(2,1)S(1)}, u32[]{:S(2)}, u32[]{:S(2)}) collective-permute-start(bf16[64,512]{1,0:T(8,128)(2,1)S(1)} %shard_map.37.white_ref), channel_id=1, source_target_pairs={{0,2},{1,3},{2,0},{3,1},{4,6},{5,7},{6,4},{7,5},{8,10},{9,11},{10,... | collective-permute-start | bytes 196616 | tf_op jit(solution)/shard_map/ppermute | solution.py:324
  3.6 1.2 %collective-permute-start = (bf16[64,512]{1,0:T(8,128)(2,1)S(1)}, bf16[64,512]{1,0:T(8,128)(2,1)S(1)}, u32[]{:S(2)}, u32[]{:S(2)}) collective-permute-start(bf16[64,512]{1,0:T(8,128)(2,1)S(1)} %shard_map.37.white_ref), channel_id=1, source_target_pairs={{0,16},{16,0},{1,17},{17,1},{2,18},{18,2},{3,19},{19,3},{4,20},{20... | collective-permute-start | bytes 196616 | tf_op jit(solution)/shard_map/ppermute | solution.py:323
  4.8 5.6 %collective-permute-start.3 = (bf16[64,512]{1,0:T(8,128)(2,1)S(1)}, bf16[64,512]{1,0:T(8,128)(2,1)S(1)}, u32[]{:S(2)}, u32[]{:S(2)}) collective-permute-start(bf16[64,512]{1,0:T(8,128)(2,1)S(1)} %shard_map.37.white_ref), channel_id=1, source_target_pairs={{3,8},{7,12},{8,3},{12,7},{19,24},{23,28},{24,19},{28,23}} | collective-permute-start | bytes 196616 | tf_op jit(solution)/shard_map/ppermute | solution.py:322
  10.4 0.0 collective-permute-done.2.diagonal_ref
  10.4 0.0 collective-permute-done.1.across_ref
  10.4 0.0 collective-permute-done.other_ref
  10.5 0.2 collective-permute-start.5
  10.7 1.9 %collective-permute-start.4 = (bf16[2,64,1024]{2,1,0:T(8,128)(2,1)S(1)}, bf16[2,64,1024]{2,1,0:T(8,128)(2,1)S(1)}, u32[]{:S(2)}, u32[]{:S(2)}) collective-permute-start(bf16[2,64,1024]{2,1,0:T(8,128)(2,1)S(1)} %shard_map.38.pair_ref.own_ref), channel_id=1, source_target_pairs={{4,8},{5,9},{6,10},{7,11},{8,4},{9,5},{10,6},{11,7},{20,24},{21,25... | collective-permute-start | bytes 786440 | tf_op jit(solution)/shard_map/ppermute | solution.py:328
  12.6 0.4 %collective-permute-done.3 = bf16[64,512]{1,0:T(8,128)(2,1)S(1)} collective-permute-done((bf16[64,512]{1,0:T(8,128)(2,1)S(1)}, bf16[64,512]{1,0:T(8,128)(2,1)S(1)}, u32[]{:S(2)}, u32[]{:S(2)}) %collective-permute-start.3) | collective-permute-done | bytes 65568 | tf_op jit(solution)/shard_map/ppermute | solution.py:322
  13.0 1.3 %collective-permute-start.6 = (bf16[2,64,1024]{2,1,0:T(8,128)(2,1)S(1)}, bf16[2,64,1024]{2,1,0:T(8,128)(2,1)S(1)}, u32[]{:S(2)}, u32[]{:S(2)}) collective-permute-start(bf16[2,64,1024]{2,1,0:T(8,128)(2,1)S(1)} %shard_map.38.pair_ref.own_ref), channel_id=1, source_target_pairs={{0,1},{1,0},{2,3},{3,2},{4,5},{5,4},{6,7},{7,6},{8,9},{9,8},{10,11... | collective-permute-start | bytes 786440 | tf_op jit(solution)/shard_map/ppermute | solution.py:331
  14.3 1.5 %shard_map.39 = (bf16[2,1040,1024]{2,1,0:T(8,128)(2,1)S(1)}, f32[11,128]{1,0:T(8,128)S(1)}) custom-call(bf16[2,64,1024]{2,1,0:T(8,128)(2,1)S(1)} %shard_map.38.pair_ref.own_ref, s32[1,11]{1,0:T(1,128)S(1)} %copy-done), custom_call_target="tpu_custom_call" | custom-call | flops 5000000000 | bytes 1048576 | tf_op jit(solution)/shard_map/pallas_call | solution.py:263
  15.9 1.3 %collective-permute-start.9 = (bf16[64,512]{1,0:T(8,128)(2,1)S(1)}, bf16[64,512]{1,0:T(8,128)(2,1)S(1)}, u32[]{:S(2)}, u32[]{:S(2)}) collective-permute-start(bf16[64,512]{1,0:T(8,128)(2,1)S(1)} %collective-permute-done.3), channel_id=1, source_target_pairs={{0,16},{16,0},{1,17},{17,1},{2,18},{18,2},{3,19},{19,3},{4,20},{20... | collective-permute-start | bytes 196616 | tf_op jit(solution)/shard_map/ppermute | solution.py:334
  17.2 0.0 collective-permute-done.6.sibling_ref
  17.2 2.4 %shard_map.40.near_ref = f32[11,1040,128]{2,1,0:T(8,128)} custom-call(bf16[2,1040,1024]{2,1,0:T(8,128)(2,1)S(1)} %get-tuple-element.17.rows_ref, f32[11,128]{1,0:T(8,128)S(1)} %get-tuple-element.18.scale_ref, bf16[2,64,1024]{2,1,0:T(8,128)(2,1)S(1)} %shard_map.38.pair_ref.own_ref, bf16[2,64,1024]{2,1,0:T(8,128)(2,1)S(1)} %collective-permute-done.6.sibling_ref), custom_call_target="tpu_custom_call" | custom-call | flops 1090519040 | bytes 2129920 | tf_op jit(solution)/shard_map/pallas_call | solution.py:294
  19.5 0.0 collective-permute-done.5.second_ref
  19.6 1.3 %collective-permute-done.4.first_ref = bf16[2,64,1024]{2,1,0:T(8,128)(2,1)S(1)} collective-permute-done((bf16[2,64,1024]{2,1,0:T(8,128)(2,1)S(1)}, bf16[2,64,1024]{2,1,0:T(8,128)(2,1)S(1)}, u32[]{:S(2)}, u32[]{:S(2)}) %collective-permute-start.4) | collective-permute-done | bytes 262176 | tf_op jit(solution)/shard_map/ppermute | solution.py:328
  20.9 0.5 %collective-permute-start.7 = (bf16[2,64,1024]{2,1,0:T(8,128)(2,1)S(1)}, bf16[2,64,1024]{2,1,0:T(8,128)(2,1)S(1)}, u32[]{:S(2)}, u32[]{:S(2)}) collective-permute-start(bf16[2,64,1024]{2,1,0:T(8,128)(2,1)S(1)} %collective-permute-done.4.first_ref), channel_id=1, source_target_pairs={{0,1},{1,0},{2,3},{3,2},{4,5},{5,4},{6,7},{7,6},{8,9},{9,8},{10,11... | collective-permute-start | bytes 786440 | tf_op jit(solution)/shard_map/ppermute | solution.py:338
  21.3 0.0 collective-permute-start.8
  21.4 0.0 collective-permute-done.9
  21.4 1.5 %shard_map.41.own_tiles_ref = f32[4,1040,128]{2,1,0:T(8,128)S(1)} custom-call(bf16[2,1040,1024]{2,1,0:T(8,128)(2,1)S(1)} %get-tuple-element.17.rows_ref, f32[11,128]{1,0:T(8,128)S(1)} %get-tuple-element.18.scale_ref, bf16[2,64,1024]{2,1,0:T(8,128)(2,1)S(1)} %collective-permute-done.4.first_ref, bf16[2,64,1024]{2,1,0:T(8,128)(2,1)S(1)} %collective-permute-done.5.second_ref), custom_call_target="tpu_custom_call" | custom-call | flops 1090519040 | bytes 2129920 | tf_op jit(solution)/shard_map/pallas_call | solution.py:294
  22.9 0.0 collective-permute-done.8.second_ref
  22.9 2.5 %shard_map.42 = f32[11,1040,128]{2,1,0:T(8,128)} custom-call(bf16[2,1040,1024]{2,1,0:T(8,128)(2,1)S(1)} %get-tuple-element.17.rows_ref, f32[11,128]{1,0:T(8,128)S(1)} %get-tuple-element.18.scale_ref, bf16[2,64,1024]{2,1,0:T(8,128)(2,1)S(1)} %collective-permute-done.7.first_ref, ...), custom_call_target="tpu_custom_call", output_to_operand_aliasing={{}: (6, {})} | custom-call | flops 1090519040 | bytes 2129920 | tf_op jit(solution)/shard_map/pallas_call | solution.py:294
  (5 shorter events, 0.0 us)
Async XLA Ops:
  0.0 14.3 %copy-start = (s32[1,11]{1,0:T(1,128)S(1)}, s32[1,11]{1,0:T(1,128)}, u32[]{:S(2)}) copy-start(s32[1,11]{1,0:T(1,128)} %partners_ref.1) | copy-start | bytes 136
  2.1 8.3 %collective-permute-start.2 = (bf16[64,512]{1,0:T(8,128)(2,1)S(1)}, bf16[64,512]{1,0:T(8,128)(2,1)S(1)}, u32[]{:S(2)}, u32[]{:S(2)}) collective-permute-start(bf16[64,512]{1,0:T(8,128)(2,1)S(1)} %shard_map.37.white_ref), channel_id=1, source_target_pairs={{0,18},{1,19},{2,16},{3,17},{4,22},{5,23},{6,20},{7,21},{8,26},{9,... | collective-permute-start | bytes 196616 | tf_op jit(solution)/shard_map/ppermute | solution.py:326
  2.4 8.1 %collective-permute-start.1 = (bf16[64,512]{1,0:T(8,128)(2,1)S(1)}, bf16[64,512]{1,0:T(8,128)(2,1)S(1)}, u32[]{:S(2)}, u32[]{:S(2)}) collective-permute-start(bf16[64,512]{1,0:T(8,128)(2,1)S(1)} %shard_map.37.white_ref), channel_id=1, source_target_pairs={{0,2},{1,3},{2,0},{3,1},{4,6},{5,7},{6,4},{7,5},{8,10},{9,11},{10,... | collective-permute-start | bytes 196616 | tf_op jit(solution)/shard_map/ppermute | solution.py:324
  3.6 6.9 %collective-permute-start = (bf16[64,512]{1,0:T(8,128)(2,1)S(1)}, bf16[64,512]{1,0:T(8,128)(2,1)S(1)}, u32[]{:S(2)}, u32[]{:S(2)}) collective-permute-start(bf16[64,512]{1,0:T(8,128)(2,1)S(1)} %shard_map.37.white_ref), channel_id=1, source_target_pairs={{0,16},{16,0},{1,17},{17,1},{2,18},{18,2},{3,19},{19,3},{4,20},{20... | collective-permute-start | bytes 196616 | tf_op jit(solution)/shard_map/ppermute | solution.py:323
  4.8 8.2 %collective-permute-start.3 = (bf16[64,512]{1,0:T(8,128)(2,1)S(1)}, bf16[64,512]{1,0:T(8,128)(2,1)S(1)}, u32[]{:S(2)}, u32[]{:S(2)}) collective-permute-start(bf16[64,512]{1,0:T(8,128)(2,1)S(1)} %shard_map.37.white_ref), channel_id=1, source_target_pairs={{3,8},{7,12},{8,3},{12,7},{19,24},{23,28},{24,19},{28,23}} | collective-permute-start | bytes 196616 | tf_op jit(solution)/shard_map/ppermute | solution.py:322
  10.5 9.1 %collective-permute-start.5 = (bf16[2,64,1024]{2,1,0:T(8,128)(2,1)S(1)}, bf16[2,64,1024]{2,1,0:T(8,128)(2,1)S(1)}, u32[]{:S(2)}, u32[]{:S(2)}) collective-permute-start(bf16[2,64,1024]{2,1,0:T(8,128)(2,1)S(1)} %shard_map.38.pair_ref.own_ref), channel_id=1, source_target_pairs={{0,4},{1,5},{2,6},{3,7},{4,0},{5,1},{6,2},{7,3},{8,12},{9,13},{10,... | collective-permute-start | bytes 786440 | tf_op jit(solution)/shard_map/ppermute | solution.py:329
  10.7 10.1 %collective-permute-start.4 = (bf16[2,64,1024]{2,1,0:T(8,128)(2,1)S(1)}, bf16[2,64,1024]{2,1,0:T(8,128)(2,1)S(1)}, u32[]{:S(2)}, u32[]{:S(2)}) collective-permute-start(bf16[2,64,1024]{2,1,0:T(8,128)(2,1)S(1)} %shard_map.38.pair_ref.own_ref), channel_id=1, source_target_pairs={{4,8},{5,9},{6,10},{7,11},{8,4},{9,5},{10,6},{11,7},{20,24},{21,25... | collective-permute-start | bytes 786440 | tf_op jit(solution)/shard_map/ppermute | solution.py:328
  13.0 4.2 %collective-permute-start.6 = (bf16[2,64,1024]{2,1,0:T(8,128)(2,1)S(1)}, bf16[2,64,1024]{2,1,0:T(8,128)(2,1)S(1)}, u32[]{:S(2)}, u32[]{:S(2)}) collective-permute-start(bf16[2,64,1024]{2,1,0:T(8,128)(2,1)S(1)} %shard_map.38.pair_ref.own_ref), channel_id=1, source_target_pairs={{0,1},{1,0},{2,3},{3,2},{4,5},{5,4},{6,7},{7,6},{8,9},{9,8},{10,11... | collective-permute-start | bytes 786440 | tf_op jit(solution)/shard_map/ppermute | solution.py:331
  15.9 5.5 %collective-permute-start.9 = (bf16[64,512]{1,0:T(8,128)(2,1)S(1)}, bf16[64,512]{1,0:T(8,128)(2,1)S(1)}, u32[]{:S(2)}, u32[]{:S(2)}) collective-permute-start(bf16[64,512]{1,0:T(8,128)(2,1)S(1)} %collective-permute-done.3), channel_id=1, source_target_pairs={{0,16},{16,0},{1,17},{17,1},{2,18},{18,2},{3,19},{19,3},{4,20},{20... | collective-permute-start | bytes 196616 | tf_op jit(solution)/shard_map/ppermute | solution.py:334
  20.9 2.0 %collective-permute-start.7 = (bf16[2,64,1024]{2,1,0:T(8,128)(2,1)S(1)}, bf16[2,64,1024]{2,1,0:T(8,128)(2,1)S(1)}, u32[]{:S(2)}, u32[]{:S(2)}) collective-permute-start(bf16[2,64,1024]{2,1,0:T(8,128)(2,1)S(1)} %collective-permute-done.4.first_ref), channel_id=1, source_target_pairs={{0,1},{1,0},{2,3},{3,2},{4,5},{5,4},{6,7},{7,6},{8,9},{9,8},{10,11... | collective-permute-start | bytes 786440 | tf_op jit(solution)/shard_map/ppermute | solution.py:338
  21.3 1.6 %collective-permute-start.8 = (bf16[2,64,1024]{2,1,0:T(8,128)(2,1)S(1)}, bf16[2,64,1024]{2,1,0:T(8,128)(2,1)S(1)}, u32[]{:S(2)}, u32[]{:S(2)}) collective-permute-start(bf16[2,64,1024]{2,1,0:T(8,128)(2,1)S(1)} %collective-permute-done.5.second_ref), channel_id=1, source_target_pairs={{0,1},{1,0},{2,3},{3,2},{4,5},{5,4},{6,7},{7,6},{8,9},{9,8},{10,11... | collective-permute-start | bytes 786440 | tf_op jit(solution)/shard_map/ppermute | solution.py:339

commit v10 on v8

--- a/solution.py
+++ b/solution.py
@@ -68,9 +68,9 @@
             imag = imag + (y_imag * cosine - y_real * sine)
     power = real * real + imag * imag
     level = jnp.mean(power, axis=1, keepdims=True)
-    denom = jnp.sqrt(power + water_level * level + epsilon)
-    white_ref[:, :BAND] = (real / denom).astype(jnp.bfloat16)
-    white_ref[:, BAND:] = (imag / denom).astype(jnp.bfloat16)
+    inverse = lax.rsqrt(power + water_level * level + epsilon)
+    white_ref[:, :BAND] = (real * inverse).astype(jnp.bfloat16)
+    white_ref[:, BAND:] = (imag * inverse).astype(jnp.bfloat16)
 
 
 def spectra(traces):

time: 25.5 us -> 25.5 us (level)
  no operation moved by 1% of the time
where the time goes in v10:
time: 25.5 us; the launch traced here: 25.3 us
  starting transfers between devices  13.8 us (54%)
  Pallas kernels  9.94 us (39%)
  waiting for transfers between devices  1.47 us (6%)
    pallas_call x3, Pallas kernels, correlate(): pl.pallas_call(kernel, out_shape=jax.ShapeDtypeStruct((QUAD if tiles_only...  6.29 us
    ppermute x1, starting transfers between devices, local(): corner = lax.ppermute(white, 'chan', corners)  5.58 us
    ppermute x1, starting transfers between devices, local(): beside = lax.ppermute(near, 'chan', sibling)  2.41 us
    pallas_call x1, Pallas kernels, spectra(): pl.pallas_call(functools.partial(spectrum_kernel, step), out_shape=jax.Sh...  2.09 us
    ppermute x1, starting transfers between devices, local(): first = lax.ppermute(quad, 'chan', plane_one)  1.91 us
    pallas_call x1, Pallas kernels, lag_rows(): pl.pallas_call(functools.partial(rows_kernel, samples, norm_scale), out_s...  1.53 us
    ppermute x1, starting transfers between devices, local(): other = lax.ppermute(white, 'seg', [(0, 1), (1, 0)])  1.24 us
    ppermute x1, starting transfers between devices, local(): across = lax.ppermute(white, 'chan', [(c, c ^ 2) for c in range(blocks)])  1.21 us
  transfers between devices with their start and end apart: 10, of which 2 were waited for; matrix products, arithmetic and copies ran while one was open for 0% of the time, Pallas kernels for 21%

profile of v10, /device:TPU:15, one launch (start us, length us, event | category | flops | bytes accessed | tf_op | source)
XLA Modules:
  0.0 25.3 jit_solution(8650578245503207725)
XLA Ops:
  0.0 2.1 %shard_map.37.white_ref = bf16[64,512]{1,0:T(8,128)(2,1)S(1)} custom-call(bf16[64,4096]{1,0:T(8,128)(2,1)} %bitcast.2, bf16[2,256,512]{2,1,0:T(8,128)(2,1)} %constant.2.clone.table_hbm), custom_call_target="tpu_custom_call" | custom-call | flops 1000000000 | bytes 1048576 | tf_op jit(solution)/shard_map/pallas_call | solution.py:81
  2.1 0.3 %collective-permute-start.2 = (bf16[64,512]{1,0:T(8,128)(2,1)S(1)}, bf16[64,512]{1,0:T(8,128)(2,1)S(1)}, u32[]{:S(2)}, u32[]{:S(2)}) collective-permute-start(bf16[64,512]{1,0:T(8,128)(2,1)S(1)} %shard_map.37.white_ref), channel_id=1, source_target_pairs={{0,18},{1,19},{2,16},{3,17},{4,22},{5,23},{6,20},{7,21},{8,26},{9,... | collective-permute-start | bytes 196616 | tf_op jit(solution)/shard_map/ppermute | solution.py:326
  2.4 1.2 %collective-permute-start.1 = (bf16[64,512]{1,0:T(8,128)(2,1)S(1)}, bf16[64,512]{1,0:T(8,128)(2,1)S(1)}, u32[]{:S(2)}, u32[]{:S(2)}) collective-permute-start(bf16[64,512]{1,0:T(8,128)(2,1)S(1)} %shard_map.37.white_ref), channel_id=1, source_target_pairs={{0,2},{1,3},{2,0},{3,1},{4,6},{5,7},{6,4},{7,5},{8,10},{9,11},{10,... | collective-permute-start | bytes 196616 | tf_op jit(solution)/shard_map/ppermute | solution.py:324
  3.6 1.2 %collective-permute-start = (bf16[64,512]{1,0:T(8,128)(2,1)S(1)}, bf16[64,512]{1,0:T(8,128)(2,1)S(1)}, u32[]{:S(2)}, u32[]{:S(2)}) collective-permute-start(bf16[64,512]{1,0:T(8,128)(2,1)S(1)} %shard_map.37.white_ref), channel_id=1, source_target_pairs={{0,16},{16,0},{1,17},{17,1},{2,18},{18,2},{3,19},{19,3},{4,20},{20... | collective-permute-start | bytes 196616 | tf_op jit(solution)/shard_map/ppermute | solution.py:323
  4.8 5.6 %collective-permute-start.3 = (bf16[64,512]{1,0:T(8,128)(2,1)S(1)}, bf16[64,512]{1,0:T(8,128)(2,1)S(1)}, u32[]{:S(2)}, u32[]{:S(2)}) collective-permute-start(bf16[64,512]{1,0:T(8,128)(2,1)S(1)} %shard_map.37.white_ref), channel_id=1, source_target_pairs={{3,8},{7,12},{8,3},{12,7},{19,24},{23,28},{24,19},{28,23}} | collective-permute-start | bytes 196616 | tf_op jit(solution)/shard_map/ppermute | solution.py:322
  10.4 0.0 collective-permute-done.2.diagonal_ref
  10.4 0.0 collective-permute-done.1.across_ref
  10.4 0.0 collective-permute-done.other_ref
  10.5 0.2 collective-permute-start.5
  10.7 1.9 %collective-permute-start.4 = (bf16[2,64,1024]{2,1,0:T(8,128)(2,1)S(1)}, bf16[2,64,1024]{2,1,0:T(8,128)(2,1)S(1)}, u32[]{:S(2)}, u32[]{:S(2)}) collective-permute-start(bf16[2,64,1024]{2,1,0:T(8,128)(2,1)S(1)} %shard_map.38.pair_ref.own_ref), channel_id=1, source_target_pairs={{4,8},{5,9},{6,10},{7,11},{8,4},{9,5},{10,6},{11,7},{20,24},{21,25... | collective-permute-start | bytes 786440 | tf_op jit(solution)/shard_map/ppermute | solution.py:328
  12.6 0.4 %collective-permute-done.3 = bf16[64,512]{1,0:T(8,128)(2,1)S(1)} collective-permute-done((bf16[64,512]{1,0:T(8,128)(2,1)S(1)}, bf16[64,512]{1,0:T(8,128)(2,1)S(1)}, u32[]{:S(2)}, u32[]{:S(2)}) %collective-permute-start.3) | collective-permute-done | bytes 65568 | tf_op jit(solution)/shard_map/ppermute | solution.py:322
  13.0 0.4 %collective-permute-start.9 = (bf16[64,512]{1,0:T(8,128)(2,1)S(1)}, bf16[64,512]{1,0:T(8,128)(2,1)S(1)}, u32[]{:S(2)}, u32[]{:S(2)}) collective-permute-start(bf16[64,512]{1,0:T(8,128)(2,1)S(1)} %collective-permute-done.3), channel_id=1, source_target_pairs={{0,16},{16,0},{1,17},{17,1},{2,18},{18,2},{3,19},{19,3},{4,20},{20... | collective-permute-start | bytes 196616 | tf_op jit(solution)/shard_map/ppermute | solution.py:331
  13.4 2.4 %collective-permute-start.6 = (bf16[2,64,1024]{2,1,0:T(8,128)(2,1)S(1)}, bf16[2,64,1024]{2,1,0:T(8,128)(2,1)S(1)}, u32[]{:S(2)}, u32[]{:S(2)}) collective-permute-start(bf16[2,64,1024]{2,1,0:T(8,128)(2,1)S(1)} %shard_map.38.pair_ref.own_ref), channel_id=1, source_target_pairs={{0,1},{1,0},{2,3},{3,2},{4,5},{5,4},{6,7},{7,6},{8,9},{9,8},{10,11... | collective-permute-start | bytes 786440 | tf_op jit(solution)/shard_map/ppermute | solution.py:332
  15.8 1.5 %shard_map.39 = (bf16[2,1040,1024]{2,1,0:T(8,128)(2,1)S(1)}, f32[11,128]{1,0:T(8,128)S(1)}) custom-call(bf16[2,64,1024]{2,1,0:T(8,128)(2,1)S(1)} %shard_map.38.pair_ref.own_ref, s32[1,11]{1,0:T(1,128)S(1)} %copy-done), custom_call_target="tpu_custom_call" | custom-call | flops 5000000000 | bytes 1048576 | tf_op jit(solution)/shard_map/pallas_call | solution.py:263
  17.4 0.0 collective-permute-done.6.sibling_ref
  17.4 2.4 %shard_map.40.near_ref = f32[11,1040,128]{2,1,0:T(8,128)} custom-call(bf16[2,1040,1024]{2,1,0:T(8,128)(2,1)S(1)} %get-tuple-element.13.rows_ref, f32[11,128]{1,0:T(8,128)S(1)} %get-tuple-element.14.scale_ref, bf16[2,64,1024]{2,1,0:T(8,128)(2,1)S(1)} %shard_map.38.pair_ref.own_ref, bf16[2,64,1024]{2,1,0:T(8,128)(2,1)S(1)} %collective-permute-done.6.sibling_ref), custom_call_target="tpu_custom_call" | custom-call | flops 1090519040 | bytes 2129920 | tf_op jit(solution)/shard_map/pallas_call | solution.py:294
  19.7 0.0 collective-permute-done.5.second_ref
  19.8 1.1 %collective-permute-done.4.first_ref = bf16[2,64,1024]{2,1,0:T(8,128)(2,1)S(1)} collective-permute-done((bf16[2,64,1024]{2,1,0:T(8,128)(2,1)S(1)}, bf16[2,64,1024]{2,1,0:T(8,128)(2,1)S(1)}, u32[]{:S(2)}, u32[]{:S(2)}) %collective-permute-start.4) | collective-permute-done | bytes 262176 | tf_op jit(solution)/shard_map/ppermute | solution.py:328
  20.8 0.5 %collective-permute-start.7 = (bf16[2,64,1024]{2,1,0:T(8,128)(2,1)S(1)}, bf16[2,64,1024]{2,1,0:T(8,128)(2,1)S(1)}, u32[]{:S(2)}, u32[]{:S(2)}) collective-permute-start(bf16[2,64,1024]{2,1,0:T(8,128)(2,1)S(1)} %collective-permute-done.4.first_ref), channel_id=1, source_target_pairs={{0,1},{1,0},{2,3},{3,2},{4,5},{5,4},{6,7},{7,6},{8,9},{9,8},{10,11... | collective-permute-start | bytes 786440 | tf_op jit(solution)/shard_map/ppermute | solution.py:337
  21.3 0.0 collective-permute-start.8
  21.4 0.0 collective-permute-done.9
  21.4 1.5 %shard_map.41.own_tiles_ref = f32[4,1040,128]{2,1,0:T(8,128)S(1)} custom-call(bf16[2,1040,1024]{2,1,0:T(8,128)(2,1)S(1)} %get-tuple-element.13.rows_ref, f32[11,128]{1,0:T(8,128)S(1)} %get-tuple-element.14.scale_ref, bf16[2,64,1024]{2,1,0:T(8,128)(2,1)S(1)} %collective-permute-done.4.first_ref, bf16[2,64,1024]{2,1,0:T(8,128)(2,1)S(1)} %collective-permute-done.5.second_ref), custom_call_target="tpu_custom_call" | custom-call | flops 1090519040 | bytes 2129920 | tf_op jit(solution)/shard_map/pallas_call | solution.py:294
  22.9 0.0 collective-permute-done.7.first_ref
  22.9 2.4 %shard_map.42 = f32[11,1040,128]{2,1,0:T(8,128)} custom-call(bf16[2,1040,1024]{2,1,0:T(8,128)(2,1)S(1)} %get-tuple-element.13.rows_ref, f32[11,128]{1,0:T(8,128)S(1)} %get-tuple-element.14.scale_ref, bf16[2,64,1024]{2,1,0:T(8,128)(2,1)S(1)} %collective-permute-done.7.first_ref, ...), custom_call_target="tpu_custom_call", output_to_operand_aliasing={{}: (6, {})} | custom-call | flops 1090519040 | bytes 2129920 | tf_op jit(solution)/shard_map/pallas_call | solution.py:294
  (5 shorter events, 0.0 us)
Async XLA Ops:
  0.0 15.8 %copy-start = (s32[1,11]{1,0:T(1,128)S(1)}, s32[1,11]{1,0:T(1,128)}, u32[]{:S(2)}) copy-start(s32[1,11]{1,0:T(1,128)} %partners_ref.1) | copy-start | bytes 136
  2.1 8.3 %collective-permute-start.2 = (bf16[64,512]{1,0:T(8,128)(2,1)S(1)}, bf16[64,512]{1,0:T(8,128)(2,1)S(1)}, u32[]{:S(2)}, u32[]{:S(2)}) collective-permute-start(bf16[64,512]{1,0:T(8,128)(2,1)S(1)} %shard_map.37.white_ref), channel_id=1, source_target_pairs={{0,18},{1,19},{2,16},{3,17},{4,22},{5,23},{6,20},{7,21},{8,26},{9,... | collective-permute-start | bytes 196616 | tf_op jit(solution)/shard_map/ppermute | solution.py:326
  2.4 8.1 %collective-permute-start.1 = (bf16[64,512]{1,0:T(8,128)(2,1)S(1)}, bf16[64,512]{1,0:T(8,128)(2,1)S(1)}, u32[]{:S(2)}, u32[]{:S(2)}) collective-permute-start(bf16[64,512]{1,0:T(8,128)(2,1)S(1)} %shard_map.37.white_ref), channel_id=1, source_target_pairs={{0,2},{1,3},{2,0},{3,1},{4,6},{5,7},{6,4},{7,5},{8,10},{9,11},{10,... | collective-permute-start | bytes 196616 | tf_op jit(solution)/shard_map/ppermute | solution.py:324
  3.6 6.9 %collective-permute-start = (bf16[64,512]{1,0:T(8,128)(2,1)S(1)}, bf16[64,512]{1,0:T(8,128)(2,1)S(1)}, u32[]{:S(2)}, u32[]{:S(2)}) collective-permute-start(bf16[64,512]{1,0:T(8,128)(2,1)S(1)} %shard_map.37.white_ref), channel_id=1, source_target_pairs={{0,16},{16,0},{1,17},{17,1},{2,18},{18,2},{3,19},{19,3},{4,20},{20... | collective-permute-start | bytes 196616 | tf_op jit(solution)/shard_map/ppermute | solution.py:323
  4.8 8.2 %collective-permute-start.3 = (bf16[64,512]{1,0:T(8,128)(2,1)S(1)}, bf16[64,512]{1,0:T(8,128)(2,1)S(1)}, u32[]{:S(2)}, u32[]{:S(2)}) collective-permute-start(bf16[64,512]{1,0:T(8,128)(2,1)S(1)} %shard_map.37.white_ref), channel_id=1, source_target_pairs={{3,8},{7,12},{8,3},{12,7},{19,24},{23,28},{24,19},{28,23}} | collective-permute-start | bytes 196616 | tf_op jit(solution)/shard_map/ppermute | solution.py:322
  10.5 9.3 %collective-permute-start.5 = (bf16[2,64,1024]{2,1,0:T(8,128)(2,1)S(1)}, bf16[2,64,1024]{2,1,0:T(8,128)(2,1)S(1)}, u32[]{:S(2)}, u32[]{:S(2)}) collective-permute-start(bf16[2,64,1024]{2,1,0:T(8,128)(2,1)S(1)} %shard_map.38.pair_ref.own_ref), channel_id=1, source_target_pairs={{0,4},{1,5},{2,6},{3,7},{4,0},{5,1},{6,2},{7,3},{8,12},{9,13},{10,... | collective-permute-start | bytes 786440 | tf_op jit(solution)/shard_map/ppermute | solution.py:329
  10.7 10.1 %collective-permute-start.4 = (bf16[2,64,1024]{2,1,0:T(8,128)(2,1)S(1)}, bf16[2,64,1024]{2,1,0:T(8,128)(2,1)S(1)}, u32[]{:S(2)}, u32[]{:S(2)}) collective-permute-start(bf16[2,64,1024]{2,1,0:T(8,128)(2,1)S(1)} %shard_map.38.pair_ref.own_ref), channel_id=1, source_target_pairs={{4,8},{5,9},{6,10},{7,11},{8,4},{9,5},{10,6},{11,7},{20,24},{21,25... | collective-permute-start | bytes 786440 | tf_op jit(solution)/shard_map/ppermute | solution.py:328
  13.0 8.4 %collective-permute-start.9 = (bf16[64,512]{1,0:T(8,128)(2,1)S(1)}, bf16[64,512]{1,0:T(8,128)(2,1)S(1)}, u32[]{:S(2)}, u32[]{:S(2)}) collective-permute-start(bf16[64,512]{1,0:T(8,128)(2,1)S(1)} %collective-permute-done.3), channel_id=1, source_target_pairs={{0,16},{16,0},{1,17},{17,1},{2,18},{18,2},{3,19},{19,3},{4,20},{20... | collective-permute-start | bytes 196616 | tf_op jit(solution)/shard_map/ppermute | solution.py:331
  13.4 4.0 %collective-permute-start.6 = (bf16[2,64,1024]{2,1,0:T(8,128)(2,1)S(1)}, bf16[2,64,1024]{2,1,0:T(8,128)(2,1)S(1)}, u32[]{:S(2)}, u32[]{:S(2)}) collective-permute-start(bf16[2,64,1024]{2,1,0:T(8,128)(2,1)S(1)} %shard_map.38.pair_ref.own_ref), channel_id=1, source_target_pairs={{0,1},{1,0},{2,3},{3,2},{4,5},{5,4},{6,7},{7,6},{8,9},{9,8},{10,11... | collective-permute-start | bytes 786440 | tf_op jit(solution)/shard_map/ppermute | solution.py:332
  20.8 2.0 %collective-permute-start.7 = (bf16[2,64,1024]{2,1,0:T(8,128)(2,1)S(1)}, bf16[2,64,1024]{2,1,0:T(8,128)(2,1)S(1)}, u32[]{:S(2)}, u32[]{:S(2)}) collective-permute-start(bf16[2,64,1024]{2,1,0:T(8,128)(2,1)S(1)} %collective-permute-done.4.first_ref), channel_id=1, source_target_pairs={{0,1},{1,0},{2,3},{3,2},{4,5},{5,4},{6,7},{7,6},{8,9},{9,8},{10,11... | collective-permute-start | bytes 786440 | tf_op jit(solution)/shard_map/ppermute | solution.py:337
  21.3 1.6 %collective-permute-start.8 = (bf16[2,64,1024]{2,1,0:T(8,128)(2,1)S(1)}, bf16[2,64,1024]{2,1,0:T(8,128)(2,1)S(1)}, u32[]{:S(2)}, u32[]{:S(2)}) collective-permute-start(bf16[2,64,1024]{2,1,0:T(8,128)(2,1)S(1)} %collective-permute-done.5.second_ref), channel_id=1, source_target_pairs={{0,1},{1,0},{2,3},{3,2},{4,5},{5,4},{6,7},{7,6},{8,9},{9,8},{10,11... | collective-permute-start | bytes 786440 | tf_op jit(solution)/shard_map/ppermute | solution.py:338

commit v11 on v8

--- a/solution.py
+++ b/solution.py
@@ -143,7 +143,7 @@
                 rows_ref[member, at, middle:right] = (real * sine + imag * cosine).astype(jnp.bfloat16)
         return carry
 
-    lax.fori_loop(0, LAGS, turn, 0, unroll=5)
+    lax.fori_loop(0, LAGS, turn, 0, unroll=13)
 
 
 def multiply(rows_ref, window, scale, tiles, done):

time: 25.5 us -> 25.5 us (level)
  transfers between devices with their start and end apart: 10 -> 10, of which waited for: 2 -> 2; matrix products, arithmetic and copies ran while one was open for 0% -> 0% of each run, Pallas kernels for 21% -> 22%
where the time goes in v11:
time: 25.5 us; the launch traced here: 25.4 us
  starting transfers between devices  13.8 us (54%)
  Pallas kernels  10.1 us (40%)
  waiting for transfers between devices  1.36 us (5%)
    pallas_call x3, Pallas kernels, correlate(): pl.pallas_call(kernel, out_shape=jax.ShapeDtypeStruct((QUAD if tiles_only...  6.32 us
    ppermute x1, starting transfers between devices, local(): corner = lax.ppermute(white, 'chan', corners)  5.58 us
    ppermute x1, starting transfers between devices, local(): beside = lax.ppermute(near, 'chan', sibling)  2.41 us
    pallas_call x1, Pallas kernels, spectra(): pl.pallas_call(functools.partial(spectrum_kernel, step), out_shape=jax.Sh...  2.11 us
    ppermute x1, starting transfers between devices, local(): first = lax.ppermute(quad, 'chan', plane_one)  1.91 us
    pallas_call x1, Pallas kernels, lag_rows(): pl.pallas_call(functools.partial(rows_kernel, samples, norm_scale), out_s...  1.63 us
    ppermute x1, starting transfers between devices, local(): other = lax.ppermute(white, 'seg', [(0, 1), (1, 0)])  1.24 us
    ppermute x1, starting transfers between devices, local(): across = lax.ppermute(white, 'chan', [(c, c ^ 2) for c in range(blocks)])  1.21 us
  transfers between devices with their start and end apart: 10, of which 2 were waited for; matrix products, arithmetic and copies ran while one was open for 0% of the time, Pallas kernels for 22%

profile of v11, /device:TPU:15, one launch (start us, length us, event | category | flops | bytes accessed | tf_op | source)
XLA Modules:
  0.0 25.4 jit_solution(336572552816250881)
XLA Ops:
  0.0 2.1 %shard_map.37.white_ref = bf16[64,512]{1,0:T(8,128)(2,1)S(1)} custom-call(bf16[64,4096]{1,0:T(8,128)(2,1)} %bitcast.2, bf16[2,256,512]{2,1,0:T(8,128)(2,1)} %constant.2.clone.table_hbm), custom_call_target="tpu_custom_call" | custom-call | flops 1000000000 | bytes 1048576 | tf_op jit(solution)/shard_map/pallas_call | solution.py:81
  2.1 0.3 %collective-permute-start.2 = (bf16[64,512]{1,0:T(8,128)(2,1)S(1)}, bf16[64,512]{1,0:T(8,128)(2,1)S(1)}, u32[]{:S(2)}, u32[]{:S(2)}) collective-permute-start(bf16[64,512]{1,0:T(8,128)(2,1)S(1)} %shard_map.37.white_ref), channel_id=1, source_target_pairs={{0,18},{1,19},{2,16},{3,17},{4,22},{5,23},{6,20},{7,21},{8,26},{9,... | collective-permute-start | bytes 196616 | tf_op jit(solution)/shard_map/ppermute | solution.py:326
  2.4 1.2 %collective-permute-start.1 = (bf16[64,512]{1,0:T(8,128)(2,1)S(1)}, bf16[64,512]{1,0:T(8,128)(2,1)S(1)}, u32[]{:S(2)}, u32[]{:S(2)}) collective-permute-start(bf16[64,512]{1,0:T(8,128)(2,1)S(1)} %shard_map.37.white_ref), channel_id=1, source_target_pairs={{0,2},{1,3},{2,0},{3,1},{4,6},{5,7},{6,4},{7,5},{8,10},{9,11},{10,... | collective-permute-start | bytes 196616 | tf_op jit(solution)/shard_map/ppermute | solution.py:324
  3.6 1.2 %collective-permute-start = (bf16[64,512]{1,0:T(8,128)(2,1)S(1)}, bf16[64,512]{1,0:T(8,128)(2,1)S(1)}, u32[]{:S(2)}, u32[]{:S(2)}) collective-permute-start(bf16[64,512]{1,0:T(8,128)(2,1)S(1)} %shard_map.37.white_ref), channel_id=1, source_target_pairs={{0,16},{16,0},{1,17},{17,1},{2,18},{18,2},{3,19},{19,3},{4,20},{20... | collective-permute-start | bytes 196616 | tf_op jit(solution)/shard_map/ppermute | solution.py:323
  4.8 5.6 %collective-permute-start.3 = (bf16[64,512]{1,0:T(8,128)(2,1)S(1)}, bf16[64,512]{1,0:T(8,128)(2,1)S(1)}, u32[]{:S(2)}, u32[]{:S(2)}) collective-permute-start(bf16[64,512]{1,0:T(8,128)(2,1)S(1)} %shard_map.37.white_ref), channel_id=1, source_target_pairs={{3,8},{7,12},{8,3},{12,7},{19,24},{23,28},{24,19},{28,23}} | collective-permute-start | bytes 196616 | tf_op jit(solution)/shard_map/ppermute | solution.py:322
  10.4 0.0 collective-permute-done.2.diagonal_ref
  10.4 0.0 collective-permute-done.1.across_ref
  10.4 0.0 collective-permute-done.other_ref
  10.5 0.2 collective-permute-start.5
  10.7 1.9 %collective-permute-start.4 = (bf16[2,64,1024]{2,1,0:T(8,128)(2,1)S(1)}, bf16[2,64,1024]{2,1,0:T(8,128)(2,1)S(1)}, u32[]{:S(2)}, u32[]{:S(2)}) collective-permute-start(bf16[2,64,1024]{2,1,0:T(8,128)(2,1)S(1)} %shard_map.38.pair_ref.own_ref), channel_id=1, source_target_pairs={{4,8},{5,9},{6,10},{7,11},{8,4},{9,5},{10,6},{11,7},{20,24},{21,25... | collective-permute-start | bytes 786440 | tf_op jit(solution)/shard_map/ppermute | solution.py:328
  12.6 0.4 %collective-permute-done.3 = bf16[64,512]{1,0:T(8,128)(2,1)S(1)} collective-permute-done((bf16[64,512]{1,0:T(8,128)(2,1)S(1)}, bf16[64,512]{1,0:T(8,128)(2,1)S(1)}, u32[]{:S(2)}, u32[]{:S(2)}) %collective-permute-start.3) | collective-permute-done | bytes 65568 | tf_op jit(solution)/shard_map/ppermute | solution.py:322
  13.0 0.4 %collective-permute-start.9 = (bf16[64,512]{1,0:T(8,128)(2,1)S(1)}, bf16[64,512]{1,0:T(8,128)(2,1)S(1)}, u32[]{:S(2)}, u32[]{:S(2)}) collective-permute-start(bf16[64,512]{1,0:T(8,128)(2,1)S(1)} %collective-permute-done.3), channel_id=1, source_target_pairs={{0,16},{16,0},{1,17},{17,1},{2,18},{18,2},{3,19},{19,3},{4,20},{20... | collective-permute-start | bytes 196616 | tf_op jit(solution)/shard_map/ppermute | solution.py:331
  13.4 2.4 %collective-permute-start.6 = (bf16[2,64,1024]{2,1,0:T(8,128)(2,1)S(1)}, bf16[2,64,1024]{2,1,0:T(8,128)(2,1)S(1)}, u32[]{:S(2)}, u32[]{:S(2)}) collective-permute-start(bf16[2,64,1024]{2,1,0:T(8,128)(2,1)S(1)} %shard_map.38.pair_ref.own_ref), channel_id=1, source_target_pairs={{0,1},{1,0},{2,3},{3,2},{4,5},{5,4},{6,7},{7,6},{8,9},{9,8},{10,11... | collective-permute-start | bytes 786440 | tf_op jit(solution)/shard_map/ppermute | solution.py:332
  15.8 1.6 %shard_map.39 = (bf16[2,1040,1024]{2,1,0:T(8,128)(2,1)S(1)}, f32[11,128]{1,0:T(8,128)S(1)}) custom-call(bf16[2,64,1024]{2,1,0:T(8,128)(2,1)S(1)} %shard_map.38.pair_ref.own_ref, s32[1,11]{1,0:T(1,128)S(1)} %copy-done), custom_call_target="tpu_custom_call" | custom-call | flops 5000000000 | bytes 1048576 | tf_op jit(solution)/shard_map/pallas_call | solution.py:263
  17.5 0.0 collective-permute-done.6.sibling_ref
  17.5 2.4 %shard_map.40.near_ref = f32[11,1040,128]{2,1,0:T(8,128)} custom-call(bf16[2,1040,1024]{2,1,0:T(8,128)(2,1)S(1)} %get-tuple-element.13.rows_ref, f32[11,128]{1,0:T(8,128)S(1)} %get-tuple-element.14.scale_ref, bf16[2,64,1024]{2,1,0:T(8,128)(2,1)S(1)} %shard_map.38.pair_ref.own_ref, bf16[2,64,1024]{2,1,0:T(8,128)(2,1)S(1)} %collective-permute-done.6.sibling_ref), custom_call_target="tpu_custom_call" | custom-call | flops 1090519040 | bytes 2129920 | tf_op jit(solution)/shard_map/pallas_call | solution.py:294
  19.9 0.0 collective-permute-done.5.second_ref
  19.9 1.0 %collective-permute-done.4.first_ref = bf16[2,64,1024]{2,1,0:T(8,128)(2,1)S(1)} collective-permute-done((bf16[2,64,1024]{2,1,0:T(8,128)(2,1)S(1)}, bf16[2,64,1024]{2,1,0:T(8,128)(2,1)S(1)}, u32[]{:S(2)}, u32[]{:S(2)}) %collective-permute-start.4) | collective-permute-done | bytes 262176 | tf_op jit(solution)/shard_map/ppermute | solution.py:328
  20.9 0.5 %collective-permute-start.7 = (bf16[2,64,1024]{2,1,0:T(8,128)(2,1)S(1)}, bf16[2,64,1024]{2,1,0:T(8,128)(2,1)S(1)}, u32[]{:S(2)}, u32[]{:S(2)}) collective-permute-start(bf16[2,64,1024]{2,1,0:T(8,128)(2,1)S(1)} %collective-permute-done.4.first_ref), channel_id=1, source_target_pairs={{0,1},{1,0},{2,3},{3,2},{4,5},{5,4},{6,7},{7,6},{8,9},{9,8},{10,11... | collective-permute-start | bytes 786440 | tf_op jit(solution)/shard_map/ppermute | solution.py:337
  21.3 0.0 collective-permute-start.8
  21.4 0.0 collective-permute-done.9
  21.4 1.5 %shard_map.41.own_tiles_ref = f32[4,1040,128]{2,1,0:T(8,128)S(1)} custom-call(bf16[2,1040,1024]{2,1,0:T(8,128)(2,1)S(1)} %get-tuple-element.13.rows_ref, f32[11,128]{1,0:T(8,128)S(1)} %get-tuple-element.14.scale_ref, bf16[2,64,1024]{2,1,0:T(8,128)(2,1)S(1)} %collective-permute-done.4.first_ref, bf16[2,64,1024]{2,1,0:T(8,128)(2,1)S(1)} %collective-permute-done.5.second_ref), custom_call_target="tpu_custom_call" | custom-call | flops 1090519040 | bytes 2129920 | tf_op jit(solution)/shard_map/pallas_call | solution.py:294
  22.9 0.0 collective-permute-done.8.second_ref
  22.9 2.5 %shard_map.42 = f32[11,1040,128]{2,1,0:T(8,128)} custom-call(bf16[2,1040,1024]{2,1,0:T(8,128)(2,1)S(1)} %get-tuple-element.13.rows_ref, f32[11,128]{1,0:T(8,128)S(1)} %get-tuple-element.14.scale_ref, bf16[2,64,1024]{2,1,0:T(8,128)(2,1)S(1)} %collective-permute-done.7.first_ref, ...), custom_call_target="tpu_custom_call", output_to_operand_aliasing={{}: (6, {})} | custom-call | flops 1090519040 | bytes 2129920 | tf_op jit(solution)/shard_map/pallas_call | solution.py:294
  (5 shorter events, 0.0 us)
Async XLA Ops:
  0.0 15.8 %copy-start = (s32[1,11]{1,0:T(1,128)S(1)}, s32[1,11]{1,0:T(1,128)}, u32[]{:S(2)}) copy-start(s32[1,11]{1,0:T(1,128)} %partners_ref.1) | copy-start | bytes 136
  2.1 8.3 %collective-permute-start.2 = (bf16[64,512]{1,0:T(8,128)(2,1)S(1)}, bf16[64,512]{1,0:T(8,128)(2,1)S(1)}, u32[]{:S(2)}, u32[]{:S(2)}) collective-permute-start(bf16[64,512]{1,0:T(8,128)(2,1)S(1)} %shard_map.37.white_ref), channel_id=1, source_target_pairs={{0,18},{1,19},{2,16},{3,17},{4,22},{5,23},{6,20},{7,21},{8,26},{9,... | collective-permute-start | bytes 196616 | tf_op jit(solution)/shard_map/ppermute | solution.py:326
  2.4 8.1 %collective-permute-start.1 = (bf16[64,512]{1,0:T(8,128)(2,1)S(1)}, bf16[64,512]{1,0:T(8,128)(2,1)S(1)}, u32[]{:S(2)}, u32[]{:S(2)}) collective-permute-start(bf16[64,512]{1,0:T(8,128)(2,1)S(1)} %shard_map.37.white_ref), channel_id=1, source_target_pairs={{0,2},{1,3},{2,0},{3,1},{4,6},{5,7},{6,4},{7,5},{8,10},{9,11},{10,... | collective-permute-start | bytes 196616 | tf_op jit(solution)/shard_map/ppermute | solution.py:324
  3.6 6.9 %collective-permute-start = (bf16[64,512]{1,0:T(8,128)(2,1)S(1)}, bf16[64,512]{1,0:T(8,128)(2,1)S(1)}, u32[]{:S(2)}, u32[]{:S(2)}) collective-permute-start(bf16[64,512]{1,0:T(8,128)(2,1)S(1)} %shard_map.37.white_ref), channel_id=1, source_target_pairs={{0,16},{16,0},{1,17},{17,1},{2,18},{18,2},{3,19},{19,3},{4,20},{20... | collective-permute-start | bytes 196616 | tf_op jit(solution)/shard_map/ppermute | solution.py:323
  4.8 8.2 %collective-permute-start.3 = (bf16[64,512]{1,0:T(8,128)(2,1)S(1)}, bf16[64,512]{1,0:T(8,128)(2,1)S(1)}, u32[]{:S(2)}, u32[]{:S(2)}) collective-permute-start(bf16[64,512]{1,0:T(8,128)(2,1)S(1)} %shard_map.37.white_ref), channel_id=1, source_target_pairs={{3,8},{7,12},{8,3},{12,7},{19,24},{23,28},{24,19},{28,23}} | collective-permute-start | bytes 196616 | tf_op jit(solution)/shard_map/ppermute | solution.py:322
  10.5 9.4 %collective-permute-start.5 = (bf16[2,64,1024]{2,1,0:T(8,128)(2,1)S(1)}, bf16[2,64,1024]{2,1,0:T(8,128)(2,1)S(1)}, u32[]{:S(2)}, u32[]{:S(2)}) collective-permute-start(bf16[2,64,1024]{2,1,0:T(8,128)(2,1)S(1)} %shard_map.38.pair_ref.own_ref), channel_id=1, source_target_pairs={{0,4},{1,5},{2,6},{3,7},{4,0},{5,1},{6,2},{7,3},{8,12},{9,13},{10,... | collective-permute-start | bytes 786440 | tf_op jit(solution)/shard_map/ppermute | solution.py:329
  10.7 10.1 %collective-permute-start.4 = (bf16[2,64,1024]{2,1,0:T(8,128)(2,1)S(1)}, bf16[2,64,1024]{2,1,0:T(8,128)(2,1)S(1)}, u32[]{:S(2)}, u32[]{:S(2)}) collective-permute-start(bf16[2,64,1024]{2,1,0:T(8,128)(2,1)S(1)} %shard_map.38.pair_ref.own_ref), channel_id=1, source_target_pairs={{4,8},{5,9},{6,10},{7,11},{8,4},{9,5},{10,6},{11,7},{20,24},{21,25... | collective-permute-start | bytes 786440 | tf_op jit(solution)/shard_map/ppermute | solution.py:328
  13.0 8.4 %collective-permute-start.9 = (bf16[64,512]{1,0:T(8,128)(2,1)S(1)}, bf16[64,512]{1,0:T(8,128)(2,1)S(1)}, u32[]{:S(2)}, u32[]{:S(2)}) collective-permute-start(bf16[64,512]{1,0:T(8,128)(2,1)S(1)} %collective-permute-done.3), channel_id=1, source_target_pairs={{0,16},{16,0},{1,17},{17,1},{2,18},{18,2},{3,19},{19,3},{4,20},{20... | collective-permute-start | bytes 196616 | tf_op jit(solution)/shard_map/ppermute | solution.py:331
  13.4 4.1 %collective-permute-start.6 = (bf16[2,64,1024]{2,1,0:T(8,128)(2,1)S(1)}, bf16[2,64,1024]{2,1,0:T(8,128)(2,1)S(1)}, u32[]{:S(2)}, u32[]{:S(2)}) collective-permute-start(bf16[2,64,1024]{2,1,0:T(8,128)(2,1)S(1)} %shard_map.38.pair_ref.own_ref), channel_id=1, source_target_pairs={{0,1},{1,0},{2,3},{3,2},{4,5},{5,4},{6,7},{7,6},{8,9},{9,8},{10,11... | collective-permute-start | bytes 786440 | tf_op jit(solution)/shard_map/ppermute | solution.py:332
  20.9 2.0 %collective-permute-start.7 = (bf16[2,64,1024]{2,1,0:T(8,128)(2,1)S(1)}, bf16[2,64,1024]{2,1,0:T(8,128)(2,1)S(1)}, u32[]{:S(2)}, u32[]{:S(2)}) collective-permute-start(bf16[2,64,1024]{2,1,0:T(8,128)(2,1)S(1)} %collective-permute-done.4.first_ref), channel_id=1, source_target_pairs={{0,1},{1,0},{2,3},{3,2},{4,5},{5,4},{6,7},{7,6},{8,9},{9,8},{10,11... | collective-permute-start | bytes 786440 | tf_op jit(solution)/shard_map/ppermute | solution.py:337
  21.3 1.6 %collective-permute-start.8 = (bf16[2,64,1024]{2,1,0:T(8,128)(2,1)S(1)}, bf16[2,64,1024]{2,1,0:T(8,128)(2,1)S(1)}, u32[]{:S(2)}, u32[]{:S(2)}) collective-permute-start(bf16[2,64,1024]{2,1,0:T(8,128)(2,1)S(1)} %collective-permute-done.5.second_ref), channel_id=1, source_target_pairs={{0,1},{1,0},{2,3},{3,2},{4,5},{5,4},{6,7},{7,6},{8,9},{9,8},{10,11... | collective-permute-start | bytes 786440 | tf_op jit(solution)/shard_map/ppermute | solution.py:338
